TPU v7x, 256 devices: a whole 4x4x8 slice. The times are simulated.
256 devices in a mesh: kvseq: 32 (over z, y), head: 8 (over x, core).
Axes of the slice: x: 4, y: 4, z: 8, core: 2. Of those that a mesh axis runs over, the one named last changes fastest.
Arguments:
- lengths: int32 [4], replicated, may hold values from 16 to 65536, as said below
- queries: bfloat16 [4, 16, 8192], P(None, None, 'head'), may hold values from -8 to 8
- cache_keys: bfloat16 [4, 65536, 1024], P(None, 'kvseq', 'head'), may hold values from -8 to 8
- cache_values: bfloat16 [4, 65536, 1024], P(None, 'kvseq', 'head'), may hold values from -8 to 8
- residual_in: bfloat16 [64, 8192], P(None, ('kvseq', 'head')), may hold values from -24 to 24
- out_weight: bfloat16 [8192, 8192], P('head', 'kvseq'), may hold values from -0.0625 to 0.0625
- norm_gain: bfloat16 [8192], P(('kvseq', 'head')), may hold values from 0.099609375 to 1.8984375
- gate_weight: bfloat16 [8192, 28672], P(None, ('kvseq', 'head')), may hold values from -0.25 to 0.25
- up_weight: bfloat16 [8192, 28672], P(None, ('kvseq', 'head')), may hold values from -0.25 to 0.25
- down_weight: bfloat16 [28672, 8192], P(('kvseq', 'head')), may hold values from -0.15625 to 0.15625
Outputs:
- layer_out: bfloat16 [64, 8192], P(None, ('kvseq', 'head'))
Inputs may be any that keep to these rules, and one draw needn't show every extreme that they name: `lengths`: every sequence holds at least its 16 new tokens; some sequence fills the whole cache of 65536 positions.
All inputs are finite; a program needn't handle non-finite values.
Results may differ from a plain program's by a relative error of at most 0.015.
Values may be sent and summed in bfloat16 or wider, within the bound.
No kernel may reach another device: no remote copies, remote signals or barrier semaphores. Data moves between devices by JAX's collectives and lax.ppermute only.
A program may use at most 128 MiB of HBM per device.

v0:
```python
import math

import jax
import jax.numpy as jnp
from jax import lax
from jax.sharding import PartitionSpec as P

D = 8192
HQ = 64
KVH = 8
HD = 128


NEG_FILL = -1e30
EPSILON = 1e-05


def joined(shard, axis, combine):
    everything = jax.tree.map(
        lambda part, kind: lax.all_gather(part.astype(kind), axis),
        shard,
        (jnp.bfloat16, jnp.bfloat16, jnp.bfloat16),
    )

    def take(k):
        return jax.tree.map(lambda part, own: part[k].astype(own.dtype), everything, shard)

    return lax.fori_loop(
        1, lax.axis_size(axis), lambda k, so_far: combine(so_far, take(k)), take(0)
    )


def combine_partials(earlier, later):
    max_one, total_one, acc_one = earlier
    max_two, total_two, acc_two = later
    joint_max = jnp.maximum(max_one, max_two)
    factor_one = jnp.exp(max_one - joint_max)
    factor_two = jnp.exp(max_two - joint_max)
    return (
        joint_max,
        total_one * factor_one + total_two * factor_two,
        acc_one * factor_one[..., None] + acc_two * factor_two[..., None],
    )


def shards(
    lengths,
    queries,
    cache_keys,
    cache_values,
    residual_in,
    out_weight,
    norm_gain,
    gate_weight,
    up_weight,
    down_weight,
):
    row_count, drafts, query_width = queries.shape
    slice_len = cache_keys.shape[1]
    kv_local = cache_keys.shape[2] // HD
    group_size = HQ // KVH
    first_key = lax.axis_index("kvseq") * slice_len
    query_pos = lengths[:, None] - drafts + jnp.arange(drafts, dtype=jnp.int32)[None, :]
    key_pos = first_key + jnp.arange(slice_len, dtype=jnp.int32)
    is_visible = (key_pos[None, None, :] <= query_pos[:, :, None])[:, None, None, :, :]
    query_heads = queries.reshape(row_count, drafts, kv_local, group_size, HD)
    key_heads = cache_keys.reshape(row_count, slice_len, kv_local, HD)
    value_heads = cache_values.reshape(row_count, slice_len, kv_local, HD)
    scores = jnp.einsum(
        "rqkgd,rskd->rkgqs", query_heads, key_heads, preferred_element_type=jnp.float32
    )
    scores = scores * (1.0 / math.sqrt(HD))
    masked = jnp.where(is_visible, scores, NEG_FILL)
    local_max = jnp.max(masked, axis=-1)
    weights = jnp.where(is_visible, jnp.exp(masked - local_max[..., None]), 0.0)
    local_total = jnp.sum(weights, axis=-1)
    local_acc = jnp.einsum(
        "rkgqs,rskd->rkgqd",
        weights.astype(jnp.bfloat16),
        value_heads,
        preferred_element_type=jnp.float32,
    )
    joint_max, joint_total, joint_acc = joined(
        (local_max, local_total, local_acc), "kvseq", combine_partials
    )
    heads_out = joint_acc / joint_total[..., None]
    attn = (
        heads_out.transpose(0, 3, 1, 2, 4)
        .reshape(row_count * drafts, query_width)
        .astype(jnp.bfloat16)
    )
    partial_proj = jnp.dot(attn, out_weight, preferred_element_type=jnp.float32)
    projected = lax.psum_scatter(
        partial_proj.astype(jnp.bfloat16), "head", scatter_dimension=1, tiled=True
    ).astype(jnp.float32)
    mixed = (residual_in.astype(jnp.float32) + projected).astype(jnp.bfloat16)
    mixed_wide = mixed.astype(jnp.float32)
    local_squares = jnp.sum(mixed_wide * mixed_wide, axis=1)
    all_squares = lax.psum(local_squares, ("kvseq", "head"))
    inv_rms = lax.rsqrt(all_squares / D + EPSILON)
    normed = (mixed_wide * inv_rms[:, None] * norm_gain.astype(jnp.float32)[None, :]).astype(
        jnp.bfloat16
    )
    piece = lax.all_gather(normed, ("kvseq", "head"), axis=1, tiled=True)
    gate = jnp.dot(piece, gate_weight, preferred_element_type=jnp.float32)
    upward = jnp.dot(piece, up_weight, preferred_element_type=jnp.float32)
    hidden = (jax.nn.silu(gate) * upward).astype(jnp.bfloat16)
    ffn_terms = jnp.dot(hidden, down_weight, preferred_element_type=jnp.float32)
    ffn_part = lax.psum_scatter(ffn_terms, ("kvseq", "head"), scatter_dimension=1, tiled=True)
    return (mixed_wide + ffn_part).astype(jnp.bfloat16)


def solution(mesh):
    placed = (
        P(),
        P(None, None, "head"),
        P(None, "kvseq", "head"),
        P(None, "kvseq", "head"),
        P(None, ("kvseq", "head")),
        P("head", "kvseq"),
        P(("kvseq", "head")),
        P(None, ("kvseq", "head")),
        P(None, ("kvseq", "head")),
        P(("kvseq", "head"), None),
    )
    return jax.shard_map(
        shards, mesh=mesh, in_specs=placed, out_specs=P(None, ("kvseq", "head")), check_vma=False
    )
```

profile of v0, /device:TPU:2, one launch (start us, length us, event | category | flops | bytes accessed | tf_op | source)
XLA Modules:
  0.0 1652.9 jit_solution(10699537784383209612)
XLA Ops:
  6.5 0.0 copy-start
  6.5 0.8 broadcast_add_fusion
  7.3 0.1 iota_add_fusion.1
  7.4 0.1 broadcast_compare_fusion
  7.6 0.6 copy-done
  8.1 1.9 fusion.5
  10.1 2.0 copy-done.1
  12.0 1.7 fusion.18
  13.8 0.0 all-gather.8.cloned.1.call-update
  13.8 0.0 reduce-scatter.3.cloned.1.call-start
  13.9 52.6 %all-gather = bf16[128,8,16]{2,1,0:T(8,128)(2,1)S(1)} all-gather(bf16[4,8,16]{2,1,0:T(8,128)(2,1)S(1)} %convert_element_type.179), channel_id=2, replica_groups=mesh['kvseq'=32,'head'=8] {'kvseq'}, dimensions={0}, use_global_device_ids=true | all-gather | bytes 33792 | tf_op jit(solution)/shard_map/all_gather | solution.py:20
  66.4 3.5 fusion.7
  69.9 48.4 %all-gather.1 = bf16[128,8,16]{2,1,0:T(8,128)(2,1)S(1)} all-gather(bf16[4,8,16]{2,1,0:T(8,128)(2,1)S(1)} %fusion.7), channel_id=3, replica_groups=mesh['kvseq'=32,'head'=8] {'kvseq'}, dimensions={0}, use_global_device_ids=true | all-gather | bytes 33792 | tf_op jit(solution)/shard_map/all_gather | solution.py:20
  118.4 0.0 all-gather.8.cloned.1.call-done
  118.4 0.9 fusion.29
  119.3 39.4 %while.19 = (s32[]{:T(128)}, f32[4,1,8,16]{3,2,1,0:T(8,128)S(1)}, f32[4,1,8,16]{3,2,1,0:T(8,128)S(1)}, f32[4,1,8,16,128]{4,3,2,1,0:T(8,128)S(1)}, bf16[32,4,1,8,...) while((s32[]{:T(128)}, f32[4,1,8,16]{3,2,1,0:T(8,128)S(1)}, ...), condition=%wide.region_3.4_spmd, body=%wide.region_2.3_spmd.sunk | while | flops 267269 | bytes 683155 | solution.py:28
  119.4 1.2 fusion.60
  120.7 1.2 fusion.60
  121.9 1.2 fusion.60
  123.2 1.2 fusion.60
  124.5 1.2 fusion.60
  125.7 1.2 fusion.60
  127.0 1.2 fusion.60
  128.3 1.2 fusion.60
  129.6 1.2 fusion.60
  130.8 1.2 fusion.60
  132.1 1.2 fusion.60
  133.4 1.2 fusion.60
  134.6 1.2 fusion.60
  135.9 1.2 fusion.60
  137.2 1.2 fusion.60
  138.5 1.2 fusion.60
  139.7 1.2 fusion.60
  141.0 1.2 fusion.60
  142.3 1.2 fusion.60
  143.5 1.2 fusion.60
  144.8 1.2 fusion.60
  146.1 1.2 fusion.60
  147.4 1.2 fusion.60
  148.6 1.2 fusion.60
  149.9 1.2 fusion.60
  151.2 1.2 fusion.60
  152.4 1.2 fusion.60
  153.7 1.2 fusion.60
  155.0 1.2 fusion.60
  156.2 1.2 fusion.60
  157.5 1.2 fusion.60
  158.7 0.1 fusion.30
  158.9 0.0 copy-done.2
  158.9 1.0 convolution_convert_fusion
  159.9 0.0 reduce-scatter.3.cloned.1.call-update
  159.9 0.0 all-gather.6.cloned.1.call-start
  160.0 26.8 %reduce-scatter.3.cloned.1.call-done = bf16[64,32]{0,1:T(8,128)(2,1)} async-done(((bf16[64,256]{0,1:T(8,128)(2,1)}), bf16[64,32]{0,1:T(8,128)(2,1)}) %reduce-scatter.3.cloned.1.call-update) | async-done | bytes 4112 | tf_op jit(solution)/shard_map/reduce_scatter | solution.py:93
  186.8 0.7 fusion.36
  187.5 77.2 %psum.7 = f32[64]{0:T(128)S(1)} all-reduce(f32[64]{0:T(128)S(1)} %fusion.36), channel_id=1, replica_groups=mesh['kvseq'=32,'head'=8] {'kvseq','head'}, use_global_device_ids=true, to_apply=%region_6.7 | all-reduce | flops 64 | bytes 512 | tf_op jit(solution)/shard_map/psum | solution.py:99
  264.7 1.4 fusion.38
  266.1 0.0 all-gather.6.cloned.1.call-update
  266.1 0.0 reduce-scatter.5.cloned.1.call-start
  266.1 102.0 %all-gather.6.cloned.1.call-done = bf16[64,8192]{0,1:T(8,128)(2,1)} async-done(((bf16[64,32]{0,1:T(8,128)(2,1)}), bf16[64,8192]{0,1:T(8,128)(2,1)}) %all-gather.6.cloned.1.call-update) | async-done | bytes 1048592 | tf_op jit(solution)/shard_map/all_gather | solution.py:104
  368.2 2.8 fusion.47
  371.0 6.9 fusion.24
  377.9 0.0 reduce-scatter.5.cloned.1.call-update
  377.9 1267.1 %reduce-scatter.5.cloned.1.call-done = f32[64,32]{0,1:T(8,128)} async-done(((f32[64,8192]{0,1:T(8,128)}), f32[64,32]{0,1:T(8,128)}) %reduce-scatter.5.cloned.1.call-update) | async-done | bytes 8208 | tf_op jit(solution)/shard_map/reduce_scatter | solution.py:109
  1645.0 1.3 fusion.39
  (111 shorter events, 1.4 us)
Async XLA Ops:
  6.5 1.6 copy-start
  6.5 111.8 %all-gather.8.cloned.1.call-start = ((), (), s32[]{:S(2)}) async-start(), calls=%async_computation.5 | async-start | bytes 4325376 | tf_op jit(solution)/shard_map/all_gather | solution.py:20
  8.1 3.9 copy-start.5
  10.1 2.0 copy-start.1
  13.8 173.0 %reduce-scatter.3.cloned.1.call-start = ((), (), s32[]{:S(2)}) async-start(), calls=%async_computation.2 | async-start | bytes 73728 | tf_op jit(solution)/shard_map/reduce_scatter | solution.py:93
  66.4 92.5 %copy-start.2 = (bf16[1024,256]{1,0:T(8,128)(2,1)S(1)}, bf16[1024,256]{1,0:T(8,128)(2,1)}, u32[]{:S(2)}) copy-start(bf16[1024,256]{1,0:T(8,128)(2,1)} %param.17) | copy-start | bytes 1572868
  69.9 90.0 %copy-start.6 = (bf16[32]{0:T(256)(128)(2,1)S(1)}, bf16[32]{0:T(256)(128)(2,1)}, u32[]{:S(2)}) copy-start(bf16[32]{0:T(256)(128)(2,1)} %param.18) | copy-start | bytes 196
  69.9 116.8 %copy-start.3 = (bf16[64,32]{0,1:T(8,128)(2,1)S(1)}, bf16[64,32]{0,1:T(8,128)(2,1)}, u32[]{:S(2)}) copy-start(bf16[64,32]{0,1:T(8,128)(2,1)} %param.16) | copy-start | bytes 12292
  159.9 208.3 %all-gather.6.cloned.1.call-start = ((), (), s32[]{:S(2)}) async-start(), calls=%async_computation.3 | async-start | bytes 2105344 | tf_op jit(solution)/shard_map/all_gather | solution.py:104
  266.1 1378.9 %reduce-scatter.5.cloned.1.call-start = ((), (), s32[]{:S(2)}) async-start(), calls=%async_computation.4 | async-start | bytes 4210688 | tf_op jit(solution)/shard_map/reduce_scatter | solution.py:109
  377.9 1267.1 %copy-start.4 = (bf16[64,32]{0,1:T(8,128)(2,1)S(1)}, bf16[64,32]{0,1:T(8,128)(2,1)}, u32[]{:S(2)}) copy-start(bf16[64,32]{0,1:T(8,128)(2,1)} %reduce-scatter.3.cloned.1.call-done) | copy-start | bytes 12292
Sparse Core Ops, SparseCore 0:
  13.9 85.3 all-gather.7
  160.0 26.6 reduce-scatter.2
  266.2 101.8 all-gather.5
  378.0 1266.9 reduce-scatter.4
where the time goes:
time: 1660 us; the launch traced here: 1650 us
  waiting for transfers between devices  1400 us (84%)
  blocking collectives  178 us (11%)
  other arithmetic  46.8 us (3%)
    reduce_scatter x1, waiting for transfers between devices, shards(): lax.psum_scatter(ffn_terms, ('kvseq', 'head'), scatter_dimension=1, tiled...  1270 us
    all_gather x1, waiting for transfers between devices, shards(): piece = lax.all_gather(normed, ('kvseq', 'head'), axis=1, tiled=True)  102 us
    all_gather x2, blocking collectives, joined(): lax.all_gather(part.astype(kind), axis)  101 us
    psum x1, blocking collectives, shards(): all_squares = lax.psum(local_squares, ('kvseq', 'head'))  77.2 us
    add x31, other arithmetic, combine_partials(): acc_one * factor_one[..., None] + acc_two * factor_two[..., None]  36.6 us
  transfers between devices with their start and end apart: 4, of which 3 were waited for; matrix products, arithmetic and copies ran while one was open for 0% of the time, Pallas kernels for 0%

commit v1 on v0

v1 whole, which is shorter than its diff:
```python
import functools
import math

import jax
import jax.numpy as jnp
from jax import lax
from jax.experimental import pallas as pl
from jax.experimental.pallas import tpu as pltpu
from jax.sharding import Mesh, PartitionSpec as P

D = 8192
FF = 28672
HD = 128
GROUP = 8
ROWS = 4
DRAFTS = 16
TOKENS = 64
KV = 32
SLICE = 2048
CHUNK = 512
NEG = -1e30
FLOOR = -1e29
EPSILON = 1e-05
LOG_SCALE = math.log2(math.e) / math.sqrt(HD)
MIB = 1024 * 1024
F32 = jnp.float32
BF16 = jnp.bfloat16
VMEM = pl.BlockSpec(memory_space=pltpu.VMEM)
SMEM = pl.BlockSpec(memory_space=pltpu.SMEM)


def nt(a, b):
    return lax.dot_general(a, b, (((1,), (1,)), ((), ())), preferred_element_type=F32)


def nn(a, b):
    return jnp.dot(a, b, preferred_element_type=F32)


def lanes(shape):
    return lax.broadcasted_iota(jnp.int32, shape, len(shape) - 1)


def attend(place_ref, lengths_ref, gain_ref, q_ref, k_ref, v_ref, out_ref, score_ref):
    row = pl.program_id(0)
    first_key = place_ref[0] * SLICE
    length = lengths_ref[row]
    queries = jnp.concatenate(
        [q_ref[0, :, g * HD : (g + 1) * HD] for g in range(GROUP)], axis=0
    )
    draft = lax.broadcasted_iota(jnp.int32, (GROUP * DRAFTS, CHUNK), 0) % DRAFTS
    limit = length - DRAFTS + draft - first_key - lanes((GROUP * DRAFTS, CHUNK))
    peak = jnp.full((GROUP * DRAFTS, HD), NEG, F32)
    for n in range(SLICE // CHUNK):
        scores = nt(queries, k_ref[0, n * CHUNK : (n + 1) * CHUNK, :]) * LOG_SCALE
        scores = jnp.where(limit >= n * CHUNK, scores, NEG)
        score_ref[:, n * CHUNK : (n + 1) * CHUNK] = scores
        for i in range(CHUNK // HD):
            peak = jnp.maximum(peak, scores[:, i * HD : (i + 1) * HD])
    top = jnp.max(peak, axis=1, keepdims=True).astype(BF16).astype(F32)
    base = jnp.maximum(top, FLOOR)
    acc = jnp.zeros((GROUP * DRAFTS, HD), F32)
    sums = jnp.zeros((GROUP * DRAFTS, HD), F32)
    for n in range(SLICE // CHUNK):
        weights = jnp.exp2(score_ref[:, n * CHUNK : (n + 1) * CHUNK] - base)
        for i in range(CHUNK // HD):
            sums = sums + weights[:, i * HD : (i + 1) * HD]
        acc = acc + nn(weights.astype(BF16), v_ref[0, n * CHUNK : (n + 1) * CHUNK, :])
    total = jnp.sum(sums, axis=1, keepdims=True)
    lane = lanes((GROUP * DRAFTS, HD))
    gain = jnp.broadcast_to(gain_ref[...].astype(F32), (GROUP * DRAFTS, HD))
    stats = jnp.where(lane < 32, top, jnp.where(lane < 64, total, gain))
    out_ref[:, 0:16, :] = acc.astype(BF16).reshape(GROUP, DRAFTS, HD)
    out_ref[:, 16:32, :] = stats.astype(BF16).reshape(GROUP, DRAFTS, HD)


def attention(place, lengths, gain_row, queries, keys, values):
    return pl.pallas_call(
        attend,
        grid=(ROWS,),
        in_specs=[
            SMEM,
            SMEM,
            pl.BlockSpec((1, HD), lambda r: (0, 0)),
            pl.BlockSpec((1, DRAFTS, GROUP * HD), lambda r: (r, 0, 0)),
            pl.BlockSpec((1, SLICE, HD), lambda r: (r, 0, 0)),
            pl.BlockSpec((1, SLICE, HD), lambda r: (r, 0, 0)),
        ],
        out_specs=pl.BlockSpec((GROUP, 32, HD), lambda r: (r, 0, 0)),
        out_shape=jax.ShapeDtypeStruct((KV, 32, HD), BF16),
        scratch_shapes=[pltpu.VMEM((GROUP * DRAFTS, SLICE), F32)],
        compiler_params=pltpu.CompilerParams(vmem_limit_bytes=16 * MIB),
        name="attention",
    )(place, lengths, gain_row, queries, keys, values)


def combine(in_ref, attn_ref, gain_ref):
    top = in_ref[:, 16:32, 0:1].astype(F32)
    total = in_ref[:, 16:32, 32:33].astype(F32)
    joint = jnp.max(top, axis=0, keepdims=True)
    factor = jnp.exp2(top - joint)
    whole = jnp.sum(total * factor, axis=0)
    acc = jnp.sum(in_ref[:, 0:16, :].astype(F32) * factor, axis=0)
    attn = (acc / whole).astype(BF16)
    attn_ref[...] = jnp.broadcast_to(attn[None], (KV, DRAFTS, HD))
    pick = lanes((KV, KV * 16)) == 16 * lax.broadcasted_iota(jnp.int32, (KV, KV * 16), 0)
    stats = in_ref[:, 16:32, :].reshape(KV * 16, HD)
    gain_ref[...] = nn(pick.astype(F32).astype(BF16), stats).astype(BF16)


def combined(parts):
    return pl.pallas_call(
        combine,
        in_specs=[VMEM],
        out_specs=[VMEM, VMEM],
        out_shape=[
            jax.ShapeDtypeStruct((KV, DRAFTS, HD), BF16),
            jax.ShapeDtypeStruct((KV, HD), BF16),
        ],
        compiler_params=pltpu.CompilerParams(vmem_limit_bytes=16 * MIB),
        name="combine",
    )(parts)


def project(place_ref, attn_ref, weight_ref, residual_ref, gain_ref, own_ref, other_ref):
    core = place_ref[2]
    head = place_ref[1] * 2 + core
    attn = jnp.concatenate(
        [
            jnp.concatenate([attn_ref[r * GROUP + g] for g in range(GROUP)], axis=1)
            for r in range(ROWS)
        ],
        axis=0,
    )
    spread = nn(attn, weight_ref[...])
    source = lax.broadcasted_iota(jnp.int32, (32, 256), 0)
    put = (lanes((32, 256)) == head * 32 + source).astype(F32).astype(BF16)
    spread = spread + nn(residual_ref[...], put)
    source = lax.broadcasted_iota(jnp.int32, (HD, 256), 0)
    put = ((lanes((HD, 256)) == head * 32 + source - 64) & (source >= 64) & (source < 96))
    gain = nn(gain_ref[...], put.astype(F32).astype(BF16))
    both = jnp.concatenate([spread, gain], axis=0)
    own_ref[...] = jnp.where(core == 0, both[:, :HD], both[:, HD:])
    other_ref[...] = jnp.where(core == 0, both[:, HD:], both[:, :HD]).astype(BF16)


def projected(place, attn, weight, residual, gain):
    return pl.pallas_call(
        project,
        in_specs=[SMEM, VMEM, VMEM, VMEM, VMEM],
        out_specs=[VMEM, VMEM],
        out_shape=[
            jax.ShapeDtypeStruct((TOKENS + KV, HD), F32),
            jax.ShapeDtypeStruct((TOKENS + KV, HD), BF16),
        ],
        compiler_params=pltpu.CompilerParams(vmem_limit_bytes=16 * MIB),
        name="project",
    )(place, attn, weight, residual, gain)


def mix(a_ref, b_ref, c_ref, d_ref, mixed_ref, gain_ref):
    total = (a_ref[...].astype(F32) + b_ref[...].astype(F32)) + (
        c_ref[...].astype(F32) + d_ref[...].astype(F32)
    )
    mixed = total[:TOKENS].astype(BF16)
    mixed_ref[...] = jnp.broadcast_to(mixed[None], (KV, TOKENS, HD))
    gain_ref[...] = total[TOKENS:].astype(BF16)


def mixing(parts):
    return pl.pallas_call(
        mix,
        in_specs=[VMEM] * 4,
        out_specs=[VMEM, VMEM],
        out_shape=[
            jax.ShapeDtypeStruct((KV, TOKENS, HD), BF16),
            jax.ShapeDtypeStruct((KV, HD), BF16),
        ],
        compiler_params=pltpu.CompilerParams(vmem_limit_bytes=16 * MIB),
        name="mix",
    )(*parts)


def feed(
    place_ref, own_ref, other_ref, own_gain_ref, other_gain_ref,
    gate_ref, up_ref, down_ref, own_out_ref, other_out_ref,
):
    core = place_ref[2]
    squares = jnp.zeros((TOKENS, HD), F32)
    for k in range(KV):
        a = own_ref[k].astype(F32)
        b = other_ref[k].astype(F32)
        squares = squares + a * a + b * b
    scale = lax.rsqrt(jnp.sum(squares, axis=1, keepdims=True) / D + EPSILON)
    gate = jnp.zeros((TOKENS, gate_ref.shape[1]), F32)
    upward = jnp.zeros((TOKENS, gate_ref.shape[1]), F32)
    for k in range(KV):
        a = own_ref[k].astype(F32) * scale * own_gain_ref[k : k + 1, :].astype(F32)
        b = other_ref[k].astype(F32) * scale * other_gain_ref[k : k + 1, :].astype(F32)
        left = jnp.where(core == 0, a, b)
        right = jnp.where(core == 0, b, a)
        normed = jnp.concatenate([left, right], axis=1).astype(BF16)
        gate = gate + nn(normed, gate_ref[k * 256 : (k + 1) * 256, :])
        upward = upward + nn(normed, up_ref[k * 256 : (k + 1) * 256, :])
    hidden = (gate / (1.0 + jnp.exp(-gate)) * upward).astype(BF16)
    for k in range(KV):
        terms = nn(hidden, down_ref[:, k * 256 : (k + 1) * 256]).astype(BF16)
        own_out_ref[k] = jnp.where(core == 0, terms[:, :HD], terms[:, HD:])
        other_out_ref[k] = jnp.where(core == 0, terms[:, HD:], terms[:, :HD])


def feeding(place, own, other, own_gain, other_gain, gate_weight, up_weight, down_weight):
    shape = jax.ShapeDtypeStruct((KV, TOKENS, HD), BF16)
    return pl.pallas_call(
        feed,
        in_specs=[SMEM] + [VMEM] * 7,
        out_specs=[VMEM, VMEM],
        out_shape=[shape, shape],
        compiler_params=pltpu.CompilerParams(vmem_limit_bytes=32 * MIB),
        name="feed",
    )(place, own, other, own_gain, other_gain, gate_weight, up_weight, down_weight)


def gather_sum(in_ref, out_ref):
    total = in_ref[0].astype(F32)
    for k in range(1, KV):
        total = total + in_ref[k].astype(F32)
    out_ref[...] = jnp.broadcast_to(total.astype(BF16)[None], (8, TOKENS, HD))


def summed(parts):
    return pl.pallas_call(
        gather_sum,
        in_specs=[VMEM],
        out_specs=VMEM,
        out_shape=jax.ShapeDtypeStruct((8, TOKENS, HD), BF16),
        compiler_params=pltpu.CompilerParams(vmem_limit_bytes=16 * MIB),
        name="gather_sum",
    )(parts)


def finish(place_ref, parts_ref, own_ref, other_ref, out_ref):
    kv, x, core = place_ref[0], place_ref[1], place_ref[2]
    half = x // 2
    total = jnp.zeros((TOKENS, HD), F32)
    for i in range(4):
        total = total + parts_ref[2 * i + half].astype(F32)
    mixed = jnp.where(half == core, own_ref[kv].astype(F32), other_ref[kv].astype(F32))
    both = mixed + total
    which = (x * 2 + core) % 4
    out = both[:, 0:32]
    for i in range(1, 4):
        out = jnp.where(which == i, both[:, i * 32 : (i + 1) * 32], out)
    out_ref[...] = out.astype(BF16)


def finished(place, parts, own, other):
    return pl.pallas_call(
        finish,
        in_specs=[SMEM] + [VMEM] * 3,
        out_specs=VMEM,
        out_shape=jax.ShapeDtypeStruct((TOKENS, 32), BF16),
        compiler_params=pltpu.CompilerParams(vmem_limit_bytes=16 * MIB),
        name="finish",
    )(place, parts, own, other)


SWAP = [(0, 1), (1, 0)]


def exchange(parts, axes):
    return lax.all_to_all(parts, axes, 0, 0, tiled=True)


def shards(
    lengths,
    queries,
    cache_keys,
    cache_values,
    residual_in,
    out_weight,
    norm_gain,
    gate_weight,
    up_weight,
    down_weight,
):
    place = jnp.stack(
        [lax.axis_index(("z", "y")), lax.axis_index("x"), lax.axis_index("c")]
    ).astype(jnp.int32)
    gain_row = jnp.tile(norm_gain, 4).reshape(1, HD)
    parts = attention(place, lengths, gain_row, queries, cache_keys, cache_values)
    attn, gain = combined(exchange(parts, ("z", "y")))
    attn = exchange(attn, ("z", "y"))
    own, other = projected(place, attn, out_weight, residual_in, gain)
    pair = (own + lax.ppermute(other, "c", SWAP).astype(F32)).astype(BF16)
    around = [lax.ppermute(pair, "x", [(i, (i + s) % 4) for i in range(4)]) for s in (1, 2, 3)]
    mixed, own_gain = mixing([pair] + around)
    other_gain = lax.ppermute(own_gain, "c", SWAP)
    own_mixed = exchange(mixed, ("z", "y"))
    other_mixed = lax.ppermute(own_mixed, "c", SWAP)
    own_terms, other_terms = feeding(
        place, own_mixed, other_mixed, own_gain, other_gain, gate_weight, up_weight, down_weight
    )
    terms = own_terms.astype(F32) + lax.ppermute(other_terms, "c", SWAP).astype(F32)
    terms = summed(exchange(terms.astype(BF16), ("z", "y")))
    return finished(place, exchange(terms, ("x", "c")), own_mixed, other_mixed)


def solution(mesh):
    fine = Mesh(mesh.devices.reshape(8, 4, 4, 2), ("z", "y", "x", "c"))
    kvseq, head = ("z", "y"), ("x", "c")
    every = kvseq + head
    placed = (
        P(),
        P(None, None, head),
        P(None, kvseq, head),
        P(None, kvseq, head),
        P(None, every),
        P(head, kvseq),
        P(every),
        P(None, every),
        P(None, every),
        P(every, None),
    )
    return jax.shard_map(
        shards, mesh=fine, in_specs=placed, out_specs=P(None, every), check_vma=False
    )
```

time: 1660 us -> 129 us (0.08)
  waiting for transfers between devices: 1400 us -> 15.6 us
  blocking collectives: 178 us -> 76.2 us
  other arithmetic: 46.8 us -> 0.27 us
    reduce_scatter x2 -> x0, waiting for transfers between devices: 1290 us -> none  [the longest x1 1270 us: shards(): lax.psum_scatter(ffn_terms, ('kvseq', 'head'), scatter_dimension=1, tiled...]
    all_gather x2 -> x0, waiting for transfers between devices: 102 us -> none  [the longest x1 102 us: shards(): piece = lax.all_gather(normed, ('kvseq', 'head'), axis=1, tiled=True)]
    all_gather x2 -> x0, blocking collectives: 101 us -> none  [joined(): lax.all_gather(part.astype(kind), axis)]
    psum x1 -> x0, blocking collectives: 77.2 us -> none  [shards(): all_squares = lax.psum(local_squares, ('kvseq', 'head'))]
    all_to_all x0 -> x4, blocking collectives: none -> 76.2 us  [exchange(): return lax.all_to_all(parts, axes, 0, 0, tiled=True)]
    add x33 -> x0, other arithmetic: 36.7 us -> none  [the longest x31 36.6 us: combine_partials(): acc_one * factor_one[..., None] + acc_two * factor_two[..., None]]
  transfers between devices with their start and end apart: 4 -> 8, of which waited for: 3 -> 5; matrix products, arithmetic and copies ran while one was open for 0% -> 6% of each run, Pallas kernels for 0% -> 0%
where the time goes in v1:
time: 129 us; the launch traced here: 127 us
  blocking collectives  76.2 us (59%)
  local copies, waits for them, and re-layouts  16.5 us (13%)
  waiting for transfers between devices  15.6 us (12%)
  starting transfers between devices  9.62 us (7%)
  Pallas kernels  8.67 us (7%)
    all_to_all x4, blocking collectives, exchange(): return lax.all_to_all(parts, axes, 0, 0, tiled=True)  76.2 us
    unnamed x19, local copies, waits for them, and re-layouts  15.1 us
    all_to_all x1, waiting for transfers between devices, exchange(): return lax.all_to_all(parts, axes, 0, 0, tiled=True)  10.5 us
    ppermute x3, starting transfers between devices, shards(): lax.ppermute(pair, 'x', [(i, (i + s) % 4) for i in range(4)])  4.83 us
    all_to_all x1, starting transfers between devices, exchange(): return lax.all_to_all(parts, axes, 0, 0, tiled=True)  4.09 us
    pallas_call x1, Pallas kernels, attention(): pl.pallas_call(attend, grid=(ROWS,), in_specs=[SMEM, SMEM, pl.BlockSpec((...  3.66 us
  transfers between devices with their start and end apart: 8, of which 5 were waited for; matrix products, arithmetic and copies ran while one was open for 6% of the time, Pallas kernels for 0%

profile of v1, /device:TPU:2, one launch (start us, length us, event | category | flops | bytes accessed | tf_op | source)
XLA Modules:
  0.0 127.0 jit_solution(11737830963528565447)
XLA Ops:
  0.0 0.7 tile.2
  0.7 0.1 reshape_tile.3.gain_ref
  0.7 0.1 pad_add_fusion.place_ref
  0.8 0.0 copy-start.1
  0.8 1.6 %copy-done.1 = bf16[4,2048,128]{2,1,0:T(8,128)(2,1)S(1)} copy-done((bf16[4,2048,128]{2,1,0:T(8,128)(2,1)S(1)}, bf16[4,2048,128]{2,1,0:T(8,128)(2,1)}, u32[]{:S(2)}) %copy-start.1) | copy-done | bytes 2097176
  2.4 0.0 copy-start.2
  2.4 1.6 %copy-done.2 = bf16[4,2048,128]{2,1,0:T(8,128)(2,1)S(1)} copy-done((bf16[4,2048,128]{2,1,0:T(8,128)(2,1)S(1)}, bf16[4,2048,128]{2,1,0:T(8,128)(2,1)}, u32[]{:S(2)}) %copy-start.2) | copy-done | bytes 2097176
  4.0 0.0 copy-start.5
  4.0 0.9 copy-done.5
  4.9 0.0 copy-start.6
  4.9 0.7 copy-done.6
  5.6 0.0 copy-start.7
  5.6 0.0 copy-start.4
  5.6 3.7 %attention.1 = bf16[32,32,128]{2,1,0:T(8,128)(2,1)S(1)} custom-call(s32[3]{0:T(128)S(1)} %pad_add_fusion.place_ref, s32[4]{0:T(128)S(1)} %copy-done.6, bf16[1,128]{1,0:T(2,128)(2,1)S(1)} %reshape_tile.3.gain_ref, bf16[4,16,1024]{2,1,0:T(8,128)(2,1)S(1)} %copy-done.5, bf16[4,2048,128]{2,1,0:T(8,128)(2,1)S(1)} %copy-done.1, bf16[4,2048,128]{2,1,0:T(8,128)(2,1)S(1)} %copy-done.2), custom_call_target="tpu_custom_call" | custom-call | tf_op jit(solution)/shard_map/attention/pallas_call | solution.py:78
  9.2 24.0 %all_to_all.25.in_ref = bf16[32,32,128]{2,1,0:T(8,128)(2,1)S(1)} all-to-all(bf16[32,32,128]{2,1,0:T(8,128)(2,1)S(1)} %attention.1), channel_id=1, replica_groups=mesh['z'=8,'y'=4,'x'=4,'c'=2] {'z','y'}, dimensions={0} | all-to-all | bytes 524288 | tf_op jit(solution)/shard_map/all_to_all | solution.py:272
  33.2 0.9 combine.1
  34.1 4.1 %all-to-all-start.1 = ((bf16[32,16,128]{2,1,0:T(8,128)(2,1)}), bf16[32,16,128]{2,1,0:T(8,128)(2,1)S(1)}, u32[]{:S(2)}, u32[]{:S(2)}) async-start(bf16[32,16,128]{2,1,0:T(8,128)(2,1)} %get-tuple-element.13), calls=%async_computation.1 | async-start | bytes 262144 | tf_op jit(solution)/shard_map/all_to_all | solution.py:272
  38.2 0.0 copy-done.7
  38.3 0.1 copy.11.residual_ref
  38.4 10.5 %all-to-all-done.1.attn_ref = bf16[32,16,128]{2,1,0:T(8,128)(2,1)S(1)} async-done(((bf16[32,16,128]{2,1,0:T(8,128)(2,1)}), bf16[32,16,128]{2,1,0:T(8,128)(2,1)S(1)}, u32[]{:S(2)}, u32[]{:S(2)}) %all-to-all-start.1) | async-done | bytes 131104 | tf_op jit(solution)/shard_map/all_to_all | solution.py:272
  48.9 0.0 copy-done.4
  48.9 0.8 project.1
  49.6 0.1 collective-permute-start
  49.7 1.2 collective-permute-done
  50.9 0.6 collective-permute-start.3
  51.5 2.4 %collective-permute-start.2 = (bf16[96,128]{1,0:T(8,128)(2,1)S(1)}, bf16[96,128]{1,0:T(8,128)(2,1)S(1)}, u32[]{:S(2)}, u32[]{:S(2)}) collective-permute-start(bf16[96,128]{1,0:T(8,128)(2,1)S(1)} %add_convert_fusion.1.a_ref), channel_id=1, source_target_pairs={{0,4},{2,6},{4,0},{6,2},{1,5},{3,7},{5,1},{7,3},{8,12},{10,14},{12... | collective-permute-start | bytes 73736 | tf_op jit(solution)/shard_map/ppermute | solution.py:296
  54.0 1.8 %collective-permute-start.1 = (bf16[96,128]{1,0:T(8,128)(2,1)S(1)}, bf16[96,128]{1,0:T(8,128)(2,1)S(1)}, u32[]{:S(2)}, u32[]{:S(2)}) collective-permute-start(bf16[96,128]{1,0:T(8,128)(2,1)S(1)} %add_convert_fusion.1.a_ref), channel_id=1, source_target_pairs={{0,2},{2,4},{4,6},{6,0},{1,3},{3,5},{5,7},{7,1},{8,10},{10,12},{12... | collective-permute-start | bytes 73736 | tf_op jit(solution)/shard_map/ppermute | solution.py:296
  55.8 0.0 collective-permute-done.3.d_ref
  55.8 1.1 collective-permute-done.2.c_ref
  56.9 0.9 collective-permute-done.1.b_ref
  57.8 0.1 mix.1
  57.9 20.4 %all_to_all.26.own_ref = bf16[32,64,128]{2,1,0:T(8,128)(2,1)S(1)} all-to-all(bf16[32,64,128]{2,1,0:T(8,128)(2,1)S(1)} %get-tuple-element.17), channel_id=1, replica_groups=mesh['z'=8,'y'=4,'x'=4,'c'=2] {'z','y'}, dimensions={0} | all-to-all | bytes 1048576 | tf_op jit(solution)/shard_map/all_to_all | solution.py:272
  78.3 0.0 collective-permute-start.4
  78.3 0.5 collective-permute-start.5
  78.8 3.2 %copy.12.gate_ref = bf16[8192,112]{1,0:T(8,128)(2,1)S(1)} copy(bf16[8192,112]{0,1:T(8,128)(2,1)} %param.17) | data formatting | bytes 3670016 | tf_op args[7]
  82.0 4.0 %copy.13.up_ref = bf16[8192,112]{1,0:T(8,128)(2,1)} copy(bf16[8192,112]{0,1:T(8,128)(2,1)} %param.18) | data formatting | bytes 3670016 | tf_op args[8]
  86.0 0.0 collective-permute-done.5.other_gain_ref
  86.0 0.0 collective-permute-done.4.other_ref
  86.0 0.0 copy-start
  86.0 1.6 %copy-done = bf16[8192,112]{1,0:T(8,128)(2,1)S(1)} copy-done((bf16[8192,112]{1,0:T(8,128)(2,1)S(1)}, bf16[8192,112]{1,0:T(8,128)(2,1)}, u32[]{:S(2)}) %copy-start) | copy-done | bytes 1835032
  87.6 0.0 copy-start.3
  87.6 1.5 %copy-done.3 = bf16[112,8192]{1,0:T(8,128)(2,1)S(1)} copy-done((bf16[112,8192]{1,0:T(8,128)(2,1)S(1)}, bf16[112,8192]{1,0:T(8,128)(2,1)}, u32[]{:S(2)}) %copy-start.3) | copy-done | bytes 1835032
  89.1 2.3 %feed.1 = (bf16[32,64,128]{2,1,0:T(8,128)(2,1)S(1)}, bf16[32,64,128]{2,1,0:T(8,128)(2,1)S(1)}) custom-call(s32[3]{0:T(128)S(1)} %pad_add_fusion.place_ref, bf16[32,64,128]{2,1,0:T(8,128)(2,1)S(1)} %all_to_all.26.own_ref, bf16[32,64,128]{2,1,0:T(8,128)(2,1)S(1)} %collective-permute-done.4.other_ref, bf16[32,128]{1,0:T(8,128)(2,1)S(1)} %get-tuple-element.18.own_gain_ref, ...), custom_call_target="tpu_custom_call" | custom-call | tf_op jit(solution)/shard_map/feed/pallas_call | solution.py:214
  91.4 0.1 collective-permute-start.6
  91.5 1.9 %collective-permute-done.6 = bf16[32,64,128]{2,1,0:T(8,128)(2,1)S(1)} collective-permute-done((bf16[32,64,128]{2,1,0:T(8,128)(2,1)S(1)}, bf16[32,64,128]{2,1,0:T(8,128)(2,1)S(1)}, u32[]{:S(2)}, u32[]{:S(2)}) %collective-permute-start.6) | collective-permute-done | bytes 524320 | tf_op jit(solution)/shard_map/ppermute | solution.py:304
  93.4 0.2 add_convert_fusion
  93.6 22.0 %all_to_all.27.in_ref = bf16[32,64,128]{2,1,0:T(8,128)(2,1)S(1)} all-to-all(bf16[32,64,128]{2,1,0:T(8,128)(2,1)S(1)} %add_convert_fusion), channel_id=1, replica_groups=mesh['z'=8,'y'=4,'x'=4,'c'=2] {'z','y'}, dimensions={0} | all-to-all | bytes 1048576 | tf_op jit(solution)/shard_map/all_to_all | solution.py:272
  115.6 0.1 gather_sum.1
  115.7 9.8 %all_to_all.28.parts_ref = bf16[8,64,128]{2,1,0:T(8,128)(2,1)S(1)} all-to-all(bf16[8,64,128]{2,1,0:T(8,128)(2,1)S(1)} %gather_sum.1), channel_id=1, replica_groups=mesh['z'=8,'y'=4,'x'=4,'c'=2] {'x','c'}, dimensions={0} | all-to-all | bytes 262144 | tf_op jit(solution)/shard_map/all_to_all | solution.py:272
  125.5 0.8 finish.1
  126.3 0.7 copy.14
  (1 shorter events, 0.0 us)
Async XLA Ops:
  0.8 1.6 %copy-start.1 = (bf16[4,2048,128]{2,1,0:T(8,128)(2,1)S(1)}, bf16[4,2048,128]{2,1,0:T(8,128)(2,1)}, u32[]{:S(2)}) copy-start(bf16[4,2048,128]{2,1,0:T(8,128)(2,1)} %k_ref.1) | copy-start | bytes 6291460
  2.4 1.6 %copy-start.2 = (bf16[4,2048,128]{2,1,0:T(8,128)(2,1)S(1)}, bf16[4,2048,128]{2,1,0:T(8,128)(2,1)}, u32[]{:S(2)}) copy-start(bf16[4,2048,128]{2,1,0:T(8,128)(2,1)} %v_ref.1) | copy-start | bytes 6291460
  4.0 0.9 copy-start.5
  4.9 0.7 copy-start.6
  5.6 32.7 %copy-start.7 = (bf16[64,32]{0,1:T(8,128)(2,1)S(1)}, bf16[64,32]{0,1:T(8,128)(2,1)}, u32[]{:S(2)}) copy-start(bf16[64,32]{0,1:T(8,128)(2,1)} %param.14) | copy-start | bytes 12292
  5.6 43.3 %copy-start.4 = (bf16[1024,256]{1,0:T(8,128)(2,1)S(1)}, bf16[1024,256]{1,0:T(8,128)(2,1)}, u32[]{:S(2)}) copy-start(bf16[1024,256]{1,0:T(8,128)(2,1)} %weight_ref.1) | copy-start | bytes 1572868
  34.1 14.7 %all-to-all-start.1 = ((bf16[32,16,128]{2,1,0:T(8,128)(2,1)}), bf16[32,16,128]{2,1,0:T(8,128)(2,1)S(1)}, u32[]{:S(2)}, u32[]{:S(2)}) async-start(bf16[32,16,128]{2,1,0:T(8,128)(2,1)} %get-tuple-element.13), calls=%async_computation.1 | async-start | bytes 262144 | tf_op jit(solution)/shard_map/all_to_all | solution.py:272
  49.6 1.3 %collective-permute-start = (bf16[96,128]{1,0:T(8,128)(2,1)S(1)}, bf16[96,128]{1,0:T(8,128)(2,1)S(1)}, u32[]{:S(2)}, u32[]{:S(2)}) collective-permute-start(bf16[96,128]{1,0:T(8,128)(2,1)S(1)} %get-tuple-element.16), channel_id=1, source_target_pairs={{0,1},{1,0},{2,3},{3,2},{4,5},{5,4},{6,7},{7,6},{8,9},{9,8},{10,11... | collective-permute-start | bytes 73736 | tf_op jit(solution)/shard_map/ppermute | solution.py:295
  50.9 4.8 %collective-permute-start.3 = (bf16[96,128]{1,0:T(8,128)(2,1)S(1)}, bf16[96,128]{1,0:T(8,128)(2,1)S(1)}, u32[]{:S(2)}, u32[]{:S(2)}) collective-permute-start(bf16[96,128]{1,0:T(8,128)(2,1)S(1)} %add_convert_fusion.1.a_ref), channel_id=1, source_target_pairs={{0,6},{2,0},{4,2},{6,4},{1,7},{3,1},{5,3},{7,5},{8,14},{10,8},{12,... | collective-permute-start | bytes 73736 | tf_op jit(solution)/shard_map/ppermute | solution.py:296
  51.5 5.3 %collective-permute-start.2 = (bf16[96,128]{1,0:T(8,128)(2,1)S(1)}, bf16[96,128]{1,0:T(8,128)(2,1)S(1)}, u32[]{:S(2)}, u32[]{:S(2)}) collective-permute-start(bf16[96,128]{1,0:T(8,128)(2,1)S(1)} %add_convert_fusion.1.a_ref), channel_id=1, source_target_pairs={{0,4},{2,6},{4,0},{6,2},{1,5},{3,7},{5,1},{7,3},{8,12},{10,14},{12... | collective-permute-start | bytes 73736 | tf_op jit(solution)/shard_map/ppermute | solution.py:296
  54.0 3.8 %collective-permute-start.1 = (bf16[96,128]{1,0:T(8,128)(2,1)S(1)}, bf16[96,128]{1,0:T(8,128)(2,1)S(1)}, u32[]{:S(2)}, u32[]{:S(2)}) collective-permute-start(bf16[96,128]{1,0:T(8,128)(2,1)S(1)} %add_convert_fusion.1.a_ref), channel_id=1, source_target_pairs={{0,2},{2,4},{4,6},{6,0},{1,3},{3,5},{5,7},{7,1},{8,10},{10,12},{12... | collective-permute-start | bytes 73736 | tf_op jit(solution)/shard_map/ppermute | solution.py:296
  78.3 7.7 %collective-permute-start.4 = (bf16[32,64,128]{2,1,0:T(8,128)(2,1)S(1)}, bf16[32,64,128]{2,1,0:T(8,128)(2,1)S(1)}, u32[]{:S(2)}, u32[]{:S(2)}) collective-permute-start(bf16[32,64,128]{2,1,0:T(8,128)(2,1)S(1)} %all_to_all.26.own_ref), channel_id=1, source_target_pairs={{0,1},{1,0},{2,3},{3,2},{4,5},{5,4},{6,7},{7,6},{8,9},{9,8},{10,11... | collective-permute-start | bytes 1572872 | tf_op jit(solution)/shard_map/ppermute | solution.py:300
  78.3 7.7 %collective-permute-start.5 = (bf16[32,128]{1,0:T(8,128)(2,1)S(1)}, bf16[32,128]{1,0:T(8,128)(2,1)S(1)}, u32[]{:S(2)}, u32[]{:S(2)}) collective-permute-start(bf16[32,128]{1,0:T(8,128)(2,1)S(1)} %get-tuple-element.18.own_gain_ref), channel_id=1, source_target_pairs={{0,1},{1,0},{2,3},{3,2},{4,5},{5,4},{6,7},{7,6},{8,9},{9,8},{10,11... | collective-permute-start | bytes 24584 | tf_op jit(solution)/shard_map/ppermute | solution.py:298
  86.0 1.6 %copy-start = (bf16[8192,112]{1,0:T(8,128)(2,1)S(1)}, bf16[8192,112]{1,0:T(8,128)(2,1)}, u32[]{:S(2)}) copy-start(bf16[8192,112]{1,0:T(8,128)(2,1)} %copy.13.up_ref) | copy-start | bytes 5505028
  87.6 1.5 %copy-start.3 = (bf16[112,8192]{1,0:T(8,128)(2,1)S(1)}, bf16[112,8192]{1,0:T(8,128)(2,1)}, u32[]{:S(2)}) copy-start(bf16[112,8192]{1,0:T(8,128)(2,1)} %down_ref.1) | copy-start | bytes 5505028
  91.4 2.0 %collective-permute-start.6 = (bf16[32,64,128]{2,1,0:T(8,128)(2,1)S(1)}, bf16[32,64,128]{2,1,0:T(8,128)(2,1)S(1)}, u32[]{:S(2)}, u32[]{:S(2)}) collective-permute-start(bf16[32,64,128]{2,1,0:T(8,128)(2,1)S(1)} %get-tuple-element.20), channel_id=1, source_target_pairs={{0,1},{1,0},{2,3},{3,2},{4,5},{5,4},{6,7},{7,6},{8,9},{9,8},{10,11... | collective-permute-start | bytes 1572872 | tf_op jit(solution)/shard_map/ppermute | solution.py:304

commit v2 on v1

v2 whole, which is shorter than its diff:
```python
import math

import jax
import jax.numpy as jnp
from jax import lax
from jax.experimental import pallas as pl
from jax.experimental.pallas import tpu as pltpu
from jax.sharding import Mesh, PartitionSpec as P

D = 8192
FF = 28672
HD = 128
GROUP = 8
ROWS = 4
DRAFTS = 16
TOKENS = 64
KV = 32
SLICE = 2048
CHUNK = 512
NEG = -1e30
FLOOR = -1e29
EPSILON = 1e-05
LOG_SCALE = math.log2(math.e) / math.sqrt(HD)
MIB = 1024 * 1024
F32 = jnp.float32
BF16 = jnp.bfloat16
VMEM = pl.BlockSpec(memory_space=pltpu.VMEM)
SMEM = pl.BlockSpec(memory_space=pltpu.SMEM)


def nt(a, b):
    return lax.dot_general(a, b, (((1,), (1,)), ((), ())), preferred_element_type=F32)


def nn(a, b):
    return jnp.dot(a, b, preferred_element_type=F32)


def tn(a, b):
    return lax.dot_general(a, b, (((0,), (0,)), ((), ())), preferred_element_type=F32)


def lanes(shape):
    return lax.broadcasted_iota(jnp.int32, shape, len(shape) - 1)


def attend(lengths_ref, gain_ref, q_ref, k_ref, v_ref, out_ref, score_ref):
    row = pl.program_id(0)
    first_key = (lax.axis_index("z") * 4 + lax.axis_index("y")) * SLICE
    length = lengths_ref[row]
    queries = jnp.concatenate(
        [q_ref[0, :, g * HD : (g + 1) * HD] for g in range(GROUP)], axis=0
    )
    draft = lax.broadcasted_iota(jnp.int32, (GROUP * DRAFTS, CHUNK), 0) % DRAFTS
    limit = length - DRAFTS + draft - first_key - lanes((GROUP * DRAFTS, CHUNK))
    peak = jnp.full((GROUP * DRAFTS, HD), NEG, F32)
    for n in range(SLICE // CHUNK):
        scores = nt(queries, k_ref[0, n * CHUNK : (n + 1) * CHUNK, :]) * LOG_SCALE
        scores = jnp.where(limit >= n * CHUNK, scores, NEG)
        score_ref[:, n * CHUNK : (n + 1) * CHUNK] = scores
        for i in range(CHUNK // HD):
            peak = jnp.maximum(peak, scores[:, i * HD : (i + 1) * HD])
    top = jnp.max(peak, axis=1, keepdims=True).astype(BF16).astype(F32)
    base = jnp.maximum(top, FLOOR)
    acc = jnp.zeros((GROUP * DRAFTS, HD), F32)
    sums = jnp.zeros((GROUP * DRAFTS, HD), F32)
    for n in range(SLICE // CHUNK):
        weights = jnp.exp2(score_ref[:, n * CHUNK : (n + 1) * CHUNK] - base)
        for i in range(CHUNK // HD):
            sums = sums + weights[:, i * HD : (i + 1) * HD]
        acc = acc + nn(weights.astype(BF16), v_ref[0, n * CHUNK : (n + 1) * CHUNK, :])
    total = jnp.sum(sums, axis=1, keepdims=True)
    lane = lanes((GROUP * DRAFTS, HD))
    gain = gain_ref[...].astype(F32).reshape(1, 32)
    gain = jnp.broadcast_to(jnp.concatenate([gain] * 4, axis=1), (GROUP * DRAFTS, HD))
    stats = jnp.where(lane < 32, top, jnp.where(lane < 64, total, gain))
    out_ref[:, 0:16, :] = acc.astype(BF16).reshape(GROUP, DRAFTS, HD)
    out_ref[:, 16:32, :] = stats.astype(BF16).reshape(GROUP, DRAFTS, HD)


def attention(lengths, gain, queries, keys, values):
    return pl.pallas_call(
        attend,
        grid=(ROWS,),
        in_specs=[
            SMEM,
            VMEM,
            pl.BlockSpec((1, DRAFTS, GROUP * HD), lambda r: (r, 0, 0)),
            pl.BlockSpec((1, SLICE, HD), lambda r: (r, 0, 0)),
            pl.BlockSpec((1, SLICE, HD), lambda r: (r, 0, 0)),
        ],
        out_specs=pl.BlockSpec((GROUP, 32, HD), lambda r: (r, 0, 0)),
        out_shape=jax.ShapeDtypeStruct((KV, 32, HD), BF16),
        scratch_shapes=[pltpu.VMEM((GROUP * DRAFTS, SLICE), F32)],
        compiler_params=pltpu.CompilerParams(vmem_limit_bytes=56 * MIB),
        name="attention",
    )(lengths, gain, queries, keys, values)


def combine(in_ref, attn_ref, gain_ref):
    top = in_ref[:, 16:32, 0:1].astype(F32)
    total = in_ref[:, 16:32, 32:33].astype(F32)
    joint = jnp.max(top, axis=0, keepdims=True)
    factor = jnp.exp2(top - joint)
    whole = jnp.sum(total * factor, axis=0)
    acc = jnp.sum(in_ref[:, 0:16, :].astype(F32) * factor, axis=0)
    attn = (acc / whole).astype(BF16)
    attn_ref[...] = jnp.broadcast_to(attn[None], (KV, DRAFTS, HD))
    pick = lanes((KV, KV * 16)) == 16 * lax.broadcasted_iota(jnp.int32, (KV, KV * 16), 0)
    stats = in_ref[:, 16:32, :].reshape(KV * 16, HD)
    gain_ref[...] = nn(pick.astype(F32).astype(BF16), stats).astype(BF16)


def combined(parts):
    return pl.pallas_call(
        combine,
        in_specs=[VMEM],
        out_specs=[VMEM, VMEM],
        out_shape=[
            jax.ShapeDtypeStruct((KV, DRAFTS, HD), BF16),
            jax.ShapeDtypeStruct((KV, HD), BF16),
        ],
        compiler_params=pltpu.CompilerParams(vmem_limit_bytes=16 * MIB),
        name="combine",
    )(parts)


def project(attn_ref, weight_ref, residual_ref, gain_ref, own_ref, other_ref):
    core = lax.axis_index("c")
    head = lax.axis_index("x") * 2 + core
    attn = jnp.concatenate(
        [
            jnp.concatenate([attn_ref[r * GROUP + g] for g in range(GROUP)], axis=1)
            for r in range(ROWS)
        ],
        axis=0,
    )
    spread = nn(attn, weight_ref[...])
    source = lax.broadcasted_iota(jnp.int32, (32, 256), 0)
    put = (lanes((32, 256)) == head * 32 + source).astype(F32).astype(BF16)
    spread = spread + tn(residual_ref[...], put)
    source = lax.broadcasted_iota(jnp.int32, (HD, 256), 0)
    put = (lanes((HD, 256)) == head * 32 + source - 64) & (source >= 64) & (source < 96)
    gain = nn(gain_ref[...], put.astype(F32).astype(BF16))
    both = jnp.concatenate([spread, gain], axis=0)
    own_ref[...] = jnp.where(core == 0, both[:, :HD], both[:, HD:])
    other_ref[...] = jnp.where(core == 0, both[:, HD:], both[:, :HD]).astype(BF16)


def projected(attn, weight, residual, gain):
    return pl.pallas_call(
        project,
        in_specs=[VMEM] * 4,
        out_specs=[VMEM, VMEM],
        out_shape=[
            jax.ShapeDtypeStruct((TOKENS + KV, HD), F32),
            jax.ShapeDtypeStruct((TOKENS + KV, HD), BF16),
        ],
        compiler_params=pltpu.CompilerParams(vmem_limit_bytes=16 * MIB),
        name="project",
    )(attn, weight, residual, gain)


def mix(a_ref, b_ref, c_ref, d_ref, spread_ref, mixed_ref, gain_ref):
    total = (a_ref[...].astype(F32) + b_ref[...].astype(F32)) + (
        c_ref[...].astype(F32) + d_ref[...].astype(F32)
    )
    mixed = total[:TOKENS].astype(BF16)
    spread_ref[...] = jnp.broadcast_to(mixed[None], (KV, TOKENS, HD))
    mixed_ref[...] = mixed
    gain_ref[...] = total[TOKENS:]


def mixing(parts):
    return pl.pallas_call(
        mix,
        in_specs=[VMEM] * 4,
        out_specs=[VMEM, VMEM, VMEM],
        out_shape=[
            jax.ShapeDtypeStruct((KV, TOKENS, HD), BF16),
            jax.ShapeDtypeStruct((TOKENS, HD), BF16),
            jax.ShapeDtypeStruct((KV, HD), F32),
        ],
        compiler_params=pltpu.CompilerParams(vmem_limit_bytes=16 * MIB),
        name="mix",
    )(*parts)


def widen(mixed_ref, gain_ref, *refs):
    weight_refs, out_ref = refs[:4], refs[4]
    core = lax.axis_index("c")
    units = weight_refs[0].shape[0]
    squares = jnp.zeros((TOKENS, HD), F32)
    sums = jnp.zeros((TOKENS, 4 * units), F32)
    for k in range(0, KV, 2):
        scaled, weights = [], []
        for i in (k, k + 1):
            part = mixed_ref[i].astype(F32)
            squares = squares + part * part
            scaled.append((part * gain_ref[i : i + 1, :]).astype(BF16))
            at = pl.ds(pl.multiple_of(i * 256 + core * HD, HD), HD)
            weights.append(jnp.concatenate([ref[:, at] for ref in weight_refs], axis=0))
        sums = sums + nt(jnp.concatenate(scaled, axis=1), jnp.concatenate(weights, axis=1))
    square = jnp.broadcast_to(jnp.sum(squares, axis=1, keepdims=True), (TOKENS, HD - units))
    for i in range(4):
        out_ref[i] = jnp.concatenate([sums[:, i * units : (i + 1) * units], square], axis=1)


def widened(mixed, gain, weights):
    return pl.pallas_call(
        widen,
        in_specs=[VMEM] * 6,
        out_specs=VMEM,
        out_shape=jax.ShapeDtypeStruct((4, TOKENS, HD), F32),
        compiler_params=pltpu.CompilerParams(vmem_limit_bytes=16 * MIB),
        name="widen",
    )(mixed, gain, *weights)


def narrow(mine_ref, theirs_ref, own_ref, other_ref, out_ref):
    core = lax.axis_index("c")
    units = own_ref.shape[0]
    square = mine_ref[0, :, units : units + 1] + theirs_ref[0, :, units : units + 1]
    scale = lax.rsqrt(square / D + EPSILON)
    hidden = []
    for i in (0, 2):
        gate = (mine_ref[i] + theirs_ref[2 - i]) * scale
        upward = (mine_ref[i + 1] + theirs_ref[3 - i]) * scale
        hidden.append((gate / (1.0 + jnp.exp(-gate)) * upward)[:, :units])
    hidden = jnp.concatenate(hidden, axis=1).astype(BF16)
    lane = lanes((TOKENS, HD))
    for y in range(4):
        for z_high in range(2):
            tiles = [None] * 4
            for z_low in range(4):
                k = (z_high * 4 + z_low) * 4 + y
                weight = jnp.concatenate(
                    [ref[:, k * 256 : (k + 1) * 256] for ref in (own_ref, other_ref)], axis=0
                )
                terms = nn(hidden, weight)
                for x in range(4):
                    part = terms[:, x // 2 * HD : (x // 2 + 1) * HD]
                    move = (z_low - x % 2 * 2 - core + 8) % 4 * 32
                    part = pltpu.roll(part, move, 1)
                    tiles[x] = (
                        part if z_low == 0 else jnp.where(lane >= z_low * 32, part, tiles[x])
                    )
            for x in range(4):
                out_ref[y * 4 + x, z_high * TOKENS : (z_high + 1) * TOKENS, :] = tiles[x].astype(
                    BF16
                )


def narrowed(mine, theirs, own, other):
    return pl.pallas_call(
        narrow,
        in_specs=[VMEM] * 4,
        out_specs=VMEM,
        out_shape=jax.ShapeDtypeStruct((16, 2 * TOKENS, HD), BF16),
        compiler_params=pltpu.CompilerParams(vmem_limit_bytes=16 * MIB),
        name="narrow",
    )(mine, theirs, own, other)


def partial_sum(in_ref, out_ref):
    total = in_ref[0].astype(F32)
    for k in range(1, 16):
        total = total + in_ref[k].astype(F32)
    lane = lanes((16, HD))
    for z in range(8):
        packed = None
        for a in range(4):
            start = z // 4 * TOKENS + a * 16
            part = pltpu.roll(total[start : start + 16], (a - z % 4) % 4 * 32, 1)
            packed = part if a == 0 else jnp.where(lane >= a * 32, part, packed)
        out_ref[z] = packed.astype(BF16)


def summed(parts):
    return pl.pallas_call(
        partial_sum,
        in_specs=[VMEM],
        out_specs=VMEM,
        out_shape=jax.ShapeDtypeStruct((8, 16, HD), BF16),
        compiler_params=pltpu.CompilerParams(vmem_limit_bytes=16 * MIB),
        name="partial_sum",
    )(parts)


def finish(parts_ref, own_ref, other_ref, out_ref):
    x, core = lax.axis_index("x"), lax.axis_index("c")
    total = parts_ref[0].astype(F32)
    for z in range(1, 8):
        total = total + parts_ref[z].astype(F32)
    tall = jnp.concatenate([pltpu.roll(total, (4 - a) % 4 * 32, 1) for a in range(4)], axis=0)
    mixed = jnp.where(x // 2 == core, own_ref[...].astype(F32), other_ref[...].astype(F32))
    mixed = pltpu.roll(mixed, (8 - x * 2 - core) % 4 * 32, 1)
    out_ref[...] = jnp.transpose(mixed + tall)[:32].astype(BF16)


def finished(parts, own, other):
    return pl.pallas_call(
        finish,
        in_specs=[VMEM] * 3,
        out_specs=VMEM,
        out_shape=jax.ShapeDtypeStruct((32, TOKENS), BF16),
        compiler_params=pltpu.CompilerParams(vmem_limit_bytes=16 * MIB),
        name="finish",
    )(parts, own, other)


SWAP = [(0, 1), (1, 0)]


def trade(part):
    return lax.ppermute(part, "c", SWAP)


def exchange(parts, axes):
    return lax.all_to_all(parts, axes, 0, 0, tiled=True)


def shards(
    lengths,
    queries,
    cache_keys,
    cache_values,
    residual_in,
    out_weight,
    norm_gain,
    gate_weight,
    up_weight,
    down_weight,
):
    weights = [gate_weight.T, up_weight.T]
    weights = weights + [trade(weight) for weight in weights]
    other_down = trade(down_weight)
    parts = attention(lengths, norm_gain, queries, cache_keys, cache_values)
    attn, gain = combined(exchange(parts, ("z", "y")))
    attn = exchange(attn, ("z", "y"))
    own, other = projected(attn, out_weight, residual_in.T, gain)
    pair = (own + trade(other).astype(F32)).astype(BF16)
    around = [lax.ppermute(pair, "x", [(i, (i + s) % 4) for i in range(4)]) for s in (1, 2, 3)]
    spread, mixed, gain = mixing([pair] + around)
    other_mixed = trade(mixed)
    sums = widened(exchange(spread, ("z", "y")), gain, weights)
    terms = narrowed(sums, trade(sums), down_weight, other_down)
    terms = summed(exchange(terms, ("y", "x")))
    return finished(exchange(terms, "z"), mixed, other_mixed).T


def solution(mesh):
    fine = Mesh(mesh.devices.reshape(8, 4, 4, 2), ("z", "y", "x", "c"))
    kvseq, head = ("z", "y"), ("x", "c")
    every = kvseq + head
    placed = (
        P(),
        P(None, None, head),
        P(None, kvseq, head),
        P(None, kvseq, head),
        P(None, every),
        P(head, kvseq),
        P(every),
        P(None, every),
        P(None, every),
        P(every, None),
    )
    return jax.shard_map(
        shards, mesh=fine, in_specs=placed, out_specs=P(None, every), check_vma=False
    )
```

time: 129 us -> 113 us (0.88); the launches traced: 127 us -> 113 us
  blocking collectives: 76.2 us -> 51.6 us
  local copies, waits for them, and re-layouts: 16.5 us -> 1.51 us
  starting transfers between devices: 9.62 us -> 20.2 us
  waiting for transfers between devices: 15.6 us -> 25.6 us
  Pallas kernels: 8.67 us -> 13.8 us
    all_to_all x4 -> x3, blocking collectives: 76.2 us -> 51.6 us  [exchange(): return lax.all_to_all(parts, axes, 0, 0, tiled=True)]
    unnamed x19 -> x10, local copies, waits for them, and re-layouts: 15.1 us -> 1.51 us
    all_to_all x1 -> x2, starting transfers between devices: 4.09 us -> 14.8 us  [exchange(): return lax.all_to_all(parts, axes, 0, 0, tiled=True)]
    all_to_all x1 -> x2, waiting for transfers between devices: 10.5 us -> 18.7 us  [exchange(): return lax.all_to_all(parts, axes, 0, 0, tiled=True)]
    pallas_call x6 -> x7, Pallas kernels: 7.74 us -> 13.6 us  [the longest x1 5.69 us: attention(): pl.pallas_call(attend, grid=(ROWS,), in_specs=[SMEM, VMEM, pl.BlockSpec((...]
    ppermute x4 -> x6, waiting for transfers between devices: 3.08 us -> 3.68 us  [trade(): return lax.ppermute(part, 'c', SWAP)]
  transfers between devices with their start and end apart: 8 -> 11, of which waited for: 5 -> 8; matrix products, arithmetic and copies ran while one was open for 6% -> 0% of each run, Pallas kernels for 0% -> 3%
where the time goes in v2:
time: 113 us
  blocking collectives  51.6 us (46%)
  waiting for transfers between devices  25.6 us (23%)
  starting transfers between devices  20.2 us (18%)
  Pallas kernels  13.8 us (12%)
  local copies, waits for them, and re-layouts  1.51 us (1%)
    all_to_all x3, blocking collectives, exchange(): return lax.all_to_all(parts, axes, 0, 0, tiled=True)  51.6 us
    all_to_all x2, waiting for transfers between devices, exchange(): return lax.all_to_all(parts, axes, 0, 0, tiled=True)  18.7 us
    all_to_all x2, starting transfers between devices, exchange(): return lax.all_to_all(parts, axes, 0, 0, tiled=True)  14.8 us
    pallas_call x1, Pallas kernels, attention(): pl.pallas_call(attend, grid=(ROWS,), in_specs=[SMEM, VMEM, pl.BlockSpec((...  5.69 us
    ppermute x3, starting transfers between devices, shards(): lax.ppermute(pair, 'x', [(i, (i + s) % 4) for i in range(4)])  4.43 us
    ppermute x6, waiting for transfers between devices, trade(): return lax.ppermute(part, 'c', SWAP)  3.68 us
    pallas_call x1, Pallas kernels, widened(): pl.pallas_call(widen, in_specs=[VMEM] * 6, out_specs=VMEM, out_shape=jax....  3.36 us
    ppermute x3, waiting for transfers between devices, shards(): lax.ppermute(pair, 'x', [(i, (i + s) % 4) for i in range(4)])  3.3 us
  transfers between devices with their start and end apart: 11, of which 8 were waited for; matrix products, arithmetic and copies ran while one was open for 0% of the time, Pallas kernels for 3%

profile of v2, /device:TPU:2, one launch (start us, length us, event | category | flops | bytes accessed | tf_op | source)
XLA Modules:
  0.0 112.9 jit_solution(5561837558303165544)
XLA Ops:
  0.0 0.0 copy-start
  0.0 0.0 copy-start.4
  0.0 0.0 copy-start.3
  0.0 5.7 %attention.1 = bf16[32,32,128]{2,1,0:T(8,128)(2,1)} custom-call(s32[4]{0:T(128)} %lengths_ref.1, bf16[32]{0:T(256)(128)(2,1)} %gain_ref.1, bf16[4,16,1024]{2,1,0:T(8,128)(2,1)} %q_ref.1, bf16[4,2048,128]{2,1,0:T(8,128)(2,1)} %k_ref.1, bf16[4,2048,128]{2,1,0:T(8,128)(2,1)} %v_ref.1), custom_call_target="tpu_custom_call" | custom-call | tf_op jit(solution)/shard_map/attention/pallas_call | solution.py:82
  5.7 11.5 %all-to-all-start = ((bf16[32,32,128]{2,1,0:T(8,128)(2,1)}), bf16[32,32,128]{2,1,0:T(8,128)(2,1)S(1)}, u32[]{:S(2)}, u32[]{:S(2)}) async-start(bf16[32,32,128]{2,1,0:T(8,128)(2,1)} %attention.1), calls=%async_computation | async-start | bytes 524288 | tf_op jit(solution)/shard_map/all_to_all | solution.py:320
  17.2 0.1 collective-permute-start.4
  17.3 0.5 collective-permute-start.5
  17.8 0.0 copy-done
  17.8 0.1 collective-permute-start.7
  17.9 12.0 %all-to-all-done.in_ref = bf16[32,32,128]{2,1,0:T(8,128)(2,1)S(1)} async-done(((bf16[32,32,128]{2,1,0:T(8,128)(2,1)}), bf16[32,32,128]{2,1,0:T(8,128)(2,1)S(1)}, u32[]{:S(2)}, u32[]{:S(2)}) %all-to-all-start) | async-done | bytes 262176 | tf_op jit(solution)/shard_map/all_to_all | solution.py:320
  29.9 0.0 copy-start.1
  29.9 0.3 combine.1
  30.2 14.7 %all_to_all.25.attn_ref = bf16[32,16,128]{2,1,0:T(8,128)(2,1)S(1)} all-to-all(bf16[32,16,128]{2,1,0:T(8,128)(2,1)S(1)} %get-tuple-element.12), channel_id=1, replica_groups=mesh['z'=8,'y'=4,'x'=4,'c'=2] {'z','y'}, dimensions={0} | all-to-all | bytes 262144 | tf_op jit(solution)/shard_map/all_to_all | solution.py:320
  44.8 0.0 copy-done.4
  44.8 0.0 copy-done.3
  44.8 0.3 project.1
  45.1 0.1 collective-permute-start
  45.2 1.2 %collective-permute-done = bf16[96,128]{1,0:T(8,128)(2,1)S(1)} collective-permute-done((bf16[96,128]{1,0:T(8,128)(2,1)S(1)}, bf16[96,128]{1,0:T(8,128)(2,1)S(1)}, u32[]{:S(2)}, u32[]{:S(2)}) %collective-permute-start) | collective-permute-done | bytes 24608 | tf_op jit(solution)/shard_map/ppermute | solution.py:316
  46.4 1.6 %collective-permute-start.1 = (bf16[96,128]{1,0:T(8,128)(2,1)S(1)}, bf16[96,128]{1,0:T(8,128)(2,1)S(1)}, u32[]{:S(2)}, u32[]{:S(2)}) collective-permute-start(bf16[96,128]{1,0:T(8,128)(2,1)S(1)} %add_convert_fusion.a_ref), channel_id=1, source_target_pairs={{0,2},{2,4},{4,6},{6,0},{1,3},{3,5},{5,7},{7,1},{8,10},{10,12},{12... | collective-permute-start | bytes 73736 | tf_op jit(solution)/shard_map/ppermute | solution.py:343
  47.9 1.1 collective-permute-start.2
  49.1 1.2 %collective-permute-done.1.b_ref = bf16[96,128]{1,0:T(8,128)(2,1)S(1)} collective-permute-done((bf16[96,128]{1,0:T(8,128)(2,1)S(1)}, bf16[96,128]{1,0:T(8,128)(2,1)S(1)}, u32[]{:S(2)}, u32[]{:S(2)}) %collective-permute-start.1) | collective-permute-done | bytes 24608 | tf_op jit(solution)/shard_map/ppermute | solution.py:343
  50.3 1.7 %collective-permute-start.3 = (bf16[96,128]{1,0:T(8,128)(2,1)S(1)}, bf16[96,128]{1,0:T(8,128)(2,1)S(1)}, u32[]{:S(2)}, u32[]{:S(2)}) collective-permute-start(bf16[96,128]{1,0:T(8,128)(2,1)S(1)} %add_convert_fusion.a_ref), channel_id=1, source_target_pairs={{0,6},{2,0},{4,2},{6,4},{1,7},{3,1},{5,3},{7,5},{8,14},{10,8},{12,... | collective-permute-start | bytes 73736 | tf_op jit(solution)/shard_map/ppermute | solution.py:343
  52.0 1.3 %collective-permute-done.2.c_ref = bf16[96,128]{1,0:T(8,128)(2,1)S(1)} collective-permute-done((bf16[96,128]{1,0:T(8,128)(2,1)S(1)}, bf16[96,128]{1,0:T(8,128)(2,1)S(1)}, u32[]{:S(2)}, u32[]{:S(2)}) %collective-permute-start.2) | collective-permute-done | bytes 24608 | tf_op jit(solution)/shard_map/ppermute | solution.py:343
  53.3 0.8 collective-permute-done.3.d_ref
  54.1 0.1 mix.1
  54.2 19.5 %all_to_all.26.mixed_ref = bf16[32,64,128]{2,1,0:T(8,128)(2,1)S(1)} all-to-all(bf16[32,64,128]{2,1,0:T(8,128)(2,1)S(1)} %get-tuple-element.16), channel_id=1, replica_groups=mesh['z'=8,'y'=4,'x'=4,'c'=2] {'z','y'}, dimensions={0} | all-to-all | bytes 1048576 | tf_op jit(solution)/shard_map/all_to_all | solution.py:320
  73.7 0.0 collective-permute-done.4.refs_2_
  73.7 0.0 collective-permute-done.5.refs_3_
  73.7 0.0 copy-done.1
  73.7 0.0 copy-start.2
  73.7 1.5 %copy-done.2 = bf16[8192,112]{0,1:T(8,128)(2,1)S(1)} copy-done((bf16[8192,112]{0,1:T(8,128)(2,1)S(1)}, bf16[8192,112]{0,1:T(8,128)(2,1)}, u32[]{:S(2)}) %copy-start.2) | copy-done | bytes 1835032
  75.2 3.4 %widen.1.mine_ref = f32[4,64,128]{2,1,0:T(8,128)S(1)} custom-call(bf16[32,64,128]{2,1,0:T(8,128)(2,1)S(1)} %all_to_all.26.mixed_ref, f32[32,128]{1,0:T(8,128)S(1)} %get-tuple-element.17.gain_ref, bf16[112,8192]{1,0:T(8,128)(2,1)S(1)} %bitcast.5, bf16[112,8192]{1,0:T(8,128)(2,1)S(1)} %bitcast.7, bf16[112,8192]{1,0:T(8,128)(2,1)} %collective-permute-done.4.refs_2_, ...), custom_call_target="tpu_custom_call" | custom-call | tf_op jit(solution)/shard_map/widen/pallas_call | solution.py:210
  78.6 0.1 collective-permute-start.6
  78.7 0.0 collective-permute-done.7.other_ref
  78.7 1.3 %collective-permute-done.6.theirs_ref = f32[4,64,128]{2,1,0:T(8,128)S(1)} collective-permute-done((f32[4,64,128]{2,1,0:T(8,128)S(1)}, f32[4,64,128]{2,1,0:T(8,128)S(1)}, u32[]{:S(2)}, u32[]{:S(2)}) %collective-permute-start.6) | collective-permute-done | bytes 131104 | tf_op jit(solution)/shard_map/ppermute | solution.py:316
  80.0 2.7 %narrow.1 = bf16[16,128,128]{2,1,0:T(8,128)(2,1)S(1)} custom-call(f32[4,64,128]{2,1,0:T(8,128)S(1)} %widen.1.mine_ref, f32[4,64,128]{2,1,0:T(8,128)S(1)} %collective-permute-done.6.theirs_ref, bf16[112,8192]{1,0:T(8,128)(2,1)S(1)} %copy-done, bf16[112,8192]{1,0:T(8,128)(2,1)} %collective-permute-done.7.other_ref), custom_call_target="tpu_custom_call" | custom-call | tf_op jit(solution)/shard_map/narrow/pallas_call | solution.py:255
  82.7 17.4 %all_to_all.27.in_ref = bf16[16,128,128]{2,1,0:T(8,128)(2,1)S(1)} all-to-all(bf16[16,128,128]{2,1,0:T(8,128)(2,1)S(1)} %narrow.1), channel_id=1, replica_groups=mesh['z'=8,'y'=4,'x'=4,'c'=2] {'y','x'}, dimensions={0} | all-to-all | bytes 1048576 | tf_op jit(solution)/shard_map/all_to_all | solution.py:320
  100.1 0.8 partial_sum.1
  100.8 3.3 %all-to-all-start.4 = ((bf16[8,16,128]{2,1,0:T(8,128)(2,1)}), bf16[8,16,128]{2,1,0:T(8,128)(2,1)S(1)}, u32[]{:S(2)}, u32[]{:S(2)}) async-start(bf16[8,16,128]{2,1,0:T(8,128)(2,1)} %partial_sum.1), calls=%async_computation.4 | async-start | bytes 65536 | tf_op jit(solution)/shard_map/all_to_all | solution.py:320
  104.2 0.1 collective-permute-start.8
  104.3 1.2 %collective-permute-done.8.other_ref = bf16[64,128]{1,0:T(8,128)(2,1)S(1)} collective-permute-done((bf16[64,128]{1,0:T(8,128)(2,1)S(1)}, bf16[64,128]{1,0:T(8,128)(2,1)S(1)}, u32[]{:S(2)}, u32[]{:S(2)}) %collective-permute-start.8) | collective-permute-done | bytes 16416 | tf_op jit(solution)/shard_map/ppermute | solution.py:316
  105.5 6.7 %all-to-all-done.4.parts_ref = bf16[8,16,128]{2,1,0:T(8,128)(2,1)S(1)} async-done(((bf16[8,16,128]{2,1,0:T(8,128)(2,1)}), bf16[8,16,128]{2,1,0:T(8,128)(2,1)S(1)}, u32[]{:S(2)}, u32[]{:S(2)}) %all-to-all-start.4) | async-done | bytes 32800 | tf_op jit(solution)/shard_map/all_to_all | solution.py:320
  112.1 0.8 finish.1
  (1 shorter events, 0.0 us)
Async XLA Ops:
  0.0 17.8 %copy-start = (bf16[112,8192]{1,0:T(8,128)(2,1)S(1)}, bf16[112,8192]{1,0:T(8,128)(2,1)}, u32[]{:S(2)}) copy-start(bf16[112,8192]{1,0:T(8,128)(2,1)} %own_ref.1) | copy-start | bytes 5505028
  0.0 44.8 %copy-start.4 = (bf16[64,32]{0,1:T(8,128)(2,1)S(1)}, bf16[64,32]{0,1:T(8,128)(2,1)}, u32[]{:S(2)}) copy-start(bf16[64,32]{0,1:T(8,128)(2,1)} %param.14) | copy-start | bytes 12292
  0.0 44.8 %copy-start.3 = (bf16[1024,256]{1,0:T(8,128)(2,1)S(1)}, bf16[1024,256]{1,0:T(8,128)(2,1)}, u32[]{:S(2)}) copy-start(bf16[1024,256]{1,0:T(8,128)(2,1)} %weight_ref.1) | copy-start | bytes 1572868
  5.7 24.2 %all-to-all-start = ((bf16[32,32,128]{2,1,0:T(8,128)(2,1)}), bf16[32,32,128]{2,1,0:T(8,128)(2,1)S(1)}, u32[]{:S(2)}, u32[]{:S(2)}) async-start(bf16[32,32,128]{2,1,0:T(8,128)(2,1)} %attention.1), calls=%async_computation | async-start | bytes 524288 | tf_op jit(solution)/shard_map/all_to_all | solution.py:320
  17.2 56.5 %collective-permute-start.4 = (bf16[112,8192]{1,0:T(8,128)(2,1)}, bf16[112,8192]{1,0:T(8,128)(2,1)}, u32[]{:S(2)}, u32[]{:S(2)}) collective-permute-start(bf16[112,8192]{1,0:T(8,128)(2,1)} %bitcast.4), channel_id=1, source_target_pairs={{0,1},{1,0},{2,3},{3,2},{4,5},{5,4},{6,7},{7,6},{8,9},{9,8},{10,11... | collective-permute-start | bytes 5505032 | tf_op jit(solution)/shard_map/ppermute | solution.py:316
  17.3 56.4 %collective-permute-start.5 = (bf16[112,8192]{1,0:T(8,128)(2,1)}, bf16[112,8192]{1,0:T(8,128)(2,1)}, u32[]{:S(2)}, u32[]{:S(2)}) collective-permute-start(bf16[112,8192]{1,0:T(8,128)(2,1)} %bitcast.6), channel_id=1, source_target_pairs={{0,1},{1,0},{2,3},{3,2},{4,5},{5,4},{6,7},{7,6},{8,9},{9,8},{10,11... | collective-permute-start | bytes 5505032 | tf_op jit(solution)/shard_map/ppermute | solution.py:316
  17.8 60.9 %collective-permute-start.7 = (bf16[112,8192]{1,0:T(8,128)(2,1)S(1)}, bf16[112,8192]{1,0:T(8,128)(2,1)}, u32[]{:S(2)}, u32[]{:S(2)}) collective-permute-start(bf16[112,8192]{1,0:T(8,128)(2,1)S(1)} %copy-done), channel_id=1, source_target_pairs={{0,1},{1,0},{2,3},{3,2},{4,5},{5,4},{6,7},{7,6},{8,9},{9,8},{10,11... | collective-permute-start | bytes 5505032 | tf_op jit(solution)/shard_map/ppermute | solution.py:316
  29.9 43.8 %copy-start.1 = (bf16[8192,112]{0,1:T(8,128)(2,1)S(1)}, bf16[8192,112]{0,1:T(8,128)(2,1)}, u32[]{:S(2)}) copy-start(bf16[8192,112]{0,1:T(8,128)(2,1)} %param.17) | copy-start | bytes 5505028
  45.1 1.3 %collective-permute-start = (bf16[96,128]{1,0:T(8,128)(2,1)S(1)}, bf16[96,128]{1,0:T(8,128)(2,1)S(1)}, u32[]{:S(2)}, u32[]{:S(2)}) collective-permute-start(bf16[96,128]{1,0:T(8,128)(2,1)S(1)} %get-tuple-element.15), channel_id=1, source_target_pairs={{0,1},{1,0},{2,3},{3,2},{4,5},{5,4},{6,7},{7,6},{8,9},{9,8},{10,11... | collective-permute-start | bytes 73736 | tf_op jit(solution)/shard_map/ppermute | solution.py:316
  46.4 3.9 %collective-permute-start.1 = (bf16[96,128]{1,0:T(8,128)(2,1)S(1)}, bf16[96,128]{1,0:T(8,128)(2,1)S(1)}, u32[]{:S(2)}, u32[]{:S(2)}) collective-permute-start(bf16[96,128]{1,0:T(8,128)(2,1)S(1)} %add_convert_fusion.a_ref), channel_id=1, source_target_pairs={{0,2},{2,4},{4,6},{6,0},{1,3},{3,5},{5,7},{7,1},{8,10},{10,12},{12... | collective-permute-start | bytes 73736 | tf_op jit(solution)/shard_map/ppermute | solution.py:343
  47.9 5.4 %collective-permute-start.2 = (bf16[96,128]{1,0:T(8,128)(2,1)S(1)}, bf16[96,128]{1,0:T(8,128)(2,1)S(1)}, u32[]{:S(2)}, u32[]{:S(2)}) collective-permute-start(bf16[96,128]{1,0:T(8,128)(2,1)S(1)} %add_convert_fusion.a_ref), channel_id=1, source_target_pairs={{0,4},{2,6},{4,0},{6,2},{1,5},{3,7},{5,1},{7,3},{8,12},{10,14},{12... | collective-permute-start | bytes 73736 | tf_op jit(solution)/shard_map/ppermute | solution.py:343
  50.3 3.8 %collective-permute-start.3 = (bf16[96,128]{1,0:T(8,128)(2,1)S(1)}, bf16[96,128]{1,0:T(8,128)(2,1)S(1)}, u32[]{:S(2)}, u32[]{:S(2)}) collective-permute-start(bf16[96,128]{1,0:T(8,128)(2,1)S(1)} %add_convert_fusion.a_ref), channel_id=1, source_target_pairs={{0,6},{2,0},{4,2},{6,4},{1,7},{3,1},{5,3},{7,5},{8,14},{10,8},{12,... | collective-permute-start | bytes 73736 | tf_op jit(solution)/shard_map/ppermute | solution.py:343
  73.7 1.5 %copy-start.2 = (bf16[8192,112]{0,1:T(8,128)(2,1)S(1)}, bf16[8192,112]{0,1:T(8,128)(2,1)}, u32[]{:S(2)}) copy-start(bf16[8192,112]{0,1:T(8,128)(2,1)} %param.18) | copy-start | bytes 5505028
  78.6 1.4 %collective-permute-start.6 = (f32[4,64,128]{2,1,0:T(8,128)S(1)}, f32[4,64,128]{2,1,0:T(8,128)S(1)}, u32[]{:S(2)}, u32[]{:S(2)}) collective-permute-start(f32[4,64,128]{2,1,0:T(8,128)S(1)} %widen.1.mine_ref), channel_id=1, source_target_pairs={{0,1},{1,0},{2,3},{3,2},{4,5},{5,4},{6,7},{7,6},{8,9},{9,8},{10,11... | collective-permute-start | bytes 393224 | tf_op jit(solution)/shard_map/ppermute | solution.py:316
  100.8 11.3 %all-to-all-start.4 = ((bf16[8,16,128]{2,1,0:T(8,128)(2,1)}), bf16[8,16,128]{2,1,0:T(8,128)(2,1)S(1)}, u32[]{:S(2)}, u32[]{:S(2)}) async-start(bf16[8,16,128]{2,1,0:T(8,128)(2,1)} %partial_sum.1), calls=%async_computation.4 | async-start | bytes 65536 | tf_op jit(solution)/shard_map/all_to_all | solution.py:320
  104.2 1.3 %collective-permute-start.8 = (bf16[64,128]{1,0:T(8,128)(2,1)S(1)}, bf16[64,128]{1,0:T(8,128)(2,1)S(1)}, u32[]{:S(2)}, u32[]{:S(2)}) collective-permute-start(bf16[64,128]{1,0:T(8,128)(2,1)S(1)} %get-tuple-element.18.own_ref), channel_id=1, source_target_pairs={{0,1},{1,0},{2,3},{3,2},{4,5},{5,4},{6,7},{7,6},{8,9},{9,8},{10,11... | collective-permute-start | bytes 49160 | tf_op jit(solution)/shard_map/ppermute | solution.py:316

commit v3 on v2

v3 whole, which is shorter than its diff:
```python
import math

import jax
import jax.numpy as jnp
from jax import lax
from jax.experimental import pallas as pl
from jax.experimental.pallas import tpu as pltpu
from jax.sharding import Mesh, PartitionSpec as P

D = 8192
FF = 28672
HD = 128
GROUP = 8
ROWS = 4
DRAFTS = 16
TOKENS = 64
KV = 32
SLICE = 2048
CHUNK = 512
NEG = -1e30
FLOOR = -1e29
EPSILON = 1e-05
LOG_SCALE = math.log2(math.e) / math.sqrt(HD)
MIB = 1024 * 1024
F32 = jnp.float32
BF16 = jnp.bfloat16
VMEM = pl.BlockSpec(memory_space=pltpu.VMEM)
SMEM = pl.BlockSpec(memory_space=pltpu.SMEM)


def nt(a, b):
    return lax.dot_general(a, b, (((1,), (1,)), ((), ())), preferred_element_type=F32)


def nn(a, b):
    return jnp.dot(a, b, preferred_element_type=F32)


def tn(a, b):
    return lax.dot_general(a, b, (((0,), (0,)), ((), ())), preferred_element_type=F32)


def lanes(shape):
    return lax.broadcasted_iota(jnp.int32, shape, len(shape) - 1)


def attend(
    lengths_ref, gain_ref, q_ref, keys_ref, values_ref, out_ref, k_ref, v_ref, score_ref, sems
):
    copies = []
    for row in range(ROWS):
        copies.append(
            [
                pltpu.make_async_copy(keys_ref.at[row], k_ref.at[row], sems.at[row, 0]),
                pltpu.make_async_copy(values_ref.at[row], v_ref.at[row], sems.at[row, 1]),
            ]
        )
        for copy in copies[row]:
            copy.start()
    first_key = (lax.axis_index("z") * 4 + lax.axis_index("y")) * SLICE
    draft = lax.broadcasted_iota(jnp.int32, (GROUP * DRAFTS, CHUNK), 0) % DRAFTS
    offset = draft - DRAFTS - lanes((GROUP * DRAFTS, CHUNK)) - first_key
    gain = gain_ref[...].astype(F32).reshape(1, 32)
    gain = jnp.concatenate([gain] * 4, axis=1).reshape(1, 1, HD)
    lane = lanes((GROUP, 8, HD))
    for row in range(ROWS):
        queries = jnp.concatenate(
            [q_ref[row, :, g * HD : (g + 1) * HD] for g in range(GROUP)], axis=0
        )
        limit = offset + lengths_ref[row]
        peak = jnp.full((GROUP * DRAFTS, HD), NEG, F32)
        copies[row][0].wait()
        for n in range(SLICE // CHUNK):
            scores = nt(queries, k_ref[row, n * CHUNK : (n + 1) * CHUNK, :]) * LOG_SCALE
            scores = jnp.where(limit >= n * CHUNK, scores, NEG)
            score_ref[row % 2, :, n * CHUNK : (n + 1) * CHUNK] = scores
            for i in range(CHUNK // HD):
                peak = jnp.maximum(peak, scores[:, i * HD : (i + 1) * HD])
        top = jnp.max(peak, axis=1, keepdims=True).astype(BF16).astype(F32)
        base = jnp.maximum(top, FLOOR)
        acc = jnp.zeros((GROUP * DRAFTS, HD), F32)
        sums = jnp.zeros((GROUP * DRAFTS, HD), F32)
        copies[row][1].wait()
        for n in range(SLICE // CHUNK):
            weights = jnp.exp2(score_ref[row % 2, :, n * CHUNK : (n + 1) * CHUNK] - base)
            for i in range(CHUNK // HD):
                sums = sums + weights[:, i * HD : (i + 1) * HD]
            acc = acc + nn(weights.astype(BF16), v_ref[row, n * CHUNK : (n + 1) * CHUNK, :])
        total = jnp.sum(sums, axis=1, keepdims=True).reshape(GROUP, DRAFTS, 1)
        top = top.reshape(GROUP, DRAFTS, 1)
        stats = jnp.where(lane < 64, total[:, 8:], gain)
        stats = jnp.where(lane < 48, total[:, :8], stats)
        stats = jnp.where(lane < 32, top[:, 8:], stats)
        stats = jnp.where(lane < 16, top[:, :8], stats)
        acc = acc.reshape(GROUP, DRAFTS, HD)
        block = jnp.concatenate([acc, stats], axis=1).astype(BF16)
        out_ref[row * GROUP : (row + 1) * GROUP] = block


def attention(lengths, gain, queries, keys, values):
    held = pl.BlockSpec(memory_space=pltpu.HBM)
    return pl.pallas_call(
        attend,
        in_specs=[SMEM, VMEM, VMEM, held, held],
        out_specs=VMEM,
        out_shape=jax.ShapeDtypeStruct((KV, 24, HD), BF16),
        scratch_shapes=[
            pltpu.VMEM((ROWS, SLICE, HD), BF16),
            pltpu.VMEM((ROWS, SLICE, HD), BF16),
            pltpu.VMEM((2, GROUP * DRAFTS, SLICE), F32),
            pltpu.SemaphoreType.DMA((ROWS, 2)),
        ],
        compiler_params=pltpu.CompilerParams(vmem_limit_bytes=57 * MIB),
        cost_estimate=pl.CostEstimate(
            flops=0, bytes_accessed=12800000, transcendentals=0
        ),
        name="attention",
    )(lengths, gain, queries, keys, values)


def combine(in_ref, attn_ref, gain_ref):
    parts = in_ref[...].astype(F32)
    stats = parts[:, 16:24]
    top = jnp.concatenate([stats[:, :, 0:1], stats[:, :, 16:17]], axis=1)
    total = jnp.concatenate([stats[:, :, 32:33], stats[:, :, 48:49]], axis=1)
    joint = jnp.max(top, axis=0, keepdims=True)
    factor = jnp.exp2(top - joint)
    whole = jnp.sum(total * factor, axis=0)
    acc = jnp.sum(parts[:, 0:16] * factor, axis=0)
    attn = (acc / whole).astype(BF16)
    attn_ref[...] = jnp.broadcast_to(attn[None], (KV, DRAFTS, HD))
    pick = lanes((KV, KV * 8)) == 8 * lax.broadcasted_iota(jnp.int32, (KV, KV * 8), 0)
    stats = stats.reshape(KV * 8, HD).astype(BF16)
    gain_ref[...] = nn(pick.astype(F32).astype(BF16), stats).astype(BF16)


def combined(parts):
    return pl.pallas_call(
        combine,
        in_specs=[VMEM],
        out_specs=[VMEM, VMEM],
        out_shape=[
            jax.ShapeDtypeStruct((KV, DRAFTS, HD), BF16),
            jax.ShapeDtypeStruct((KV, HD), BF16),
        ],
        compiler_params=pltpu.CompilerParams(vmem_limit_bytes=16 * MIB),
        cost_estimate=pl.CostEstimate(
            flops=0, bytes_accessed=38400000, transcendentals=0
        ),
        name="combine",
    )(parts)


def project(attn_ref, weight_ref, residual_ref, gain_ref, out_ref):
    head = lax.axis_index("x") * 2 + lax.axis_index("c")
    attn = jnp.concatenate(
        [
            jnp.concatenate([attn_ref[r * GROUP + g] for g in range(GROUP)], axis=1)
            for r in range(ROWS)
        ],
        axis=0,
    )
    spread = nn(attn, weight_ref[...])
    source = lax.broadcasted_iota(jnp.int32, (32, 256), 0)
    put = (lanes((32, 256)) == head * 32 + source).astype(F32).astype(BF16)
    spread = spread + tn(residual_ref[...], put)
    source = lax.broadcasted_iota(jnp.int32, (HD, 256), 0)
    put = (lanes((HD, 256)) == head * 32 + source - 64) & (source >= 64) & (source < 96)
    gain = nn(gain_ref[...], put.astype(F32).astype(BF16))
    both = jnp.concatenate([spread, gain], axis=0).astype(BF16)
    for i in range(8):
        out_ref[i, : TOKENS + KV] = both[:, i % 2 * HD : (i % 2 + 1) * HD]
    spot = lanes((DRAFTS, HD)) // 32
    for half in range(2):
        part = spread[:, half * HD : (half + 1) * HD]
        rows = [part[a * DRAFTS : (a + 1) * DRAFTS] for a in range(4)]
        rows = [pltpu.roll(row, a * 32, 1) if a else row for a, row in enumerate(rows)]
        for i in range(4):
            tile = rows[0]
            for a in range(1, 4):
                tile = jnp.where(spot == (i + a) % 4, rows[a], tile)
            out_ref[half * 4 + i, TOKENS + KV :] = tile.astype(BF16)


def projected(attn, weight, residual, gain):
    return pl.pallas_call(
        project,
        in_specs=[VMEM] * 4,
        out_specs=VMEM,
        out_shape=jax.ShapeDtypeStruct((8, TOKENS + KV + DRAFTS, HD), BF16),
        compiler_params=pltpu.CompilerParams(vmem_limit_bytes=8 * MIB),
        cost_estimate=pl.CostEstimate(
            flops=0, bytes_accessed=3200000, transcendentals=0
        ),
        name="project",
    )(attn, weight, residual, gain)


def mix(in_ref, *refs):
    spread_ref, mixed_ref, gain_ref = refs[-3:]
    total = in_ref[0].astype(F32)
    for i in range(1, 8):
        total = total + in_ref[i].astype(F32)
    spread_ref[...] = jnp.broadcast_to(total[:TOKENS].astype(BF16)[None], (KV, TOKENS, HD))
    gain_ref[...] = total[TOKENS : TOKENS + KV]
    mixed_ref[...] = total[TOKENS + KV :].astype(BF16)


def mixing(parts, held):
    return pl.pallas_call(
        mix,
        in_specs=[VMEM] + [pl.BlockSpec(memory_space=pl.ANY)] * len(held),
        out_specs=[VMEM, VMEM, VMEM],
        out_shape=[
            jax.ShapeDtypeStruct((KV, TOKENS, HD), BF16),
            jax.ShapeDtypeStruct((DRAFTS, HD), BF16),
            jax.ShapeDtypeStruct((KV, HD), F32),
        ],
        compiler_params=pltpu.CompilerParams(vmem_limit_bytes=8 * MIB),
        cost_estimate=pl.CostEstimate(
            flops=0, bytes_accessed=38400000, transcendentals=0
        ),
        name="mix",
    )(parts, *held)


def widen(mixed_ref, gain_ref, *refs):
    weight_refs, out_ref = refs[:4], refs[4]
    core = lax.axis_index("c")
    units = weight_refs[0].shape[0]
    squares = jnp.zeros((TOKENS, HD), F32)
    sums = [jnp.zeros((units, TOKENS), F32) for _ in weight_refs]
    for k in range(0, KV, 2):
        scaled, places = [], []
        for i in (k, k + 1):
            part = mixed_ref[i].astype(F32)
            squares = squares + part * part
            scaled.append((part * gain_ref[i : i + 1, :]).astype(BF16))
            places.append(pl.ds(pl.multiple_of(i * 256 + core * HD, HD), HD))
        scaled = jnp.concatenate(scaled, axis=1)
        for i, ref in enumerate(weight_refs):
            weight = jnp.concatenate([ref[:, at] for at in places], axis=1)
            sums[i] = sums[i] + nt(weight, scaled)
    square = jnp.sum(jnp.transpose(squares), axis=0, keepdims=True)
    square = jnp.broadcast_to(square, (8, TOKENS))
    own = jnp.concatenate([sums[0], sums[1], square], axis=0)
    other = jnp.concatenate([sums[2], sums[3], square], axis=0)
    out_ref[...] = jnp.concatenate([own, other], axis=1)


def widened(mixed, gain, weights):
    return pl.pallas_call(
        widen,
        in_specs=[VMEM] * 6,
        out_specs=VMEM,
        out_shape=jax.ShapeDtypeStruct((2 * weights[0].shape[0] + 8, HD), F32),
        compiler_params=pltpu.CompilerParams(vmem_limit_bytes=16 * MIB),
        cost_estimate=pl.CostEstimate(
            flops=0, bytes_accessed=6400000, transcendentals=0
        ),
        name="widen",
    )(mixed, gain, *weights)


def narrow(mine_ref, theirs_ref, own_ref, other_ref, out_ref):
    core = lax.axis_index("c")
    units = own_ref.shape[0]
    total = mine_ref[...] + pltpu.roll(theirs_ref[...], TOKENS, 1)
    scale = lax.rsqrt(total[2 * units : 2 * units + 1] / D + EPSILON)
    gate = total[:units] * scale
    upward = total[units : 2 * units] * scale
    hidden = jnp.transpose(gate / (1.0 + jnp.exp(-gate)) * upward)
    hidden = jnp.concatenate([hidden[:TOKENS], hidden[TOKENS:]], axis=1).astype(BF16)
    spot = lanes((TOKENS, HD)) // 32
    masks = [spot == (core + i) % 4 for i in range(4)]
    for y in range(4):
        for z_high in range(2):
            tiles = [None] * 4
            for z_low in range(4):
                k = (z_high * 4 + z_low) * 4 + y
                weight = jnp.concatenate(
                    [ref[:, k * 256 : (k + 1) * 256] for ref in (own_ref, other_ref)], axis=0
                )
                terms = nn(hidden, weight)
                for half in range(2):
                    part = terms[:, half * HD : (half + 1) * HD]
                    if z_low:
                        part = pltpu.roll(part, z_low * 32, 1)
                    for odd in range(2):
                        x = 2 * half + odd
                        mask = masks[(2 * odd + z_low) % 4]
                        tiles[x] = jnp.where(mask, part, tiles[x]) if z_low else part
            for x in range(4):
                out_ref[y * 4 + x, z_high * TOKENS : (z_high + 1) * TOKENS, :] = tiles[x].astype(
                    BF16
                )


def narrowed(mine, theirs, own, other):
    return pl.pallas_call(
        narrow,
        in_specs=[VMEM] * 4,
        out_specs=VMEM,
        out_shape=jax.ShapeDtypeStruct((16, 2 * TOKENS, HD), BF16),
        compiler_params=pltpu.CompilerParams(vmem_limit_bytes=16 * MIB),
        cost_estimate=pl.CostEstimate(
            flops=0, bytes_accessed=6400000, transcendentals=0
        ),
        name="narrow",
    )(mine, theirs, own, other)


def partial_sum(in_ref, out_ref):
    total = in_ref[0].astype(F32)
    for k in range(1, 16):
        total = total + in_ref[k].astype(F32)
    shift = lax.axis_index("x") * 2 + lax.axis_index("c")
    total = pltpu.roll(total, (8 - shift) % 4 * 32, 1)
    lane = lanes((16, HD))
    for z in range(8):
        packed = None
        for a in range(4):
            start = z // 4 * TOKENS + a * 16
            part = pltpu.roll(total[start : start + 16], (a - z % 4) % 4 * 32, 1)
            packed = part if a == 0 else jnp.where(lane >= a * 32, part, packed)
        out_ref[z] = packed.astype(BF16)


def summed(parts):
    return pl.pallas_call(
        partial_sum,
        in_specs=[VMEM],
        out_specs=VMEM,
        out_shape=jax.ShapeDtypeStruct((8, 16, HD), BF16),
        compiler_params=pltpu.CompilerParams(vmem_limit_bytes=16 * MIB),
        cost_estimate=pl.CostEstimate(
            flops=0, bytes_accessed=3200000, transcendentals=0
        ),
        name="partial_sum",
    )(parts)


def finish(parts_ref, mixed_ref, out_ref):
    total = parts_ref[0].astype(F32)
    for z in range(1, 8):
        total = total + parts_ref[z].astype(F32)
    shift = lax.axis_index("x") * 2 + lax.axis_index("c")
    total = total + pltpu.roll(mixed_ref[...].astype(F32), (8 - shift) % 4 * 32, 1)
    tall = jnp.concatenate([pltpu.roll(total, (4 - a) % 4 * 32, 1) for a in range(4)], axis=0)
    out_ref[...] = jnp.transpose(tall)[:32].astype(BF16)


def finished(parts, mixed):
    return pl.pallas_call(
        finish,
        in_specs=[VMEM] * 2,
        out_specs=VMEM,
        out_shape=jax.ShapeDtypeStruct((32, TOKENS), BF16),
        compiler_params=pltpu.CompilerParams(vmem_limit_bytes=8 * MIB),
        cost_estimate=pl.CostEstimate(
            flops=0, bytes_accessed=3200000, transcendentals=0
        ),
        name="finish",
    )(parts, mixed)


SWAP = [(0, 1), (1, 0)]


def trade(part):
    return lax.ppermute(part, "c", SWAP)


def exchange(parts, axes):
    return lax.all_to_all(parts, axes, 0, 0, tiled=True)


def shards(
    lengths,
    queries,
    cache_keys,
    cache_values,
    residual_in,
    out_weight,
    norm_gain,
    gate_weight,
    up_weight,
    down_weight,
):
    weights = [gate_weight.T, up_weight.T]
    parts = attention(lengths, norm_gain, queries, cache_keys, cache_values)
    parts, weights, down_weight = lax.optimization_barrier((parts, weights, down_weight))
    weights = weights + [trade(weight) for weight in weights]
    other_down = trade(down_weight)
    attn, gain = combined(exchange(parts, ("z", "y")))
    attn = exchange(attn, ("z", "y"))
    parts = exchange(projected(attn, out_weight, residual_in.T, gain), ("x", "c"))
    spread, mixed, gain = mixing(parts, weights + [down_weight, other_down])
    sums = widened(exchange(spread, ("z", "y")), gain, weights)
    terms = narrowed(sums, trade(sums), down_weight, other_down)
    terms = summed(exchange(terms, ("y", "x")))
    return finished(exchange(terms, "z"), mixed).T


def solution(mesh):
    fine = Mesh(mesh.devices.reshape(8, 4, 4, 2), ("z", "y", "x", "c"))
    kvseq, head = ("z", "y"), ("x", "c")
    every = kvseq + head
    placed = (
        P(),
        P(None, None, head),
        P(None, kvseq, head),
        P(None, kvseq, head),
        P(None, every),
        P(head, kvseq),
        P(every),
        P(None, every),
        P(None, every),
        P(every, None),
    )
    return jax.shard_map(
        shards, mesh=fine, in_specs=placed, out_specs=P(None, every), check_vma=False
    )
```

time: 113 us -> 108 us (0.956)
  blocking collectives: 51.6 us -> 95.2 us
  waiting for transfers between devices: 25.6 us -> 1.32 us
  starting transfers between devices: 20.2 us -> 0.78 us
  Pallas kernels: 13.8 us -> 10.2 us
  local copies, waits for them, and re-layouts: 1.51 us -> 0.02 us
    all_to_all x3 -> x6, blocking collectives: 51.6 us -> 95.2 us  [exchange(): return lax.all_to_all(parts, axes, 0, 0, tiled=True)]
    all_to_all x2 -> x0, waiting for transfers between devices: 18.7 us -> none  [exchange(): return lax.all_to_all(parts, axes, 0, 0, tiled=True)]
    all_to_all x2 -> x0, starting transfers between devices: 14.8 us -> none  [exchange(): return lax.all_to_all(parts, axes, 0, 0, tiled=True)]
    ppermute x3 -> x0, starting transfers between devices: 4.43 us -> none  [shards(): lax.ppermute(pair, 'x', [(i, (i + s) % 4) for i in range(4)])]
    ppermute x3 -> x0, waiting for transfers between devices: 3.3 us -> none  [shards(): lax.ppermute(pair, 'x', [(i, (i + s) % 4) for i in range(4)])]
    ppermute x6 -> x4, waiting for transfers between devices: 3.68 us -> 1.32 us  [trade(): return lax.ppermute(part, 'c', SWAP)]
    pallas_call x1, Pallas kernels: 3.36 us -> 1.23 us  [widened(): pl.pallas_call(widen, in_specs=[VMEM] * 6, out_specs=VMEM, out_shape=jax....]
    pallas_call x1, Pallas kernels: 2.68 us -> 1.13 us  [narrowed(): pl.pallas_call(narrow, in_specs=[VMEM] * 4, out_specs=VMEM, out_shape=jax...]
  transfers between devices with their start and end apart: 11 -> 4, of which waited for: 8 -> 1; matrix products, arithmetic and copies ran while one was open for 0% -> 0% of each run, Pallas kernels for 3% -> 1%
where the time goes in v3:
time: 108 us
  blocking collectives  95.2 us (88%)
  Pallas kernels  10.2 us (9%)
  waiting for transfers between devices  1.32 us (1%)
    all_to_all x6, blocking collectives, exchange(): return lax.all_to_all(parts, axes, 0, 0, tiled=True)  95.2 us
    pallas_call x1, Pallas kernels, attention(): pl.pallas_call(attend, in_specs=[SMEM, VMEM, VMEM, held, held], out_specs...  6.05 us
  transfers between devices with their start and end apart: 4, of which 1 were waited for; matrix products, arithmetic and copies ran while one was open for 0% of the time, Pallas kernels for 1%

profile of v3, /device:TPU:2, one launch (start us, length us, event | category | flops | bytes accessed | tf_op | source)
XLA Modules:
  0.0 107.6 jit_solution(5390005980087230974)
XLA Ops:
  0.0 0.0 copy-start.1
  0.0 0.0 copy-start
  0.0 0.0 copy-start.3
  0.0 0.0 copy-start.4
  0.0 6.1 %attention.1 = bf16[32,24,128]{2,1,0:T(8,128)(2,1)} custom-call(s32[4]{0:T(128)} %lengths_ref.1, bf16[32]{0:T(256)(128)(2,1)} %gain_ref.1, bf16[4,16,1024]{2,1,0:T(8,128)(2,1)} %q_ref.1, bf16[4,2048,128]{2,1,0:T(8,128)(2,1)} %keys_ref.1, bf16[4,2048,128]{2,1,0:T(8,128)(2,1)} %values_ref.1), custom_call_target="tpu_custom_call" | custom-call | bytes 12800000 | tf_op jit(solution)/shard_map/attention/pallas_call | solution.py:102
  6.1 0.0 copy-start.2
  6.1 0.0 copy-done
  6.1 0.1 collective-permute-start
  6.2 0.0 copy-done.1
  6.2 0.5 collective-permute-start.1
  6.7 0.1 collective-permute-start.2
  6.8 23.8 %all_to_all.30.in_ref = bf16[32,24,128]{2,1,0:T(8,128)(2,1)S(1)} all-to-all(bf16[32,24,128]{2,1,0:T(8,128)(2,1)} %attention.1), channel_id=1, replica_groups=mesh['z'=8,'y'=4,'x'=4,'c'=2] {'z','y'}, dimensions={0} | all-to-all | bytes 393216 | tf_op jit(solution)/shard_map/all_to_all | solution.py:375
  30.6 0.3 combine.1
  30.9 14.0 %all_to_all.31.attn_ref = bf16[32,16,128]{2,1,0:T(8,128)(2,1)S(1)} all-to-all(bf16[32,16,128]{2,1,0:T(8,128)(2,1)S(1)} %get-tuple-element.15), channel_id=1, replica_groups=mesh['z'=8,'y'=4,'x'=4,'c'=2] {'z','y'}, dimensions={0} | all-to-all | bytes 262144 | tf_op jit(solution)/shard_map/all_to_all | solution.py:375
  44.9 0.0 copy-done.3
  44.9 0.0 copy-done.4
  44.9 0.3 project.1
  45.3 10.4 %all_to_all.32.in_ref = bf16[8,112,128]{2,1,0:T(8,128)(2,1)S(1)} all-to-all(bf16[8,112,128]{2,1,0:T(8,128)(2,1)S(1)} %project.1), channel_id=1, replica_groups=mesh['z'=8,'y'=4,'x'=4,'c'=2] {'x','c'}, dimensions={0} | all-to-all | bytes 458752 | tf_op jit(solution)/shard_map/all_to_all | solution.py:375
  55.6 0.0 collective-permute-done.refs_2_
  55.6 0.0 collective-permute-done.1.refs_3_
  55.6 0.0 collective-permute-done.2.refs_5_.other_ref
  55.6 0.0 copy-done.2
  55.7 0.1 mix.1
  55.7 20.7 %all_to_all.33.mixed_ref = bf16[32,64,128]{2,1,0:T(8,128)(2,1)S(1)} all-to-all(bf16[32,64,128]{2,1,0:T(8,128)(2,1)S(1)} %get-tuple-element.20), channel_id=1, replica_groups=mesh['z'=8,'y'=4,'x'=4,'c'=2] {'z','y'}, dimensions={0} | all-to-all | bytes 1048576 | tf_op jit(solution)/shard_map/all_to_all | solution.py:375
  76.5 1.2 %widen.1.mine_ref = f32[232,128]{1,0:T(8,128)S(1)} custom-call(bf16[32,64,128]{2,1,0:T(8,128)(2,1)S(1)} %all_to_all.33.mixed_ref, f32[32,128]{1,0:T(8,128)S(1)} %get-tuple-element.21.gain_ref, bf16[112,8192]{1,0:T(8,128)(2,1)S(1)} %bitcast.6, bf16[112,8192]{1,0:T(8,128)(2,1)S(1)} %bitcast.9, bf16[112,8192]{1,0:T(8,128)(2,1)S(1)} %collective-permute-done.refs_2_, ...), custom_call_target="tpu_custom_call" | custom-call | bytes 6400000 | tf_op jit(solution)/shard_map/widen/pallas_call | solution.py:252
  77.7 0.1 collective-permute-start.3
  77.8 1.3 %collective-permute-done.3.theirs_ref = f32[232,128]{1,0:T(8,128)S(1)} collective-permute-done((f32[232,128]{1,0:T(8,128)S(1)}, f32[232,128]{1,0:T(8,128)S(1)}, u32[]{:S(2)}, u32[]{:S(2)}) %collective-permute-start.3) | collective-permute-done | bytes 118816 | tf_op jit(solution)/shard_map/ppermute | solution.py:371
  79.1 1.1 %narrow.1 = bf16[16,128,128]{2,1,0:T(8,128)(2,1)S(1)} custom-call(f32[232,128]{1,0:T(8,128)S(1)} %widen.1.mine_ref, f32[232,128]{1,0:T(8,128)S(1)} %collective-permute-done.3.theirs_ref, bf16[112,8192]{1,0:T(8,128)(2,1)S(1)} %copy-done.2, bf16[112,8192]{1,0:T(8,128)(2,1)S(1)} %collective-permute-done.2.refs_5_.other_ref), custom_call_target="tpu_custom_call" | custom-call | bytes 6400000 | tf_op jit(solution)/shard_map/narrow/pallas_call | solution.py:300
  80.2 15.9 %all_to_all.34.in_ref = bf16[16,128,128]{2,1,0:T(8,128)(2,1)S(1)} all-to-all(bf16[16,128,128]{2,1,0:T(8,128)(2,1)S(1)} %narrow.1), channel_id=1, replica_groups=mesh['z'=8,'y'=4,'x'=4,'c'=2] {'y','x'}, dimensions={0} | all-to-all | bytes 1048576 | tf_op jit(solution)/shard_map/all_to_all | solution.py:375
  96.2 0.2 partial_sum.1
  96.4 10.4 %all_to_all.35.parts_ref = bf16[8,16,128]{2,1,0:T(8,128)(2,1)S(1)} all-to-all(bf16[8,16,128]{2,1,0:T(8,128)(2,1)S(1)} %partial_sum.1), channel_id=1, replica_groups=mesh['z'=8,'y'=4,'x'=4,'c'=2] {'z'}, dimensions={0} | all-to-all | bytes 65536 | tf_op jit(solution)/shard_map/all_to_all | solution.py:375
  106.8 0.8 finish.1
Async XLA Ops:
  0.0 6.2 %copy-start.1 = (bf16[8192,112]{0,1:T(8,128)(2,1)S(1)}, bf16[8192,112]{0,1:T(8,128)(2,1)}, u32[]{:S(2)}) copy-start(bf16[8192,112]{0,1:T(8,128)(2,1)} %param.18) | copy-start | bytes 5505028
  0.0 6.1 %copy-start = (bf16[8192,112]{0,1:T(8,128)(2,1)S(1)}, bf16[8192,112]{0,1:T(8,128)(2,1)}, u32[]{:S(2)}) copy-start(bf16[8192,112]{0,1:T(8,128)(2,1)} %param.17) | copy-start | bytes 5505028
  0.0 44.9 %copy-start.3 = (bf16[1024,256]{1,0:T(8,128)(2,1)S(1)}, bf16[1024,256]{1,0:T(8,128)(2,1)}, u32[]{:S(2)}) copy-start(bf16[1024,256]{1,0:T(8,128)(2,1)} %weight_ref.1) | copy-start | bytes 1572868
  0.0 44.9 %copy-start.4 = (bf16[64,32]{0,1:T(8,128)(2,1)S(1)}, bf16[64,32]{0,1:T(8,128)(2,1)}, u32[]{:S(2)}) copy-start(bf16[64,32]{0,1:T(8,128)(2,1)} %param.14) | copy-start | bytes 12292
  6.1 49.6 %copy-start.2 = (bf16[112,8192]{1,0:T(8,128)(2,1)S(1)}, bf16[112,8192]{1,0:T(8,128)(2,1)}, u32[]{:S(2)}) copy-start(bf16[112,8192]{1,0:T(8,128)(2,1)} %own_ref) | copy-start | bytes 5505028
  6.1 49.5 %collective-permute-start = (bf16[112,8192]{1,0:T(8,128)(2,1)S(1)}, bf16[112,8192]{1,0:T(8,128)(2,1)S(1)}, u32[]{:S(2)}, u32[]{:S(2)}) collective-permute-start(bf16[112,8192]{1,0:T(8,128)(2,1)S(1)} %bitcast.4), channel_id=1, source_target_pairs={{0,1},{1,0},{2,3},{3,2},{4,5},{5,4},{6,7},{7,6},{8,9},{9,8},{10,11... | collective-permute-start | bytes 5505032 | tf_op jit(solution)/shard_map/ppermute | solution.py:371
  6.2 49.4 %collective-permute-start.1 = (bf16[112,8192]{1,0:T(8,128)(2,1)S(1)}, bf16[112,8192]{1,0:T(8,128)(2,1)S(1)}, u32[]{:S(2)}, u32[]{:S(2)}) collective-permute-start(bf16[112,8192]{1,0:T(8,128)(2,1)S(1)} %bitcast.7), channel_id=1, source_target_pairs={{0,1},{1,0},{2,3},{3,2},{4,5},{5,4},{6,7},{7,6},{8,9},{9,8},{10,11... | collective-permute-start | bytes 5505032 | tf_op jit(solution)/shard_map/ppermute | solution.py:371
  6.7 48.9 %collective-permute-start.2 = (bf16[112,8192]{1,0:T(8,128)(2,1)}, bf16[112,8192]{1,0:T(8,128)(2,1)S(1)}, u32[]{:S(2)}, u32[]{:S(2)}) collective-permute-start(bf16[112,8192]{1,0:T(8,128)(2,1)} %own_ref), channel_id=1, source_target_pairs={{0,1},{1,0},{2,3},{3,2},{4,5},{5,4},{6,7},{7,6},{8,9},{9,8},{10,11... | collective-permute-start | bytes 5505032 | tf_op jit(solution)/shard_map/ppermute | solution.py:371
  77.7 1.4 %collective-permute-start.3 = (f32[232,128]{1,0:T(8,128)S(1)}, f32[232,128]{1,0:T(8,128)S(1)}, u32[]{:S(2)}, u32[]{:S(2)}) collective-permute-start(f32[232,128]{1,0:T(8,128)S(1)} %widen.1.mine_ref), channel_id=1, source_target_pairs={{0,1},{1,0},{2,3},{3,2},{4,5},{5,4},{6,7},{7,6},{8,9},{9,8},{10,11... | collective-permute-start | bytes 356360 | tf_op jit(solution)/shard_map/ppermute | solution.py:371

commit v4 on v3

--- a/solution.py
+++ b/solution.py
@@ -45,18 +45,20 @@
 
 
 def attend(
-    lengths_ref, gain_ref, q_ref, keys_ref, values_ref, out_ref, k_ref, v_ref, score_ref, sems
+    lengths_ref, gain_ref, queries_ref, keys_ref, values_ref, out_ref,
+    q_ref, k_ref, v_ref, score_ref, sems,
 ):
     copies = []
-    for row in range(ROWS):
+    pairs = [(queries_ref, q_ref), (keys_ref, k_ref), (values_ref, v_ref)]
+    for n, (first, last) in enumerate([(0, 1), (1, ROWS)]):
         copies.append(
             [
-                pltpu.make_async_copy(keys_ref.at[row], k_ref.at[row], sems.at[row, 0]),
-                pltpu.make_async_copy(values_ref.at[row], v_ref.at[row], sems.at[row, 1]),
+                pltpu.make_async_copy(a.at[first:last], b.at[first:last], sems.at[n, i])
+                for i, (a, b) in enumerate(pairs)
             ]
         )
-        for copy in copies[row]:
-            copy.start()
+        for i in (1, 0, 2):
+            copies[n][i].start()
     first_key = (lax.axis_index("z") * 4 + lax.axis_index("y")) * SLICE
     draft = lax.broadcasted_iota(jnp.int32, (GROUP * DRAFTS, CHUNK), 0) % DRAFTS
     offset = draft - DRAFTS - lanes((GROUP * DRAFTS, CHUNK)) - first_key
@@ -64,12 +66,15 @@
     gain = jnp.concatenate([gain] * 4, axis=1).reshape(1, 1, HD)
     lane = lanes((GROUP, 8, HD))
     for row in range(ROWS):
+        if row < 2:
+            copies[row][0].wait()
         queries = jnp.concatenate(
             [q_ref[row, :, g * HD : (g + 1) * HD] for g in range(GROUP)], axis=0
         )
         limit = offset + lengths_ref[row]
         peak = jnp.full((GROUP * DRAFTS, HD), NEG, F32)
-        copies[row][0].wait()
+        if row < 2:
+            copies[row][1].wait()
         for n in range(SLICE // CHUNK):
             scores = nt(queries, k_ref[row, n * CHUNK : (n + 1) * CHUNK, :]) * LOG_SCALE
             scores = jnp.where(limit >= n * CHUNK, scores, NEG)
@@ -80,7 +85,8 @@
         base = jnp.maximum(top, FLOOR)
         acc = jnp.zeros((GROUP * DRAFTS, HD), F32)
         sums = jnp.zeros((GROUP * DRAFTS, HD), F32)
-        copies[row][1].wait()
+        if row < 2:
+            copies[row][2].wait()
         for n in range(SLICE // CHUNK):
             weights = jnp.exp2(score_ref[row % 2, :, n * CHUNK : (n + 1) * CHUNK] - base)
             for i in range(CHUNK // HD):
@@ -101,19 +107,17 @@
     held = pl.BlockSpec(memory_space=pltpu.HBM)
     return pl.pallas_call(
         attend,
-        in_specs=[SMEM, VMEM, VMEM, held, held],
+        in_specs=[SMEM, VMEM, held, held, held],
         out_specs=VMEM,
         out_shape=jax.ShapeDtypeStruct((KV, 24, HD), BF16),
         scratch_shapes=[
+            pltpu.VMEM((ROWS, DRAFTS, GROUP * HD), BF16),
             pltpu.VMEM((ROWS, SLICE, HD), BF16),
             pltpu.VMEM((ROWS, SLICE, HD), BF16),
             pltpu.VMEM((2, GROUP * DRAFTS, SLICE), F32),
-            pltpu.SemaphoreType.DMA((ROWS, 2)),
+            pltpu.SemaphoreType.DMA((2, 3)),
         ],
         compiler_params=pltpu.CompilerParams(vmem_limit_bytes=57 * MIB),
-        cost_estimate=pl.CostEstimate(
-            flops=0, bytes_accessed=12800000, transcendentals=0
-        ),
         name="attention",
     )(lengths, gain, queries, keys, values)
 
@@ -145,13 +149,14 @@
         ],
         compiler_params=pltpu.CompilerParams(vmem_limit_bytes=16 * MIB),
         cost_estimate=pl.CostEstimate(
-            flops=0, bytes_accessed=38400000, transcendentals=0
+            flops=10000000000, bytes_accessed=0, transcendentals=0
         ),
         name="combine",
     )(parts)
 
 
-def project(attn_ref, weight_ref, residual_ref, gain_ref, out_ref):
+def project(attn_ref, weight_ref, residual_ref, gain_ref, *refs):
+    own_ref, other_ref = refs[-2:]
     head = lax.axis_index("x") * 2 + lax.axis_index("c")
     attn = jnp.concatenate(
         [
@@ -167,40 +172,74 @@
     source = lax.broadcasted_iota(jnp.int32, (HD, 256), 0)
     put = (lanes((HD, 256)) == head * 32 + source - 64) & (source >= 64) & (source < 96)
     gain = nn(gain_ref[...], put.astype(F32).astype(BF16))
-    both = jnp.concatenate([spread, gain], axis=0).astype(BF16)
-    for i in range(8):
-        out_ref[i, : TOKENS + KV] = both[:, i % 2 * HD : (i % 2 + 1) * HD]
+    both = jnp.concatenate([spread, gain], axis=0)
+    core = lax.axis_index("c")
+    own_ref[: TOKENS + KV] = jnp.where(core == 0, both[:, :HD], both[:, HD:])
+    other_ref[: TOKENS + KV] = jnp.where(core == 0, both[:, HD:], both[:, :HD]).astype(BF16)
     spot = lanes((DRAFTS, HD)) // 32
     for half in range(2):
         part = spread[:, half * HD : (half + 1) * HD]
         rows = [part[a * DRAFTS : (a + 1) * DRAFTS] for a in range(4)]
         rows = [pltpu.roll(row, a * 32, 1) if a else row for a, row in enumerate(rows)]
-        for i in range(4):
-            tile = rows[0]
-            for a in range(1, 4):
-                tile = jnp.where(spot == (i + a) % 4, rows[a], tile)
-            out_ref[half * 4 + i, TOKENS + KV :] = tile.astype(BF16)
-
-
-def projected(attn, weight, residual, gain):
+        for i in range(0, 4, 2):
+            tiles = []
+            for j in (i, i + 1):
+                tile = rows[0]
+                for a in range(1, 4):
+                    tile = jnp.where(spot == (j + a) % 4, rows[a], tile)
+                tiles.append(tile)
+            start = TOKENS + KV + (half * 2 + i // 2) * DRAFTS
+            own_ref[start : start + DRAFTS] = jnp.where(core == 0, tiles[0], tiles[1])
+            other_ref[start : start + DRAFTS] = jnp.where(core == 0, tiles[1], tiles[0]).astype(BF16)
+
+
+def projected(attn, weight, residual, gain, held):
     return pl.pallas_call(
         project,
-        in_specs=[VMEM] * 4,
-        out_specs=VMEM,
-        out_shape=jax.ShapeDtypeStruct((8, TOKENS + KV + DRAFTS, HD), BF16),
+        in_specs=[VMEM] * 4 + [pl.BlockSpec(memory_space=pl.ANY)] * len(held),
+        out_specs=[VMEM, VMEM],
+        out_shape=[
+            jax.ShapeDtypeStruct((TOKENS + KV + 4 * DRAFTS, HD), F32),
+            jax.ShapeDtypeStruct((TOKENS + KV + 4 * DRAFTS, HD), BF16),
+        ],
         compiler_params=pltpu.CompilerParams(vmem_limit_bytes=8 * MIB),
         cost_estimate=pl.CostEstimate(
-            flops=0, bytes_accessed=3200000, transcendentals=0
+            flops=1000000000, bytes_accessed=0, transcendentals=0
         ),
         name="project",
-    )(attn, weight, residual, gain)
-
-
-def mix(in_ref, *refs):
+    )(attn, weight, residual, gain, *held)
+
+
+def pair(own_ref, other_ref, *refs):
+    sum_ref = refs[4]
+    sum_ref[...] = own_ref[...] + other_ref[...].astype(F32)
+    common = sum_ref[: TOKENS + KV].astype(BF16)
+    for s in range(4):
+        x = (lax.axis_index("x") + s) % 4
+        start = pl.multiple_of(TOKENS + KV + x * DRAFTS, DRAFTS)
+        refs[s][: TOKENS + KV] = common
+        refs[s][TOKENS + KV :] = sum_ref[pl.ds(start, DRAFTS), :].astype(BF16)
+
+
+def paired(own, other):
+    shape = jax.ShapeDtypeStruct((TOKENS + KV + DRAFTS, HD), BF16)
+    return pl.pallas_call(
+        pair,
+        in_specs=[VMEM, VMEM],
+        out_specs=[VMEM] * 4,
+        out_shape=[shape] * 4,
+        scratch_shapes=[pltpu.VMEM((TOKENS + KV + 4 * DRAFTS, HD), F32)],
+        compiler_params=pltpu.CompilerParams(vmem_limit_bytes=8 * MIB),
+        name="pair",
+    )(own, other)
+
+
+def mix(*refs):
+    parts = refs[:4]
     spread_ref, mixed_ref, gain_ref = refs[-3:]
-    total = in_ref[0].astype(F32)
-    for i in range(1, 8):
-        total = total + in_ref[i].astype(F32)
+    total = (parts[0][...].astype(F32) + parts[1][...].astype(F32)) + (
+        parts[2][...].astype(F32) + parts[3][...].astype(F32)
+    )
     spread_ref[...] = jnp.broadcast_to(total[:TOKENS].astype(BF16)[None], (KV, TOKENS, HD))
     gain_ref[...] = total[TOKENS : TOKENS + KV]
     mixed_ref[...] = total[TOKENS + KV :].astype(BF16)
@@ -209,7 +248,7 @@
 def mixing(parts, held):
     return pl.pallas_call(
         mix,
-        in_specs=[VMEM] + [pl.BlockSpec(memory_space=pl.ANY)] * len(held),
+        in_specs=[VMEM] * 4 + [pl.BlockSpec(memory_space=pl.ANY)] * len(held),
         out_specs=[VMEM, VMEM, VMEM],
         out_shape=[
             jax.ShapeDtypeStruct((KV, TOKENS, HD), BF16),
@@ -218,10 +257,10 @@
         ],
         compiler_params=pltpu.CompilerParams(vmem_limit_bytes=8 * MIB),
         cost_estimate=pl.CostEstimate(
-            flops=0, bytes_accessed=38400000, transcendentals=0
+            flops=1000000000, bytes_accessed=0, transcendentals=0
         ),
         name="mix",
-    )(parts, *held)
+    )(*parts, *held)
 
 
 def widen(mixed_ref, gain_ref, *refs):
@@ -255,9 +294,6 @@
         out_specs=VMEM,
         out_shape=jax.ShapeDtypeStruct((2 * weights[0].shape[0] + 8, HD), F32),
         compiler_params=pltpu.CompilerParams(vmem_limit_bytes=16 * MIB),
-        cost_estimate=pl.CostEstimate(
-            flops=0, bytes_accessed=6400000, transcendentals=0
-        ),
         name="widen",
     )(mixed, gain, *weights)
 
@@ -303,9 +339,6 @@
         out_specs=VMEM,
         out_shape=jax.ShapeDtypeStruct((16, 2 * TOKENS, HD), BF16),
         compiler_params=pltpu.CompilerParams(vmem_limit_bytes=16 * MIB),
-        cost_estimate=pl.CostEstimate(
-            flops=0, bytes_accessed=6400000, transcendentals=0
-        ),
         name="narrow",
     )(mine, theirs, own, other)
 
@@ -333,9 +366,6 @@
         out_specs=VMEM,
         out_shape=jax.ShapeDtypeStruct((8, 16, HD), BF16),
         compiler_params=pltpu.CompilerParams(vmem_limit_bytes=16 * MIB),
-        cost_estimate=pl.CostEstimate(
-            flops=0, bytes_accessed=3200000, transcendentals=0
-        ),
         name="partial_sum",
     )(parts)
 
@@ -357,9 +387,6 @@
         out_specs=VMEM,
         out_shape=jax.ShapeDtypeStruct((32, TOKENS), BF16),
         compiler_params=pltpu.CompilerParams(vmem_limit_bytes=8 * MIB),
-        cost_estimate=pl.CostEstimate(
-            flops=0, bytes_accessed=3200000, transcendentals=0
-        ),
         name="finish",
     )(parts, mixed)
 
@@ -394,8 +421,13 @@
     other_down = trade(down_weight)
     attn, gain = combined(exchange(parts, ("z", "y")))
     attn = exchange(attn, ("z", "y"))
-    parts = exchange(projected(attn, out_weight, residual_in.T, gain), ("x", "c"))
-    spread, mixed, gain = mixing(parts, weights + [down_weight, other_down])
+    own, other = projected(attn, out_weight, residual_in.T, gain, weights[2:] + [other_down])
+    parts = list(paired(own, trade(other)))
+    parts[1:] = [
+        lax.ppermute(part, "x", [(i, (i + s) % 4) for i in range(4)])
+        for s, part in enumerate(parts[1:], 1)
+    ]
+    spread, mixed, gain = mixing(parts, [])
     sums = widened(exchange(spread, ("z", "y")), gain, weights)
     terms = narrowed(sums, trade(sums), down_weight, other_down)
     terms = summed(exchange(terms, ("y", "x")))

time: 108 us -> 106 us (0.981)
  blocking collectives: 95.2 us -> 85.6 us
  starting transfers between devices: 0.78 us -> 5.7 us
  waiting for transfers between devices: 1.32 us -> 4.64 us
    all_to_all x6 -> x5, blocking collectives: 95.2 us -> 85.6 us  [exchange(): return lax.all_to_all(parts, axes, 0, 0, tiled=True)]
    ppermute x0 -> x3, starting transfers between devices: none -> 4.83 us  [shards(): lax.ppermute(part, 'x', [(i, (i + s) % 4) for i in range(4)])]
    ppermute x0 -> x3, waiting for transfers between devices: none -> 2.11 us  [shards(): lax.ppermute(part, 'x', [(i, (i + s) % 4) for i in range(4)])]
    ppermute x4 -> x5, waiting for transfers between devices: 1.32 us -> 2.53 us  [trade(): return lax.ppermute(part, 'c', SWAP)]
    pallas_call x3 -> x4, Pallas kernels: 6.45 us -> 5.76 us  [the longest x1 5.34 us: attention(): pl.pallas_call(attend, in_specs=[SMEM, VMEM, held, held, held], out_specs...]
  transfers between devices with their start and end apart: 4 -> 8, of which waited for: 1 -> 3; matrix products, arithmetic and copies ran while one was open for 0% -> 0% of each run, Pallas kernels for 1% -> 0%
where the time goes in v4:
time: 106 us
  blocking collectives  85.6 us (81%)
  Pallas kernels  9.46 us (9%)
  starting transfers between devices  5.7 us (5%)
  waiting for transfers between devices  4.64 us (4%)
    all_to_all x5, blocking collectives, exchange(): return lax.all_to_all(parts, axes, 0, 0, tiled=True)  85.6 us
    pallas_call x1, Pallas kernels, attention(): pl.pallas_call(attend, in_specs=[SMEM, VMEM, held, held, held], out_specs...  5.34 us
    ppermute x3, starting transfers between devices, shards(): lax.ppermute(part, 'x', [(i, (i + s) % 4) for i in range(4)])  4.83 us
    ppermute x5, waiting for transfers between devices, trade(): return lax.ppermute(part, 'c', SWAP)  2.53 us
  transfers between devices with their start and end apart: 8, of which 3 were waited for; matrix products, arithmetic and copies ran while one was open for 0% of the time, Pallas kernels for 0%

profile of v4, /device:TPU:2, one launch (start us, length us, event | category | flops | bytes accessed | tf_op | source)
XLA Modules:
  0.0 105.6 jit_solution(4866259027743767019)
XLA Ops:
  0.0 0.0 copy-start.1
  0.0 0.0 copy-start
  0.0 5.3 %attention.1 = bf16[32,24,128]{2,1,0:T(8,128)(2,1)} custom-call(s32[4]{0:T(128)} %lengths_ref.1, bf16[32]{0:T(256)(128)(2,1)} %gain_ref.1, bf16[4,16,1024]{2,1,0:T(8,128)(2,1)} %queries_ref.1, bf16[4,2048,128]{2,1,0:T(8,128)(2,1)} %keys_ref.1, bf16[4,2048,128]{2,1,0:T(8,128)(2,1)} %values_ref.1), custom_call_target="tpu_custom_call" | custom-call | tf_op jit(solution)/shard_map/attention/pallas_call | solution.py:108
  5.4 0.0 copy-done
  5.4 0.1 collective-permute-start
  5.5 0.0 copy-done.1
  5.5 0.5 collective-permute-start.1
  6.0 0.1 collective-permute-start.2
  6.1 23.8 %all_to_all.25.in_ref = bf16[32,24,128]{2,1,0:T(8,128)(2,1)S(1)} all-to-all(bf16[32,24,128]{2,1,0:T(8,128)(2,1)} %attention.1), channel_id=1, replica_groups=mesh['z'=8,'y'=4,'x'=4,'c'=2] {'z','y'}, dimensions={0} | all-to-all | bytes 393216 | tf_op jit(solution)/shard_map/all_to_all | solution.py:402
  29.9 0.0 copy-start.3
  29.9 0.0 copy-start.4
  29.9 0.3 combine.1
  30.2 14.0 %all_to_all.26.attn_ref = bf16[32,16,128]{2,1,0:T(8,128)(2,1)S(1)} all-to-all(bf16[32,16,128]{2,1,0:T(8,128)(2,1)S(1)} %get-tuple-element.21), channel_id=1, replica_groups=mesh['z'=8,'y'=4,'x'=4,'c'=2] {'z','y'}, dimensions={0} | all-to-all | bytes 262144 | tf_op jit(solution)/shard_map/all_to_all | solution.py:402
  44.2 0.0 collective-permute-done.refs_0_.refs_2_
  44.2 0.0 collective-permute-done.1.refs_1_.refs_3_
  44.2 0.0 collective-permute-done.2.refs_2_.other_ref
  44.2 0.0 copy-done.3
  44.2 0.0 copy-done.4
  44.2 0.3 project.1
  44.6 0.1 collective-permute-start.3
  44.7 1.2 %collective-permute-done.3.other_ref = bf16[160,128]{1,0:T(8,128)(2,1)S(1)} collective-permute-done((bf16[160,128]{1,0:T(8,128)(2,1)S(1)}, bf16[160,128]{1,0:T(8,128)(2,1)S(1)}, u32[]{:S(2)}, u32[]{:S(2)}) %collective-permute-start.3) | collective-permute-done | bytes 40992 | tf_op jit(solution)/shard_map/ppermute | solution.py:398
  45.9 1.6 %collective-permute-start.4 = (bf16[112,128]{1,0:T(8,128)(2,1)S(1)}, bf16[112,128]{1,0:T(8,128)(2,1)S(1)}, u32[]{:S(2)}, u32[]{:S(2)}) collective-permute-start(bf16[112,128]{1,0:T(8,128)(2,1)S(1)} %get-tuple-element.29), channel_id=1, source_target_pairs={{0,2},{2,4},{4,6},{6,0},{1,3},{3,5},{5,7},{7,1},{8,10},{10,12},{12... | collective-permute-start | bytes 86024 | tf_op jit(solution)/shard_map/ppermute | solution.py:427
  47.5 1.1 %collective-permute-start.5 = (bf16[112,128]{1,0:T(8,128)(2,1)S(1)}, bf16[112,128]{1,0:T(8,128)(2,1)S(1)}, u32[]{:S(2)}, u32[]{:S(2)}) collective-permute-start(bf16[112,128]{1,0:T(8,128)(2,1)S(1)} %get-tuple-element.30), channel_id=1, source_target_pairs={{0,4},{2,6},{4,0},{6,2},{1,5},{3,7},{5,1},{7,3},{8,12},{10,14},{12... | collective-permute-start | bytes 86024 | tf_op jit(solution)/shard_map/ppermute | solution.py:427
  48.6 2.1 %collective-permute-start.6 = (bf16[112,128]{1,0:T(8,128)(2,1)S(1)}, bf16[112,128]{1,0:T(8,128)(2,1)S(1)}, u32[]{:S(2)}, u32[]{:S(2)}) collective-permute-start(bf16[112,128]{1,0:T(8,128)(2,1)S(1)} %get-tuple-element.31), channel_id=1, source_target_pairs={{0,6},{2,0},{4,2},{6,4},{1,7},{3,1},{5,3},{7,5},{8,14},{10,8},{12,... | collective-permute-start | bytes 86024 | tf_op jit(solution)/shard_map/ppermute | solution.py:427
  50.7 0.0 collective-permute-done.4.refs_1_
  50.7 2.1 %collective-permute-done.5.refs_2_ = bf16[112,128]{1,0:T(8,128)(2,1)S(1)} collective-permute-done((bf16[112,128]{1,0:T(8,128)(2,1)S(1)}, bf16[112,128]{1,0:T(8,128)(2,1)S(1)}, u32[]{:S(2)}, u32[]{:S(2)}) %collective-permute-start.5) | collective-permute-done | bytes 28704 | tf_op jit(solution)/shard_map/ppermute | solution.py:427
  52.8 0.0 collective-permute-done.6.refs_3_
  52.8 0.1 mix.1
  52.9 20.0 %all_to_all.27.mixed_ref = bf16[32,64,128]{2,1,0:T(8,128)(2,1)S(1)} all-to-all(bf16[32,64,128]{2,1,0:T(8,128)(2,1)S(1)} %get-tuple-element.32), channel_id=1, replica_groups=mesh['z'=8,'y'=4,'x'=4,'c'=2] {'z','y'}, dimensions={0} | all-to-all | bytes 1048576 | tf_op jit(solution)/shard_map/all_to_all | solution.py:402
  72.9 0.0 copy-start.2
  72.9 1.2 %widen.1.mine_ref = f32[232,128]{1,0:T(8,128)S(1)} custom-call(bf16[32,64,128]{2,1,0:T(8,128)(2,1)S(1)} %all_to_all.27.mixed_ref, f32[32,128]{1,0:T(8,128)S(1)} %get-tuple-element.33.gain_ref, bf16[112,8192]{1,0:T(8,128)(2,1)S(1)} %bitcast.5, bf16[112,8192]{1,0:T(8,128)(2,1)S(1)} %bitcast.7, bf16[112,8192]{1,0:T(8,128)(2,1)S(1)} %collective-permute-done.refs_0_.refs_2_, ...), custom_call_target="tpu_custom_call" | custom-call | tf_op jit(solution)/shard_map/widen/pallas_call | solution.py:291
  74.1 0.1 collective-permute-start.7
  74.2 1.3 %collective-permute-done.7.theirs_ref = f32[232,128]{1,0:T(8,128)S(1)} collective-permute-done((f32[232,128]{1,0:T(8,128)S(1)}, f32[232,128]{1,0:T(8,128)S(1)}, u32[]{:S(2)}, u32[]{:S(2)}) %collective-permute-start.7) | collective-permute-done | bytes 118816 | tf_op jit(solution)/shard_map/ppermute | solution.py:398
  75.6 0.0 copy-done.2
  75.6 1.1 %narrow.1 = bf16[16,128,128]{2,1,0:T(8,128)(2,1)S(1)} custom-call(f32[232,128]{1,0:T(8,128)S(1)} %widen.1.mine_ref, f32[232,128]{1,0:T(8,128)S(1)} %collective-permute-done.7.theirs_ref, bf16[112,8192]{1,0:T(8,128)(2,1)S(1)} %copy-done.2, bf16[112,8192]{1,0:T(8,128)(2,1)S(1)} %collective-permute-done.2.refs_2_.other_ref), custom_call_target="tpu_custom_call" | custom-call | tf_op jit(solution)/shard_map/narrow/pallas_call | solution.py:336
  76.7 17.4 %all_to_all.28.in_ref = bf16[16,128,128]{2,1,0:T(8,128)(2,1)S(1)} all-to-all(bf16[16,128,128]{2,1,0:T(8,128)(2,1)S(1)} %narrow.1), channel_id=1, replica_groups=mesh['z'=8,'y'=4,'x'=4,'c'=2] {'y','x'}, dimensions={0} | all-to-all | bytes 1048576 | tf_op jit(solution)/shard_map/all_to_all | solution.py:402
  94.1 0.2 partial_sum.1
  94.3 10.4 %all_to_all.29.parts_ref = bf16[8,16,128]{2,1,0:T(8,128)(2,1)S(1)} all-to-all(bf16[8,16,128]{2,1,0:T(8,128)(2,1)S(1)} %partial_sum.1), channel_id=1, replica_groups=mesh['z'=8,'y'=4,'x'=4,'c'=2] {'z'}, dimensions={0} | all-to-all | bytes 65536 | tf_op jit(solution)/shard_map/all_to_all | solution.py:402
  104.7 0.8 finish.1
  (1 shorter events, 0.0 us)
Async XLA Ops:
  0.0 5.5 %copy-start.1 = (bf16[8192,112]{0,1:T(8,128)(2,1)S(1)}, bf16[8192,112]{0,1:T(8,128)(2,1)}, u32[]{:S(2)}) copy-start(bf16[8192,112]{0,1:T(8,128)(2,1)} %param.18) | copy-start | bytes 5505028
  0.0 5.4 %copy-start = (bf16[8192,112]{0,1:T(8,128)(2,1)S(1)}, bf16[8192,112]{0,1:T(8,128)(2,1)}, u32[]{:S(2)}) copy-start(bf16[8192,112]{0,1:T(8,128)(2,1)} %param.17) | copy-start | bytes 5505028
  5.4 38.8 %collective-permute-start = (bf16[112,8192]{1,0:T(8,128)(2,1)S(1)}, bf16[112,8192]{1,0:T(8,128)(2,1)S(1)}, u32[]{:S(2)}, u32[]{:S(2)}) collective-permute-start(bf16[112,8192]{1,0:T(8,128)(2,1)S(1)} %bitcast.4), channel_id=1, source_target_pairs={{0,1},{1,0},{2,3},{3,2},{4,5},{5,4},{6,7},{7,6},{8,9},{9,8},{10,11... | collective-permute-start | bytes 5505032 | tf_op jit(solution)/shard_map/ppermute | solution.py:398
  5.5 38.7 %collective-permute-start.1 = (bf16[112,8192]{1,0:T(8,128)(2,1)S(1)}, bf16[112,8192]{1,0:T(8,128)(2,1)S(1)}, u32[]{:S(2)}, u32[]{:S(2)}) collective-permute-start(bf16[112,8192]{1,0:T(8,128)(2,1)S(1)} %bitcast.6), channel_id=1, source_target_pairs={{0,1},{1,0},{2,3},{3,2},{4,5},{5,4},{6,7},{7,6},{8,9},{9,8},{10,11... | collective-permute-start | bytes 5505032 | tf_op jit(solution)/shard_map/ppermute | solution.py:398
  6.0 38.2 %collective-permute-start.2 = (bf16[112,8192]{1,0:T(8,128)(2,1)}, bf16[112,8192]{1,0:T(8,128)(2,1)S(1)}, u32[]{:S(2)}, u32[]{:S(2)}) collective-permute-start(bf16[112,8192]{1,0:T(8,128)(2,1)} %own_ref), channel_id=1, source_target_pairs={{0,1},{1,0},{2,3},{3,2},{4,5},{5,4},{6,7},{7,6},{8,9},{9,8},{10,11... | collective-permute-start | bytes 5505032 | tf_op jit(solution)/shard_map/ppermute | solution.py:398
  29.9 14.4 %copy-start.3 = (bf16[1024,256]{1,0:T(8,128)(2,1)S(1)}, bf16[1024,256]{1,0:T(8,128)(2,1)}, u32[]{:S(2)}) copy-start(bf16[1024,256]{1,0:T(8,128)(2,1)} %weight_ref.1) | copy-start | bytes 1572868
  29.9 14.4 %copy-start.4 = (bf16[64,32]{0,1:T(8,128)(2,1)S(1)}, bf16[64,32]{0,1:T(8,128)(2,1)}, u32[]{:S(2)}) copy-start(bf16[64,32]{0,1:T(8,128)(2,1)} %param.14) | copy-start | bytes 12292
  44.6 1.3 %collective-permute-start.3 = (bf16[160,128]{1,0:T(8,128)(2,1)S(1)}, bf16[160,128]{1,0:T(8,128)(2,1)S(1)}, u32[]{:S(2)}, u32[]{:S(2)}) collective-permute-start(bf16[160,128]{1,0:T(8,128)(2,1)S(1)} %get-tuple-element.27), channel_id=1, source_target_pairs={{0,1},{1,0},{2,3},{3,2},{4,5},{5,4},{6,7},{7,6},{8,9},{9,8},{10,11... | collective-permute-start | bytes 122888 | tf_op jit(solution)/shard_map/ppermute | solution.py:398
  45.9 4.8 %collective-permute-start.4 = (bf16[112,128]{1,0:T(8,128)(2,1)S(1)}, bf16[112,128]{1,0:T(8,128)(2,1)S(1)}, u32[]{:S(2)}, u32[]{:S(2)}) collective-permute-start(bf16[112,128]{1,0:T(8,128)(2,1)S(1)} %get-tuple-element.29), channel_id=1, source_target_pairs={{0,2},{2,4},{4,6},{6,0},{1,3},{3,5},{5,7},{7,1},{8,10},{10,12},{12... | collective-permute-start | bytes 86024 | tf_op jit(solution)/shard_map/ppermute | solution.py:427
  47.5 5.4 %collective-permute-start.5 = (bf16[112,128]{1,0:T(8,128)(2,1)S(1)}, bf16[112,128]{1,0:T(8,128)(2,1)S(1)}, u32[]{:S(2)}, u32[]{:S(2)}) collective-permute-start(bf16[112,128]{1,0:T(8,128)(2,1)S(1)} %get-tuple-element.30), channel_id=1, source_target_pairs={{0,4},{2,6},{4,0},{6,2},{1,5},{3,7},{5,1},{7,3},{8,12},{10,14},{12... | collective-permute-start | bytes 86024 | tf_op jit(solution)/shard_map/ppermute | solution.py:427
  48.6 4.3 %collective-permute-start.6 = (bf16[112,128]{1,0:T(8,128)(2,1)S(1)}, bf16[112,128]{1,0:T(8,128)(2,1)S(1)}, u32[]{:S(2)}, u32[]{:S(2)}) collective-permute-start(bf16[112,128]{1,0:T(8,128)(2,1)S(1)} %get-tuple-element.31), channel_id=1, source_target_pairs={{0,6},{2,0},{4,2},{6,4},{1,7},{3,1},{5,3},{7,5},{8,14},{10,8},{12,... | collective-permute-start | bytes 86024 | tf_op jit(solution)/shard_map/ppermute | solution.py:427
  72.9 2.6 %copy-start.2 = (bf16[112,8192]{1,0:T(8,128)(2,1)S(1)}, bf16[112,8192]{1,0:T(8,128)(2,1)}, u32[]{:S(2)}) copy-start(bf16[112,8192]{1,0:T(8,128)(2,1)} %own_ref) | copy-start | bytes 5505028
  74.1 1.4 %collective-permute-start.7 = (f32[232,128]{1,0:T(8,128)S(1)}, f32[232,128]{1,0:T(8,128)S(1)}, u32[]{:S(2)}, u32[]{:S(2)}) collective-permute-start(f32[232,128]{1,0:T(8,128)S(1)} %widen.1.mine_ref), channel_id=1, source_target_pairs={{0,1},{1,0},{2,3},{3,2},{4,5},{5,4},{6,7},{7,6},{8,9},{9,8},{10,11... | collective-permute-start | bytes 356360 | tf_op jit(solution)/shard_map/ppermute | solution.py:398

commit v5 on v4

--- a/solution.py
+++ b/solution.py
@@ -298,7 +298,7 @@
     )(mixed, gain, *weights)
 
 
-def narrow(mine_ref, theirs_ref, own_ref, other_ref, out_ref):
+def narrow(mine_ref, theirs_ref, own_ref, other_ref, *out_refs):
     core = lax.axis_index("c")
     units = own_ref.shape[0]
     total = mine_ref[...] + pltpu.roll(theirs_ref[...], TOKENS, 1)
@@ -307,75 +307,64 @@
     upward = total[units : 2 * units] * scale
     hidden = jnp.transpose(gate / (1.0 + jnp.exp(-gate)) * upward)
     hidden = jnp.concatenate([hidden[:TOKENS], hidden[TOKENS:]], axis=1).astype(BF16)
-    spot = lanes((TOKENS, HD)) // 32
+    spot = lanes((DRAFTS, HD)) // 32
     masks = [spot == (core + i) % 4 for i in range(4)]
-    for y in range(4):
-        for z_high in range(2):
-            tiles = [None] * 4
-            for z_low in range(4):
-                k = (z_high * 4 + z_low) * 4 + y
-                weight = jnp.concatenate(
-                    [ref[:, k * 256 : (k + 1) * 256] for ref in (own_ref, other_ref)], axis=0
-                )
-                terms = nn(hidden, weight)
-                for half in range(2):
-                    part = terms[:, half * HD : (half + 1) * HD]
-                    if z_low:
-                        part = pltpu.roll(part, z_low * 32, 1)
-                    for odd in range(2):
-                        x = 2 * half + odd
-                        mask = masks[(2 * odd + z_low) % 4]
-                        tiles[x] = jnp.where(mask, part, tiles[x]) if z_low else part
-            for x in range(4):
-                out_ref[y * 4 + x, z_high * TOKENS : (z_high + 1) * TOKENS, :] = tiles[x].astype(
-                    BF16
-                )
+    here = [(lax.axis_index("x") + s) % 4 for s in range(4)]
+    for k in range(KV):
+        weight = jnp.concatenate(
+            [ref[:, k * 256 : (k + 1) * 256] for ref in (own_ref, other_ref)], axis=0
+        )
+        terms = nn(hidden, weight)
+        tiles = []
+        for half in range(2):
+            part = terms[:, half * HD : (half + 1) * HD]
+            pair_tiles = [part[:DRAFTS], part[:DRAFTS]]
+            for a in range(1, 4):
+                rows = pltpu.roll(part[a * DRAFTS : (a + 1) * DRAFTS], a * 32, 1)
+                for odd in range(2):
+                    pair_tiles[odd] = jnp.where(masks[(2 * odd + a) % 4], rows, pair_tiles[odd])
+            tiles.extend(pair_tiles)
+        for s in range(4):
+            low = jnp.where(here[s] == 0, tiles[0], tiles[1])
+            high = jnp.where(here[s] == 2, tiles[2], tiles[3])
+            out_refs[s][k] = jnp.where(here[s] < 2, low, high).astype(BF16)
 
 
 def narrowed(mine, theirs, own, other):
     return pl.pallas_call(
         narrow,
         in_specs=[VMEM] * 4,
-        out_specs=VMEM,
-        out_shape=jax.ShapeDtypeStruct((16, 2 * TOKENS, HD), BF16),
+        out_specs=[VMEM] * 4,
+        out_shape=[jax.ShapeDtypeStruct((KV, DRAFTS, HD), BF16)] * 4,
         compiler_params=pltpu.CompilerParams(vmem_limit_bytes=16 * MIB),
         name="narrow",
     )(mine, theirs, own, other)
 
 
-def partial_sum(in_ref, out_ref):
-    total = in_ref[0].astype(F32)
-    for k in range(1, 16):
-        total = total + in_ref[k].astype(F32)
+def partial_sum(*refs):
+    total = (refs[0][...].astype(F32) + refs[1][...].astype(F32)) + (
+        refs[2][...].astype(F32) + refs[3][...].astype(F32)
+    )
+    refs[4][...] = total.astype(BF16)
+
+
+def summed(parts):
+    return pl.pallas_call(
+        partial_sum,
+        in_specs=[VMEM] * 4,
+        out_specs=VMEM,
+        out_shape=jax.ShapeDtypeStruct((KV, DRAFTS, HD), BF16),
+        compiler_params=pltpu.CompilerParams(vmem_limit_bytes=8 * MIB),
+        name="partial_sum",
+    )(*parts)
+
+
+def finish(parts_ref, mixed_ref, out_ref):
+    total = parts_ref[0].astype(F32) + mixed_ref[...].astype(F32)
+    for k in range(1, KV):
+        total = total + parts_ref[k].astype(F32)
     shift = lax.axis_index("x") * 2 + lax.axis_index("c")
     total = pltpu.roll(total, (8 - shift) % 4 * 32, 1)
-    lane = lanes((16, HD))
-    for z in range(8):
-        packed = None
-        for a in range(4):
-            start = z // 4 * TOKENS + a * 16
-            part = pltpu.roll(total[start : start + 16], (a - z % 4) % 4 * 32, 1)
-            packed = part if a == 0 else jnp.where(lane >= a * 32, part, packed)
-        out_ref[z] = packed.astype(BF16)
-
-
-def summed(parts):
-    return pl.pallas_call(
-        partial_sum,
-        in_specs=[VMEM],
-        out_specs=VMEM,
-        out_shape=jax.ShapeDtypeStruct((8, 16, HD), BF16),
-        compiler_params=pltpu.CompilerParams(vmem_limit_bytes=16 * MIB),
-        name="partial_sum",
-    )(parts)
-
-
-def finish(parts_ref, mixed_ref, out_ref):
-    total = parts_ref[0].astype(F32)
-    for z in range(1, 8):
-        total = total + parts_ref[z].astype(F32)
-    shift = lax.axis_index("x") * 2 + lax.axis_index("c")
-    total = total + pltpu.roll(mixed_ref[...].astype(F32), (8 - shift) % 4 * 32, 1)
     tall = jnp.concatenate([pltpu.roll(total, (4 - a) % 4 * 32, 1) for a in range(4)], axis=0)
     out_ref[...] = jnp.transpose(tall)[:32].astype(BF16)
 
@@ -396,6 +385,13 @@
 
 def trade(part):
     return lax.ppermute(part, "c", SWAP)
+
+
+def around(parts):
+    return [parts[0]] + [
+        lax.ppermute(part, "x", [(i, (i + s) % 4) for i in range(4)])
+        for s, part in enumerate(parts[1:], 1)
+    ]
 
 
 def exchange(parts, axes):
@@ -416,22 +412,18 @@
 ):
     weights = [gate_weight.T, up_weight.T]
     parts = attention(lengths, norm_gain, queries, cache_keys, cache_values)
-    parts, weights, down_weight = lax.optimization_barrier((parts, weights, down_weight))
-    weights = weights + [trade(weight) for weight in weights]
+    parts, down_weight = lax.optimization_barrier((parts, down_weight))
     other_down = trade(down_weight)
     attn, gain = combined(exchange(parts, ("z", "y")))
     attn = exchange(attn, ("z", "y"))
-    own, other = projected(attn, out_weight, residual_in.T, gain, weights[2:] + [other_down])
-    parts = list(paired(own, trade(other)))
-    parts[1:] = [
-        lax.ppermute(part, "x", [(i, (i + s) % 4) for i in range(4)])
-        for s, part in enumerate(parts[1:], 1)
-    ]
-    spread, mixed, gain = mixing(parts, [])
+    own, other = projected(attn, out_weight, residual_in.T, gain, [])
+    parts = paired(own, trade(other))
+    parts, weights = lax.optimization_barrier((parts, weights))
+    weights = weights + [trade(weight) for weight in weights]
+    spread, mixed, gain = mixing(around(parts), [])
     sums = widened(exchange(spread, ("z", "y")), gain, weights)
-    terms = narrowed(sums, trade(sums), down_weight, other_down)
-    terms = summed(exchange(terms, ("y", "x")))
-    return finished(exchange(terms, "z"), mixed).T
+    terms = summed(around(narrowed(sums, trade(sums), down_weight, other_down)))
+    return finished(exchange(terms, ("z", "y")), mixed).T
 
 
 def solution(mesh):

time: 106 us -> 104 us (0.981)
  blocking collectives: 85.6 us -> 72 us
  waiting for transfers between devices: 4.64 us -> 11.3 us
  starting transfers between devices: 5.7 us -> 11 us
    all_to_all x5 -> x4, blocking collectives: 85.6 us -> 72 us  [exchange(): return lax.all_to_all(parts, axes, 0, 0, tiled=True)]
    ppermute x3 -> x6, waiting for transfers between devices: 2.11 us -> 8.74 us  [around(): lax.ppermute(part, 'x', [(i, (i + s) % 4) for i in range(4)])]
    ppermute x3 -> x6, starting transfers between devices: 4.83 us -> 10 us  [around(): lax.ppermute(part, 'x', [(i, (i + s) % 4) for i in range(4)])]
  transfers between devices with their start and end apart: 8 -> 11, of which waited for: 3 -> 7; matrix products, arithmetic and copies ran while one was open for 0% -> 0% of each run, Pallas kernels for 0% -> 1%
where the time goes in v5:
time: 104 us
  blocking collectives  72 us (69%)
  waiting for transfers between devices  11.3 us (11%)
  starting transfers between devices  11 us (11%)
  Pallas kernels  9.16 us (9%)
    all_to_all x4, blocking collectives, exchange(): return lax.all_to_all(parts, axes, 0, 0, tiled=True)  72 us
    ppermute x6, starting transfers between devices, around(): lax.ppermute(part, 'x', [(i, (i + s) % 4) for i in range(4)])  10 us
    ppermute x6, waiting for transfers between devices, around(): lax.ppermute(part, 'x', [(i, (i + s) % 4) for i in range(4)])  8.74 us
    pallas_call x1, Pallas kernels, attention(): pl.pallas_call(attend, in_specs=[SMEM, VMEM, held, held, held], out_specs...  5.11 us
    ppermute x5, waiting for transfers between devices, trade(): return lax.ppermute(part, 'c', SWAP)  2.52 us
  transfers between devices with their start and end apart: 11, of which 7 were waited for; matrix products, arithmetic and copies ran while one was open for 0% of the time, Pallas kernels for 1%

profile of v5, /device:TPU:2, one launch (start us, length us, event | category | flops | bytes accessed | tf_op | source)
XLA Modules:
  0.0 103.6 jit_solution(14653894379622205659)
XLA Ops:
  0.0 5.1 %attention.1 = bf16[32,24,128]{2,1,0:T(8,128)(2,1)} custom-call(s32[4]{0:T(128)} %lengths_ref.1, bf16[32]{0:T(256)(128)(2,1)} %gain_ref.1, bf16[4,16,1024]{2,1,0:T(8,128)(2,1)} %queries_ref.1, bf16[4,2048,128]{2,1,0:T(8,128)(2,1)} %keys_ref.1, bf16[4,2048,128]{2,1,0:T(8,128)(2,1)} %values_ref.1), custom_call_target="tpu_custom_call" | custom-call | tf_op jit(solution)/shard_map/attention/pallas_call | solution.py:108
  5.1 23.2 %all_to_all.20.in_ref = bf16[32,24,128]{2,1,0:T(8,128)(2,1)S(1)} all-to-all(bf16[32,24,128]{2,1,0:T(8,128)(2,1)} %attention.1), channel_id=1, replica_groups=mesh['z'=8,'y'=4,'x'=4,'c'=2] {'z','y'}, dimensions={0} | all-to-all | bytes 393216 | tf_op jit(solution)/shard_map/all_to_all | solution.py:398
  28.3 0.0 copy-start.3
  28.3 0.0 copy-start.4
  28.3 0.0 copy-start.2
  28.3 0.3 combine.1
  28.7 14.2 %all_to_all.21.attn_ref = bf16[32,16,128]{2,1,0:T(8,128)(2,1)S(1)} all-to-all(bf16[32,16,128]{2,1,0:T(8,128)(2,1)S(1)} %get-tuple-element.29), channel_id=1, replica_groups=mesh['z'=8,'y'=4,'x'=4,'c'=2] {'z','y'}, dimensions={0} | all-to-all | bytes 262144 | tf_op jit(solution)/shard_map/all_to_all | solution.py:398
  42.9 0.0 copy-done.3
  42.9 0.0 copy-done.4
  42.9 0.0 copy-start
  42.9 0.0 copy-start.1
  42.9 0.3 project.1
  43.3 0.1 collective-permute-start
  43.4 1.2 %collective-permute-done.other_ref = bf16[160,128]{1,0:T(8,128)(2,1)S(1)} collective-permute-done((bf16[160,128]{1,0:T(8,128)(2,1)S(1)}, bf16[160,128]{1,0:T(8,128)(2,1)S(1)}, u32[]{:S(2)}, u32[]{:S(2)}) %collective-permute-start) | collective-permute-done | bytes 40992 | tf_op jit(solution)/shard_map/ppermute | solution.py:387
  44.6 0.0 copy-done
  44.6 0.2 collective-permute-start.4
  44.8 0.1 copy-done.1
  45.0 0.2 collective-permute-start.5
  45.2 0.0 copy-done.2
  45.2 0.3 collective-permute-start.7
  45.5 1.5 %collective-permute-start.1 = (bf16[112,128]{1,0:T(8,128)(2,1)S(1)}, bf16[112,128]{1,0:T(8,128)(2,1)S(1)}, u32[]{:S(2)}, u32[]{:S(2)}) collective-permute-start(bf16[112,128]{1,0:T(8,128)(2,1)S(1)} %get-tuple-element.38), channel_id=1, source_target_pairs={{0,2},{2,4},{4,6},{6,0},{1,3},{3,5},{5,7},{7,1},{8,10},{10,12},{12... | collective-permute-start | bytes 86024 | tf_op jit(solution)/shard_map/ppermute | solution.py:392
  47.0 1.1 %collective-permute-start.2 = (bf16[112,128]{1,0:T(8,128)(2,1)S(1)}, bf16[112,128]{1,0:T(8,128)(2,1)S(1)}, u32[]{:S(2)}, u32[]{:S(2)}) collective-permute-start(bf16[112,128]{1,0:T(8,128)(2,1)S(1)} %get-tuple-element.39), channel_id=1, source_target_pairs={{0,4},{2,6},{4,0},{6,2},{1,5},{3,7},{5,1},{7,3},{8,12},{10,14},{12... | collective-permute-start | bytes 86024 | tf_op jit(solution)/shard_map/ppermute | solution.py:392
  48.1 1.3 %collective-permute-done.1.refs_1_ = bf16[112,128]{1,0:T(8,128)(2,1)S(1)} collective-permute-done((bf16[112,128]{1,0:T(8,128)(2,1)S(1)}, bf16[112,128]{1,0:T(8,128)(2,1)S(1)}, u32[]{:S(2)}, u32[]{:S(2)}) %collective-permute-start.1) | collective-permute-done | bytes 28704 | tf_op jit(solution)/shard_map/ppermute | solution.py:392
  49.3 1.7 %collective-permute-start.3 = (bf16[112,128]{1,0:T(8,128)(2,1)S(1)}, bf16[112,128]{1,0:T(8,128)(2,1)S(1)}, u32[]{:S(2)}, u32[]{:S(2)}) collective-permute-start(bf16[112,128]{1,0:T(8,128)(2,1)S(1)} %get-tuple-element.40), channel_id=1, source_target_pairs={{0,6},{2,0},{4,2},{6,4},{1,7},{3,1},{5,3},{7,5},{8,14},{10,8},{12,... | collective-permute-start | bytes 86024 | tf_op jit(solution)/shard_map/ppermute | solution.py:392
  51.1 1.5 %collective-permute-done.2.refs_2_ = bf16[112,128]{1,0:T(8,128)(2,1)S(1)} collective-permute-done((bf16[112,128]{1,0:T(8,128)(2,1)S(1)}, bf16[112,128]{1,0:T(8,128)(2,1)S(1)}, u32[]{:S(2)}, u32[]{:S(2)}) %collective-permute-start.2) | collective-permute-done | bytes 28704 | tf_op jit(solution)/shard_map/ppermute | solution.py:392
  52.6 0.6 collective-permute-done.3.refs_3_
  53.2 0.1 mix.1
  53.3 19.8 %all_to_all.22.mixed_ref = bf16[32,64,128]{2,1,0:T(8,128)(2,1)S(1)} all-to-all(bf16[32,64,128]{2,1,0:T(8,128)(2,1)S(1)} %get-tuple-element.41), channel_id=1, replica_groups=mesh['z'=8,'y'=4,'x'=4,'c'=2] {'z','y'}, dimensions={0} | all-to-all | bytes 1048576 | tf_op jit(solution)/shard_map/all_to_all | solution.py:398
  73.0 0.0 collective-permute-done.4.refs_2_
  73.0 0.0 collective-permute-done.5.refs_3_
  73.0 1.2 %widen.1.mine_ref = f32[232,128]{1,0:T(8,128)S(1)} custom-call(bf16[32,64,128]{2,1,0:T(8,128)(2,1)S(1)} %all_to_all.22.mixed_ref, f32[32,128]{1,0:T(8,128)S(1)} %get-tuple-element.42.gain_ref, bf16[112,8192]{1,0:T(8,128)(2,1)S(1)} %bitcast.5, bf16[112,8192]{1,0:T(8,128)(2,1)S(1)} %bitcast.7, bf16[112,8192]{1,0:T(8,128)(2,1)S(1)} %collective-permute-done.4.refs_2_, ...), custom_call_target="tpu_custom_call" | custom-call | tf_op jit(solution)/shard_map/widen/pallas_call | solution.py:291
  74.3 0.1 collective-permute-start.6
  74.4 0.0 collective-permute-done.7.other_ref
  74.4 1.3 %collective-permute-done.6.theirs_ref = f32[232,128]{1,0:T(8,128)S(1)} collective-permute-done((f32[232,128]{1,0:T(8,128)S(1)}, f32[232,128]{1,0:T(8,128)S(1)}, u32[]{:S(2)}, u32[]{:S(2)}) %collective-permute-start.6) | collective-permute-done | bytes 118816 | tf_op jit(solution)/shard_map/ppermute | solution.py:387
  75.7 1.2 %narrow.1 = (bf16[32,16,128]{2,1,0:T(8,128)(2,1)S(1)}, bf16[32,16,128]{2,1,0:T(8,128)(2,1)S(1)}, bf16[32,16,128]{2,1,0:T(8,128)(2,1)S(1)}, bf16[32,16,128]{2,1,0:T(8,128)(2,1)S(1)}) custom-call(f32[232,128]{1,0:T(8,128)S(1)} %widen.1.mine_ref, f32[232,128]{1,0:T(8,128)S(1)} %collective-permute-done.6.theirs_ref, bf16[112,8192]{1,0:T(8,128)(2,1)S(1)} %copy-done.2, ...), custom_call_target="tpu_custom_call" | custom-call | tf_op jit(solution)/shard_map/narrow/pallas_call | solution.py:334
  76.9 1.4 %collective-permute-start.8 = (bf16[32,16,128]{2,1,0:T(8,128)(2,1)S(1)}, bf16[32,16,128]{2,1,0:T(8,128)(2,1)S(1)}, u32[]{:S(2)}, u32[]{:S(2)}) collective-permute-start(bf16[32,16,128]{2,1,0:T(8,128)(2,1)S(1)} %get-tuple-element.47), channel_id=1, source_target_pairs={{0,2},{2,4},{4,6},{6,0},{1,3},{3,5},{5,7},{7,1},{8,10},{10,12},{12... | collective-permute-start | bytes 393224 | tf_op jit(solution)/shard_map/ppermute | solution.py:392
  78.3 2.2 %collective-permute-start.9 = (bf16[32,16,128]{2,1,0:T(8,128)(2,1)S(1)}, bf16[32,16,128]{2,1,0:T(8,128)(2,1)S(1)}, u32[]{:S(2)}, u32[]{:S(2)}) collective-permute-start(bf16[32,16,128]{2,1,0:T(8,128)(2,1)S(1)} %get-tuple-element.48), channel_id=1, source_target_pairs={{0,4},{2,6},{4,0},{6,2},{1,5},{3,7},{5,1},{7,3},{8,12},{10,14},{12... | collective-permute-start | bytes 393224 | tf_op jit(solution)/shard_map/ppermute | solution.py:392
  80.5 2.1 %collective-permute-start.10 = (bf16[32,16,128]{2,1,0:T(8,128)(2,1)S(1)}, bf16[32,16,128]{2,1,0:T(8,128)(2,1)S(1)}, u32[]{:S(2)}, u32[]{:S(2)}) collective-permute-start(bf16[32,16,128]{2,1,0:T(8,128)(2,1)S(1)} %get-tuple-element.49), channel_id=1, source_target_pairs={{0,6},{2,0},{4,2},{6,4},{1,7},{3,1},{5,3},{7,5},{8,14},{10,8},{12,... | collective-permute-start | bytes 393224 | tf_op jit(solution)/shard_map/ppermute | solution.py:392
  82.6 0.0 collective-permute-done.8.refs_1_
  82.6 3.6 %collective-permute-done.9.refs_2_ = bf16[32,16,128]{2,1,0:T(8,128)(2,1)S(1)} collective-permute-done((bf16[32,16,128]{2,1,0:T(8,128)(2,1)S(1)}, bf16[32,16,128]{2,1,0:T(8,128)(2,1)S(1)}, u32[]{:S(2)}, u32[]{:S(2)}) %collective-permute-start.9) | collective-permute-done | bytes 131104 | tf_op jit(solution)/shard_map/ppermute | solution.py:392
  86.2 1.7 %collective-permute-done.10.refs_3_ = bf16[32,16,128]{2,1,0:T(8,128)(2,1)S(1)} collective-permute-done((bf16[32,16,128]{2,1,0:T(8,128)(2,1)S(1)}, bf16[32,16,128]{2,1,0:T(8,128)(2,1)S(1)}, u32[]{:S(2)}, u32[]{:S(2)}) %collective-permute-start.10) | collective-permute-done | bytes 131104 | tf_op jit(solution)/shard_map/ppermute | solution.py:392
  87.9 0.1 partial_sum.1
  88.0 14.8 %all_to_all.23.parts_ref = bf16[32,16,128]{2,1,0:T(8,128)(2,1)S(1)} all-to-all(bf16[32,16,128]{2,1,0:T(8,128)(2,1)S(1)} %partial_sum.1), channel_id=1, replica_groups=mesh['z'=8,'y'=4,'x'=4,'c'=2] {'z','y'}, dimensions={0} | all-to-all | bytes 262144 | tf_op jit(solution)/shard_map/all_to_all | solution.py:398
  102.8 0.8 finish.1
  (1 shorter events, 0.0 us)
Async XLA Ops:
  28.3 14.6 %copy-start.3 = (bf16[1024,256]{1,0:T(8,128)(2,1)S(1)}, bf16[1024,256]{1,0:T(8,128)(2,1)}, u32[]{:S(2)}) copy-start(bf16[1024,256]{1,0:T(8,128)(2,1)} %weight_ref.1) | copy-start | bytes 1572868
  28.3 14.6 %copy-start.4 = (bf16[64,32]{0,1:T(8,128)(2,1)S(1)}, bf16[64,32]{0,1:T(8,128)(2,1)}, u32[]{:S(2)}) copy-start(bf16[64,32]{0,1:T(8,128)(2,1)} %param.14) | copy-start | bytes 12292
  28.3 16.9 %copy-start.2 = (bf16[112,8192]{1,0:T(8,128)(2,1)S(1)}, bf16[112,8192]{1,0:T(8,128)(2,1)}, u32[]{:S(2)}) copy-start(bf16[112,8192]{1,0:T(8,128)(2,1)} %own_ref) | copy-start | bytes 5505028
  42.9 1.7 %copy-start = (bf16[8192,112]{0,1:T(8,128)(2,1)S(1)}, bf16[8192,112]{0,1:T(8,128)(2,1)}, u32[]{:S(2)}) copy-start(bf16[8192,112]{0,1:T(8,128)(2,1)} %param.17) | copy-start | bytes 5505028
  42.9 2.1 %copy-start.1 = (bf16[8192,112]{0,1:T(8,128)(2,1)S(1)}, bf16[8192,112]{0,1:T(8,128)(2,1)}, u32[]{:S(2)}) copy-start(bf16[8192,112]{0,1:T(8,128)(2,1)} %param.18) | copy-start | bytes 5505028
  43.3 1.3 %collective-permute-start = (bf16[160,128]{1,0:T(8,128)(2,1)S(1)}, bf16[160,128]{1,0:T(8,128)(2,1)S(1)}, u32[]{:S(2)}, u32[]{:S(2)}) collective-permute-start(bf16[160,128]{1,0:T(8,128)(2,1)S(1)} %get-tuple-element.32), channel_id=1, source_target_pairs={{0,1},{1,0},{2,3},{3,2},{4,5},{5,4},{6,7},{7,6},{8,9},{9,8},{10,11... | collective-permute-start | bytes 122888 | tf_op jit(solution)/shard_map/ppermute | solution.py:387
  44.6 28.4 %collective-permute-start.4 = (bf16[112,8192]{1,0:T(8,128)(2,1)S(1)}, bf16[112,8192]{1,0:T(8,128)(2,1)S(1)}, u32[]{:S(2)}, u32[]{:S(2)}) collective-permute-start(bf16[112,8192]{1,0:T(8,128)(2,1)S(1)} %bitcast.4), channel_id=1, source_target_pairs={{0,1},{1,0},{2,3},{3,2},{4,5},{5,4},{6,7},{7,6},{8,9},{9,8},{10,11... | collective-permute-start | bytes 5505032 | tf_op jit(solution)/shard_map/ppermute | solution.py:387
  45.0 28.1 %collective-permute-start.5 = (bf16[112,8192]{1,0:T(8,128)(2,1)S(1)}, bf16[112,8192]{1,0:T(8,128)(2,1)S(1)}, u32[]{:S(2)}, u32[]{:S(2)}) collective-permute-start(bf16[112,8192]{1,0:T(8,128)(2,1)S(1)} %bitcast.6), channel_id=1, source_target_pairs={{0,1},{1,0},{2,3},{3,2},{4,5},{5,4},{6,7},{7,6},{8,9},{9,8},{10,11... | collective-permute-start | bytes 5505032 | tf_op jit(solution)/shard_map/ppermute | solution.py:387
  45.2 29.2 %collective-permute-start.7 = (bf16[112,8192]{1,0:T(8,128)(2,1)S(1)}, bf16[112,8192]{1,0:T(8,128)(2,1)S(1)}, u32[]{:S(2)}, u32[]{:S(2)}) collective-permute-start(bf16[112,8192]{1,0:T(8,128)(2,1)S(1)} %copy-done.2), channel_id=1, source_target_pairs={{0,1},{1,0},{2,3},{3,2},{4,5},{5,4},{6,7},{7,6},{8,9},{9,8},{10,11... | collective-permute-start | bytes 5505032 | tf_op jit(solution)/shard_map/ppermute | solution.py:387
  45.5 3.9 %collective-permute-start.1 = (bf16[112,128]{1,0:T(8,128)(2,1)S(1)}, bf16[112,128]{1,0:T(8,128)(2,1)S(1)}, u32[]{:S(2)}, u32[]{:S(2)}) collective-permute-start(bf16[112,128]{1,0:T(8,128)(2,1)S(1)} %get-tuple-element.38), channel_id=1, source_target_pairs={{0,2},{2,4},{4,6},{6,0},{1,3},{3,5},{5,7},{7,1},{8,10},{10,12},{12... | collective-permute-start | bytes 86024 | tf_op jit(solution)/shard_map/ppermute | solution.py:392
  47.0 5.6 %collective-permute-start.2 = (bf16[112,128]{1,0:T(8,128)(2,1)S(1)}, bf16[112,128]{1,0:T(8,128)(2,1)S(1)}, u32[]{:S(2)}, u32[]{:S(2)}) collective-permute-start(bf16[112,128]{1,0:T(8,128)(2,1)S(1)} %get-tuple-element.39), channel_id=1, source_target_pairs={{0,4},{2,6},{4,0},{6,2},{1,5},{3,7},{5,1},{7,3},{8,12},{10,14},{12... | collective-permute-start | bytes 86024 | tf_op jit(solution)/shard_map/ppermute | solution.py:392
  49.3 3.9 %collective-permute-start.3 = (bf16[112,128]{1,0:T(8,128)(2,1)S(1)}, bf16[112,128]{1,0:T(8,128)(2,1)S(1)}, u32[]{:S(2)}, u32[]{:S(2)}) collective-permute-start(bf16[112,128]{1,0:T(8,128)(2,1)S(1)} %get-tuple-element.40), channel_id=1, source_target_pairs={{0,6},{2,0},{4,2},{6,4},{1,7},{3,1},{5,3},{7,5},{8,14},{10,8},{12,... | collective-permute-start | bytes 86024 | tf_op jit(solution)/shard_map/ppermute | solution.py:392
  74.3 1.4 %collective-permute-start.6 = (f32[232,128]{1,0:T(8,128)S(1)}, f32[232,128]{1,0:T(8,128)S(1)}, u32[]{:S(2)}, u32[]{:S(2)}) collective-permute-start(f32[232,128]{1,0:T(8,128)S(1)} %widen.1.mine_ref), channel_id=1, source_target_pairs={{0,1},{1,0},{2,3},{3,2},{4,5},{5,4},{6,7},{7,6},{8,9},{9,8},{10,11... | collective-permute-start | bytes 356360 | tf_op jit(solution)/shard_map/ppermute | solution.py:387
  76.9 5.7 %collective-permute-start.8 = (bf16[32,16,128]{2,1,0:T(8,128)(2,1)S(1)}, bf16[32,16,128]{2,1,0:T(8,128)(2,1)S(1)}, u32[]{:S(2)}, u32[]{:S(2)}) collective-permute-start(bf16[32,16,128]{2,1,0:T(8,128)(2,1)S(1)} %get-tuple-element.47), channel_id=1, source_target_pairs={{0,2},{2,4},{4,6},{6,0},{1,3},{3,5},{5,7},{7,1},{8,10},{10,12},{12... | collective-permute-start | bytes 393224 | tf_op jit(solution)/shard_map/ppermute | solution.py:392
  78.3 7.9 %collective-permute-start.9 = (bf16[32,16,128]{2,1,0:T(8,128)(2,1)S(1)}, bf16[32,16,128]{2,1,0:T(8,128)(2,1)S(1)}, u32[]{:S(2)}, u32[]{:S(2)}) collective-permute-start(bf16[32,16,128]{2,1,0:T(8,128)(2,1)S(1)} %get-tuple-element.48), channel_id=1, source_target_pairs={{0,4},{2,6},{4,0},{6,2},{1,5},{3,7},{5,1},{7,3},{8,12},{10,14},{12... | collective-permute-start | bytes 393224 | tf_op jit(solution)/shard_map/ppermute | solution.py:392
  80.5 7.4 %collective-permute-start.10 = (bf16[32,16,128]{2,1,0:T(8,128)(2,1)S(1)}, bf16[32,16,128]{2,1,0:T(8,128)(2,1)S(1)}, u32[]{:S(2)}, u32[]{:S(2)}) collective-permute-start(bf16[32,16,128]{2,1,0:T(8,128)(2,1)S(1)} %get-tuple-element.49), channel_id=1, source_target_pairs={{0,6},{2,0},{4,2},{6,4},{1,7},{3,1},{5,3},{7,5},{8,14},{10,8},{12,... | collective-permute-start | bytes 393224 | tf_op jit(solution)/shard_map/ppermute | solution.py:392

commit v6 on v5

--- a/solution.py
+++ b/solution.py
@@ -117,7 +117,7 @@
             pltpu.VMEM((2, GROUP * DRAFTS, SLICE), F32),
             pltpu.SemaphoreType.DMA((2, 3)),
         ],
-        compiler_params=pltpu.CompilerParams(vmem_limit_bytes=57 * MIB),
+        compiler_params=pltpu.CompilerParams(vmem_limit_bytes=61 * MIB),
         name="attention",
     )(lengths, gain, queries, keys, values)
 

time: 104 us -> 104 us (level)
  no operation moved by 1% of the time
where the time goes in v6:
time: 104 us
  blocking collectives  72 us (69%)
  waiting for transfers between devices  11.3 us (11%)
  starting transfers between devices  11 us (11%)
  Pallas kernels  9.16 us (9%)
    all_to_all x4, blocking collectives, exchange(): return lax.all_to_all(parts, axes, 0, 0, tiled=True)  72 us
    ppermute x6, starting transfers between devices, around(): lax.ppermute(part, 'x', [(i, (i + s) % 4) for i in range(4)])  10 us
    ppermute x6, waiting for transfers between devices, around(): lax.ppermute(part, 'x', [(i, (i + s) % 4) for i in range(4)])  8.74 us
    pallas_call x1, Pallas kernels, attention(): pl.pallas_call(attend, in_specs=[SMEM, VMEM, held, held, held], out_specs...  5.11 us
    ppermute x5, waiting for transfers between devices, trade(): return lax.ppermute(part, 'c', SWAP)  2.52 us
  transfers between devices with their start and end apart: 11, of which 7 were waited for; matrix products, arithmetic and copies ran while one was open for 0% of the time, Pallas kernels for 1%

profile of v6, /device:TPU:2, one launch (start us, length us, event | category | flops | bytes accessed | tf_op | source)
XLA Modules:
  0.0 103.6 jit_solution(14653894379622205659)
XLA Ops:
  0.0 5.1 %attention.1 = bf16[32,24,128]{2,1,0:T(8,128)(2,1)} custom-call(s32[4]{0:T(128)} %lengths_ref.1, bf16[32]{0:T(256)(128)(2,1)} %gain_ref.1, bf16[4,16,1024]{2,1,0:T(8,128)(2,1)} %queries_ref.1, bf16[4,2048,128]{2,1,0:T(8,128)(2,1)} %keys_ref.1, bf16[4,2048,128]{2,1,0:T(8,128)(2,1)} %values_ref.1), custom_call_target="tpu_custom_call" | custom-call | tf_op jit(solution)/shard_map/attention/pallas_call | solution.py:108
  5.1 23.2 %all_to_all.20.in_ref = bf16[32,24,128]{2,1,0:T(8,128)(2,1)S(1)} all-to-all(bf16[32,24,128]{2,1,0:T(8,128)(2,1)} %attention.1), channel_id=1, replica_groups=mesh['z'=8,'y'=4,'x'=4,'c'=2] {'z','y'}, dimensions={0} | all-to-all | bytes 393216 | tf_op jit(solution)/shard_map/all_to_all | solution.py:398
  28.3 0.0 copy-start.3
  28.3 0.0 copy-start.4
  28.3 0.0 copy-start.2
  28.3 0.3 combine.1
  28.7 14.2 %all_to_all.21.attn_ref = bf16[32,16,128]{2,1,0:T(8,128)(2,1)S(1)} all-to-all(bf16[32,16,128]{2,1,0:T(8,128)(2,1)S(1)} %get-tuple-element.29), channel_id=1, replica_groups=mesh['z'=8,'y'=4,'x'=4,'c'=2] {'z','y'}, dimensions={0} | all-to-all | bytes 262144 | tf_op jit(solution)/shard_map/all_to_all | solution.py:398
  42.9 0.0 copy-done.3
  42.9 0.0 copy-done.4
  42.9 0.0 copy-start
  42.9 0.0 copy-start.1
  42.9 0.3 project.1
  43.3 0.1 collective-permute-start
  43.4 1.2 %collective-permute-done.other_ref = bf16[160,128]{1,0:T(8,128)(2,1)S(1)} collective-permute-done((bf16[160,128]{1,0:T(8,128)(2,1)S(1)}, bf16[160,128]{1,0:T(8,128)(2,1)S(1)}, u32[]{:S(2)}, u32[]{:S(2)}) %collective-permute-start) | collective-permute-done | bytes 40992 | tf_op jit(solution)/shard_map/ppermute | solution.py:387
  44.6 0.0 copy-done
  44.6 0.2 collective-permute-start.4
  44.8 0.1 copy-done.1
  45.0 0.2 collective-permute-start.5
  45.2 0.0 copy-done.2
  45.2 0.3 collective-permute-start.7
  45.5 1.5 %collective-permute-start.1 = (bf16[112,128]{1,0:T(8,128)(2,1)S(1)}, bf16[112,128]{1,0:T(8,128)(2,1)S(1)}, u32[]{:S(2)}, u32[]{:S(2)}) collective-permute-start(bf16[112,128]{1,0:T(8,128)(2,1)S(1)} %get-tuple-element.38), channel_id=1, source_target_pairs={{0,2},{2,4},{4,6},{6,0},{1,3},{3,5},{5,7},{7,1},{8,10},{10,12},{12... | collective-permute-start | bytes 86024 | tf_op jit(solution)/shard_map/ppermute | solution.py:392
  47.0 1.1 %collective-permute-start.2 = (bf16[112,128]{1,0:T(8,128)(2,1)S(1)}, bf16[112,128]{1,0:T(8,128)(2,1)S(1)}, u32[]{:S(2)}, u32[]{:S(2)}) collective-permute-start(bf16[112,128]{1,0:T(8,128)(2,1)S(1)} %get-tuple-element.39), channel_id=1, source_target_pairs={{0,4},{2,6},{4,0},{6,2},{1,5},{3,7},{5,1},{7,3},{8,12},{10,14},{12... | collective-permute-start | bytes 86024 | tf_op jit(solution)/shard_map/ppermute | solution.py:392
  48.1 1.3 %collective-permute-done.1.refs_1_ = bf16[112,128]{1,0:T(8,128)(2,1)S(1)} collective-permute-done((bf16[112,128]{1,0:T(8,128)(2,1)S(1)}, bf16[112,128]{1,0:T(8,128)(2,1)S(1)}, u32[]{:S(2)}, u32[]{:S(2)}) %collective-permute-start.1) | collective-permute-done | bytes 28704 | tf_op jit(solution)/shard_map/ppermute | solution.py:392
  49.3 1.7 %collective-permute-start.3 = (bf16[112,128]{1,0:T(8,128)(2,1)S(1)}, bf16[112,128]{1,0:T(8,128)(2,1)S(1)}, u32[]{:S(2)}, u32[]{:S(2)}) collective-permute-start(bf16[112,128]{1,0:T(8,128)(2,1)S(1)} %get-tuple-element.40), channel_id=1, source_target_pairs={{0,6},{2,0},{4,2},{6,4},{1,7},{3,1},{5,3},{7,5},{8,14},{10,8},{12,... | collective-permute-start | bytes 86024 | tf_op jit(solution)/shard_map/ppermute | solution.py:392
  51.1 1.5 %collective-permute-done.2.refs_2_ = bf16[112,128]{1,0:T(8,128)(2,1)S(1)} collective-permute-done((bf16[112,128]{1,0:T(8,128)(2,1)S(1)}, bf16[112,128]{1,0:T(8,128)(2,1)S(1)}, u32[]{:S(2)}, u32[]{:S(2)}) %collective-permute-start.2) | collective-permute-done | bytes 28704 | tf_op jit(solution)/shard_map/ppermute | solution.py:392
  52.6 0.6 collective-permute-done.3.refs_3_
  53.2 0.1 mix.1
  53.3 19.8 %all_to_all.22.mixed_ref = bf16[32,64,128]{2,1,0:T(8,128)(2,1)S(1)} all-to-all(bf16[32,64,128]{2,1,0:T(8,128)(2,1)S(1)} %get-tuple-element.41), channel_id=1, replica_groups=mesh['z'=8,'y'=4,'x'=4,'c'=2] {'z','y'}, dimensions={0} | all-to-all | bytes 1048576 | tf_op jit(solution)/shard_map/all_to_all | solution.py:398
  73.0 0.0 collective-permute-done.4.refs_2_
  73.0 0.0 collective-permute-done.5.refs_3_
  73.0 1.2 %widen.1.mine_ref = f32[232,128]{1,0:T(8,128)S(1)} custom-call(bf16[32,64,128]{2,1,0:T(8,128)(2,1)S(1)} %all_to_all.22.mixed_ref, f32[32,128]{1,0:T(8,128)S(1)} %get-tuple-element.42.gain_ref, bf16[112,8192]{1,0:T(8,128)(2,1)S(1)} %bitcast.5, bf16[112,8192]{1,0:T(8,128)(2,1)S(1)} %bitcast.7, bf16[112,8192]{1,0:T(8,128)(2,1)S(1)} %collective-permute-done.4.refs_2_, ...), custom_call_target="tpu_custom_call" | custom-call | tf_op jit(solution)/shard_map/widen/pallas_call | solution.py:291
  74.3 0.1 collective-permute-start.6
  74.4 0.0 collective-permute-done.7.other_ref
  74.4 1.3 %collective-permute-done.6.theirs_ref = f32[232,128]{1,0:T(8,128)S(1)} collective-permute-done((f32[232,128]{1,0:T(8,128)S(1)}, f32[232,128]{1,0:T(8,128)S(1)}, u32[]{:S(2)}, u32[]{:S(2)}) %collective-permute-start.6) | collective-permute-done | bytes 118816 | tf_op jit(solution)/shard_map/ppermute | solution.py:387
  75.7 1.2 %narrow.1 = (bf16[32,16,128]{2,1,0:T(8,128)(2,1)S(1)}, bf16[32,16,128]{2,1,0:T(8,128)(2,1)S(1)}, bf16[32,16,128]{2,1,0:T(8,128)(2,1)S(1)}, bf16[32,16,128]{2,1,0:T(8,128)(2,1)S(1)}) custom-call(f32[232,128]{1,0:T(8,128)S(1)} %widen.1.mine_ref, f32[232,128]{1,0:T(8,128)S(1)} %collective-permute-done.6.theirs_ref, bf16[112,8192]{1,0:T(8,128)(2,1)S(1)} %copy-done.2, ...), custom_call_target="tpu_custom_call" | custom-call | tf_op jit(solution)/shard_map/narrow/pallas_call | solution.py:334
  76.9 1.4 %collective-permute-start.8 = (bf16[32,16,128]{2,1,0:T(8,128)(2,1)S(1)}, bf16[32,16,128]{2,1,0:T(8,128)(2,1)S(1)}, u32[]{:S(2)}, u32[]{:S(2)}) collective-permute-start(bf16[32,16,128]{2,1,0:T(8,128)(2,1)S(1)} %get-tuple-element.47), channel_id=1, source_target_pairs={{0,2},{2,4},{4,6},{6,0},{1,3},{3,5},{5,7},{7,1},{8,10},{10,12},{12... | collective-permute-start | bytes 393224 | tf_op jit(solution)/shard_map/ppermute | solution.py:392
  78.3 2.2 %collective-permute-start.9 = (bf16[32,16,128]{2,1,0:T(8,128)(2,1)S(1)}, bf16[32,16,128]{2,1,0:T(8,128)(2,1)S(1)}, u32[]{:S(2)}, u32[]{:S(2)}) collective-permute-start(bf16[32,16,128]{2,1,0:T(8,128)(2,1)S(1)} %get-tuple-element.48), channel_id=1, source_target_pairs={{0,4},{2,6},{4,0},{6,2},{1,5},{3,7},{5,1},{7,3},{8,12},{10,14},{12... | collective-permute-start | bytes 393224 | tf_op jit(solution)/shard_map/ppermute | solution.py:392
  80.5 2.1 %collective-permute-start.10 = (bf16[32,16,128]{2,1,0:T(8,128)(2,1)S(1)}, bf16[32,16,128]{2,1,0:T(8,128)(2,1)S(1)}, u32[]{:S(2)}, u32[]{:S(2)}) collective-permute-start(bf16[32,16,128]{2,1,0:T(8,128)(2,1)S(1)} %get-tuple-element.49), channel_id=1, source_target_pairs={{0,6},{2,0},{4,2},{6,4},{1,7},{3,1},{5,3},{7,5},{8,14},{10,8},{12,... | collective-permute-start | bytes 393224 | tf_op jit(solution)/shard_map/ppermute | solution.py:392
  82.6 0.0 collective-permute-done.8.refs_1_
  82.6 3.6 %collective-permute-done.9.refs_2_ = bf16[32,16,128]{2,1,0:T(8,128)(2,1)S(1)} collective-permute-done((bf16[32,16,128]{2,1,0:T(8,128)(2,1)S(1)}, bf16[32,16,128]{2,1,0:T(8,128)(2,1)S(1)}, u32[]{:S(2)}, u32[]{:S(2)}) %collective-permute-start.9) | collective-permute-done | bytes 131104 | tf_op jit(solution)/shard_map/ppermute | solution.py:392
  86.2 1.7 %collective-permute-done.10.refs_3_ = bf16[32,16,128]{2,1,0:T(8,128)(2,1)S(1)} collective-permute-done((bf16[32,16,128]{2,1,0:T(8,128)(2,1)S(1)}, bf16[32,16,128]{2,1,0:T(8,128)(2,1)S(1)}, u32[]{:S(2)}, u32[]{:S(2)}) %collective-permute-start.10) | collective-permute-done | bytes 131104 | tf_op jit(solution)/shard_map/ppermute | solution.py:392
  87.9 0.1 partial_sum.1
  88.0 14.8 %all_to_all.23.parts_ref = bf16[32,16,128]{2,1,0:T(8,128)(2,1)S(1)} all-to-all(bf16[32,16,128]{2,1,0:T(8,128)(2,1)S(1)} %partial_sum.1), channel_id=1, replica_groups=mesh['z'=8,'y'=4,'x'=4,'c'=2] {'z','y'}, dimensions={0} | all-to-all | bytes 262144 | tf_op jit(solution)/shard_map/all_to_all | solution.py:398
  102.8 0.8 finish.1
  (1 shorter events, 0.0 us)
Async XLA Ops:
  28.3 14.6 %copy-start.3 = (bf16[1024,256]{1,0:T(8,128)(2,1)S(1)}, bf16[1024,256]{1,0:T(8,128)(2,1)}, u32[]{:S(2)}) copy-start(bf16[1024,256]{1,0:T(8,128)(2,1)} %weight_ref.1) | copy-start | bytes 1572868
  28.3 14.6 %copy-start.4 = (bf16[64,32]{0,1:T(8,128)(2,1)S(1)}, bf16[64,32]{0,1:T(8,128)(2,1)}, u32[]{:S(2)}) copy-start(bf16[64,32]{0,1:T(8,128)(2,1)} %param.14) | copy-start | bytes 12292
  28.3 16.9 %copy-start.2 = (bf16[112,8192]{1,0:T(8,128)(2,1)S(1)}, bf16[112,8192]{1,0:T(8,128)(2,1)}, u32[]{:S(2)}) copy-start(bf16[112,8192]{1,0:T(8,128)(2,1)} %own_ref) | copy-start | bytes 5505028
  42.9 1.7 %copy-start = (bf16[8192,112]{0,1:T(8,128)(2,1)S(1)}, bf16[8192,112]{0,1:T(8,128)(2,1)}, u32[]{:S(2)}) copy-start(bf16[8192,112]{0,1:T(8,128)(2,1)} %param.17) | copy-start | bytes 5505028
  42.9 2.1 %copy-start.1 = (bf16[8192,112]{0,1:T(8,128)(2,1)S(1)}, bf16[8192,112]{0,1:T(8,128)(2,1)}, u32[]{:S(2)}) copy-start(bf16[8192,112]{0,1:T(8,128)(2,1)} %param.18) | copy-start | bytes 5505028
  43.3 1.3 %collective-permute-start = (bf16[160,128]{1,0:T(8,128)(2,1)S(1)}, bf16[160,128]{1,0:T(8,128)(2,1)S(1)}, u32[]{:S(2)}, u32[]{:S(2)}) collective-permute-start(bf16[160,128]{1,0:T(8,128)(2,1)S(1)} %get-tuple-element.32), channel_id=1, source_target_pairs={{0,1},{1,0},{2,3},{3,2},{4,5},{5,4},{6,7},{7,6},{8,9},{9,8},{10,11... | collective-permute-start | bytes 122888 | tf_op jit(solution)/shard_map/ppermute | solution.py:387
  44.6 28.4 %collective-permute-start.4 = (bf16[112,8192]{1,0:T(8,128)(2,1)S(1)}, bf16[112,8192]{1,0:T(8,128)(2,1)S(1)}, u32[]{:S(2)}, u32[]{:S(2)}) collective-permute-start(bf16[112,8192]{1,0:T(8,128)(2,1)S(1)} %bitcast.4), channel_id=1, source_target_pairs={{0,1},{1,0},{2,3},{3,2},{4,5},{5,4},{6,7},{7,6},{8,9},{9,8},{10,11... | collective-permute-start | bytes 5505032 | tf_op jit(solution)/shard_map/ppermute | solution.py:387
  45.0 28.1 %collective-permute-start.5 = (bf16[112,8192]{1,0:T(8,128)(2,1)S(1)}, bf16[112,8192]{1,0:T(8,128)(2,1)S(1)}, u32[]{:S(2)}, u32[]{:S(2)}) collective-permute-start(bf16[112,8192]{1,0:T(8,128)(2,1)S(1)} %bitcast.6), channel_id=1, source_target_pairs={{0,1},{1,0},{2,3},{3,2},{4,5},{5,4},{6,7},{7,6},{8,9},{9,8},{10,11... | collective-permute-start | bytes 5505032 | tf_op jit(solution)/shard_map/ppermute | solution.py:387
  45.2 29.2 %collective-permute-start.7 = (bf16[112,8192]{1,0:T(8,128)(2,1)S(1)}, bf16[112,8192]{1,0:T(8,128)(2,1)S(1)}, u32[]{:S(2)}, u32[]{:S(2)}) collective-permute-start(bf16[112,8192]{1,0:T(8,128)(2,1)S(1)} %copy-done.2), channel_id=1, source_target_pairs={{0,1},{1,0},{2,3},{3,2},{4,5},{5,4},{6,7},{7,6},{8,9},{9,8},{10,11... | collective-permute-start | bytes 5505032 | tf_op jit(solution)/shard_map/ppermute | solution.py:387
  45.5 3.9 %collective-permute-start.1 = (bf16[112,128]{1,0:T(8,128)(2,1)S(1)}, bf16[112,128]{1,0:T(8,128)(2,1)S(1)}, u32[]{:S(2)}, u32[]{:S(2)}) collective-permute-start(bf16[112,128]{1,0:T(8,128)(2,1)S(1)} %get-tuple-element.38), channel_id=1, source_target_pairs={{0,2},{2,4},{4,6},{6,0},{1,3},{3,5},{5,7},{7,1},{8,10},{10,12},{12... | collective-permute-start | bytes 86024 | tf_op jit(solution)/shard_map/ppermute | solution.py:392
  47.0 5.6 %collective-permute-start.2 = (bf16[112,128]{1,0:T(8,128)(2,1)S(1)}, bf16[112,128]{1,0:T(8,128)(2,1)S(1)}, u32[]{:S(2)}, u32[]{:S(2)}) collective-permute-start(bf16[112,128]{1,0:T(8,128)(2,1)S(1)} %get-tuple-element.39), channel_id=1, source_target_pairs={{0,4},{2,6},{4,0},{6,2},{1,5},{3,7},{5,1},{7,3},{8,12},{10,14},{12... | collective-permute-start | bytes 86024 | tf_op jit(solution)/shard_map/ppermute | solution.py:392
  49.3 3.9 %collective-permute-start.3 = (bf16[112,128]{1,0:T(8,128)(2,1)S(1)}, bf16[112,128]{1,0:T(8,128)(2,1)S(1)}, u32[]{:S(2)}, u32[]{:S(2)}) collective-permute-start(bf16[112,128]{1,0:T(8,128)(2,1)S(1)} %get-tuple-element.40), channel_id=1, source_target_pairs={{0,6},{2,0},{4,2},{6,4},{1,7},{3,1},{5,3},{7,5},{8,14},{10,8},{12,... | collective-permute-start | bytes 86024 | tf_op jit(solution)/shard_map/ppermute | solution.py:392
  74.3 1.4 %collective-permute-start.6 = (f32[232,128]{1,0:T(8,128)S(1)}, f32[232,128]{1,0:T(8,128)S(1)}, u32[]{:S(2)}, u32[]{:S(2)}) collective-permute-start(f32[232,128]{1,0:T(8,128)S(1)} %widen.1.mine_ref), channel_id=1, source_target_pairs={{0,1},{1,0},{2,3},{3,2},{4,5},{5,4},{6,7},{7,6},{8,9},{9,8},{10,11... | collective-permute-start | bytes 356360 | tf_op jit(solution)/shard_map/ppermute | solution.py:387
  76.9 5.7 %collective-permute-start.8 = (bf16[32,16,128]{2,1,0:T(8,128)(2,1)S(1)}, bf16[32,16,128]{2,1,0:T(8,128)(2,1)S(1)}, u32[]{:S(2)}, u32[]{:S(2)}) collective-permute-start(bf16[32,16,128]{2,1,0:T(8,128)(2,1)S(1)} %get-tuple-element.47), channel_id=1, source_target_pairs={{0,2},{2,4},{4,6},{6,0},{1,3},{3,5},{5,7},{7,1},{8,10},{10,12},{12... | collective-permute-start | bytes 393224 | tf_op jit(solution)/shard_map/ppermute | solution.py:392
  78.3 7.9 %collective-permute-start.9 = (bf16[32,16,128]{2,1,0:T(8,128)(2,1)S(1)}, bf16[32,16,128]{2,1,0:T(8,128)(2,1)S(1)}, u32[]{:S(2)}, u32[]{:S(2)}) collective-permute-start(bf16[32,16,128]{2,1,0:T(8,128)(2,1)S(1)} %get-tuple-element.48), channel_id=1, source_target_pairs={{0,4},{2,6},{4,0},{6,2},{1,5},{3,7},{5,1},{7,3},{8,12},{10,14},{12... | collective-permute-start | bytes 393224 | tf_op jit(solution)/shard_map/ppermute | solution.py:392
  80.5 7.4 %collective-permute-start.10 = (bf16[32,16,128]{2,1,0:T(8,128)(2,1)S(1)}, bf16[32,16,128]{2,1,0:T(8,128)(2,1)S(1)}, u32[]{:S(2)}, u32[]{:S(2)}) collective-permute-start(bf16[32,16,128]{2,1,0:T(8,128)(2,1)S(1)} %get-tuple-element.49), channel_id=1, source_target_pairs={{0,6},{2,0},{4,2},{6,4},{1,7},{3,1},{5,3},{7,5},{8,14},{10,8},{12,... | collective-permute-start | bytes 393224 | tf_op jit(solution)/shard_map/ppermute | solution.py:392

commit v7 on v5

--- a/solution.py
+++ b/solution.py
@@ -309,11 +309,10 @@
     hidden = jnp.concatenate([hidden[:TOKENS], hidden[TOKENS:]], axis=1).astype(BF16)
     spot = lanes((DRAFTS, HD)) // 32
     masks = [spot == (core + i) % 4 for i in range(4)]
-    here = [(lax.axis_index("x") + s) % 4 for s in range(4)]
-    for k in range(KV):
-        weight = jnp.concatenate(
-            [ref[:, k * 256 : (k + 1) * 256] for ref in (own_ref, other_ref)], axis=0
-        )
+    for n in range(KV):
+        y = (lax.axis_index("y") + n // 8) % 4
+        at = pl.ds(pl.multiple_of((n % 8 * 4 + y) * 256, 256), 256)
+        weight = jnp.concatenate([ref[:, at] for ref in (own_ref, other_ref)], axis=0)
         terms = nn(hidden, weight)
         tiles = []
         for half in range(2):
@@ -324,10 +323,8 @@
                 for odd in range(2):
                     pair_tiles[odd] = jnp.where(masks[(2 * odd + a) % 4], rows, pair_tiles[odd])
             tiles.extend(pair_tiles)
-        for s in range(4):
-            low = jnp.where(here[s] == 0, tiles[0], tiles[1])
-            high = jnp.where(here[s] == 2, tiles[2], tiles[3])
-            out_refs[s][k] = jnp.where(here[s] < 2, low, high).astype(BF16)
+        for x in range(4):
+            out_refs[n // 8][n % 8 * 4 + x] = tiles[x].astype(BF16)
 
 
 def narrowed(mine, theirs, own, other):
@@ -387,9 +384,9 @@
     return lax.ppermute(part, "c", SWAP)
 
 
-def around(parts):
+def around(parts, axis):
     return [parts[0]] + [
-        lax.ppermute(part, "x", [(i, (i + s) % 4) for i in range(4)])
+        lax.ppermute(part, axis, [(i, (i + s) % 4) for i in range(4)])
         for s, part in enumerate(parts[1:], 1)
     ]
 
@@ -420,10 +417,10 @@
     parts = paired(own, trade(other))
     parts, weights = lax.optimization_barrier((parts, weights))
     weights = weights + [trade(weight) for weight in weights]
-    spread, mixed, gain = mixing(around(parts), [])
+    spread, mixed, gain = mixing(around(parts, "x"), [])
     sums = widened(exchange(spread, ("z", "y")), gain, weights)
-    terms = summed(around(narrowed(sums, trade(sums), down_weight, other_down)))
-    return finished(exchange(terms, ("z", "y")), mixed).T
+    terms = summed(around(narrowed(sums, trade(sums), down_weight, other_down), "y"))
+    return finished(exchange(terms, ("z", "x")), mixed).T
 
 
 def solution(mesh):

time: 104 us -> 105 us (level); the launches traced: 104 us -> 103 us
  transfers between devices with their start and end apart: 11 -> 11, of which waited for: 7 -> 8; matrix products, arithmetic and copies ran while one was open for 0% -> 0% of each run, Pallas kernels for 1% -> 1%
where the time goes in v7:
time: 105 us; the launch traced here: 103 us
  blocking collectives  72.7 us (69%)
  waiting for transfers between devices  11.4 us (11%)
  starting transfers between devices  10 us (10%)
  Pallas kernels  9.13 us (9%)
    all_to_all x4, blocking collectives, exchange(): return lax.all_to_all(parts, axes, 0, 0, tiled=True)  72.7 us
    ppermute x6, starting transfers between devices, around(): lax.ppermute(part, axis, [(i, (i + s) % 4) for i in range(4)])  9.08 us
    ppermute x6, waiting for transfers between devices, around(): lax.ppermute(part, axis, [(i, (i + s) % 4) for i in range(4)])  8.88 us
    pallas_call x1, Pallas kernels, attention(): pl.pallas_call(attend, in_specs=[SMEM, VMEM, held, held, held], out_specs...  5.11 us
    ppermute x5, waiting for transfers between devices, trade(): return lax.ppermute(part, 'c', SWAP)  2.52 us
  transfers between devices with their start and end apart: 11, of which 8 were waited for; matrix products, arithmetic and copies ran while one was open for 0% of the time, Pallas kernels for 1%

profile of v7, /device:TPU:2, one launch (start us, length us, event | category | flops | bytes accessed | tf_op | source)
XLA Modules:
  0.0 103.5 jit_solution(5464601547971551028)
XLA Ops:
  0.0 5.1 %attention.1 = bf16[32,24,128]{2,1,0:T(8,128)(2,1)} custom-call(s32[4]{0:T(128)} %lengths_ref.1, bf16[32]{0:T(256)(128)(2,1)} %gain_ref.1, bf16[4,16,1024]{2,1,0:T(8,128)(2,1)} %queries_ref.1, bf16[4,2048,128]{2,1,0:T(8,128)(2,1)} %keys_ref.1, bf16[4,2048,128]{2,1,0:T(8,128)(2,1)} %values_ref.1), custom_call_target="tpu_custom_call" | custom-call | tf_op jit(solution)/shard_map/attention/pallas_call | solution.py:108
  5.1 23.2 %all_to_all.20.in_ref = bf16[32,24,128]{2,1,0:T(8,128)(2,1)S(1)} all-to-all(bf16[32,24,128]{2,1,0:T(8,128)(2,1)} %attention.1), channel_id=1, replica_groups=mesh['z'=8,'y'=4,'x'=4,'c'=2] {'z','y'}, dimensions={0} | all-to-all | bytes 393216 | tf_op jit(solution)/shard_map/all_to_all | solution.py:395
  28.3 0.0 copy-start.3
  28.3 0.0 copy-start.4
  28.3 0.0 copy-start.2
  28.3 0.3 combine.1
  28.7 14.2 %all_to_all.21.attn_ref = bf16[32,16,128]{2,1,0:T(8,128)(2,1)S(1)} all-to-all(bf16[32,16,128]{2,1,0:T(8,128)(2,1)S(1)} %get-tuple-element.29), channel_id=1, replica_groups=mesh['z'=8,'y'=4,'x'=4,'c'=2] {'z','y'}, dimensions={0} | all-to-all | bytes 262144 | tf_op jit(solution)/shard_map/all_to_all | solution.py:395
  42.9 0.0 copy-done.3
  42.9 0.0 copy-done.4
  42.9 0.0 copy-start
  42.9 0.0 copy-start.1
  42.9 0.3 project.1
  43.3 0.1 collective-permute-start
  43.4 1.2 %collective-permute-done.other_ref = bf16[160,128]{1,0:T(8,128)(2,1)S(1)} collective-permute-done((bf16[160,128]{1,0:T(8,128)(2,1)S(1)}, bf16[160,128]{1,0:T(8,128)(2,1)S(1)}, u32[]{:S(2)}, u32[]{:S(2)}) %collective-permute-start) | collective-permute-done | bytes 40992 | tf_op jit(solution)/shard_map/ppermute | solution.py:384
  44.6 0.0 copy-done
  44.6 0.2 collective-permute-start.4
  44.8 0.1 copy-done.1
  45.0 0.2 collective-permute-start.5
  45.2 0.0 copy-done.2
  45.2 0.3 collective-permute-start.7
  45.5 1.5 %collective-permute-start.1 = (bf16[112,128]{1,0:T(8,128)(2,1)S(1)}, bf16[112,128]{1,0:T(8,128)(2,1)S(1)}, u32[]{:S(2)}, u32[]{:S(2)}) collective-permute-start(bf16[112,128]{1,0:T(8,128)(2,1)S(1)} %get-tuple-element.38), channel_id=1, source_target_pairs={{0,2},{2,4},{4,6},{6,0},{1,3},{3,5},{5,7},{7,1},{8,10},{10,12},{12... | collective-permute-start | bytes 86024 | tf_op jit(solution)/shard_map/ppermute | solution.py:389
  47.0 1.1 %collective-permute-start.2 = (bf16[112,128]{1,0:T(8,128)(2,1)S(1)}, bf16[112,128]{1,0:T(8,128)(2,1)S(1)}, u32[]{:S(2)}, u32[]{:S(2)}) collective-permute-start(bf16[112,128]{1,0:T(8,128)(2,1)S(1)} %get-tuple-element.39), channel_id=1, source_target_pairs={{0,4},{2,6},{4,0},{6,2},{1,5},{3,7},{5,1},{7,3},{8,12},{10,14},{12... | collective-permute-start | bytes 86024 | tf_op jit(solution)/shard_map/ppermute | solution.py:389
  48.1 1.3 %collective-permute-done.1.refs_1_ = bf16[112,128]{1,0:T(8,128)(2,1)S(1)} collective-permute-done((bf16[112,128]{1,0:T(8,128)(2,1)S(1)}, bf16[112,128]{1,0:T(8,128)(2,1)S(1)}, u32[]{:S(2)}, u32[]{:S(2)}) %collective-permute-start.1) | collective-permute-done | bytes 28704 | tf_op jit(solution)/shard_map/ppermute | solution.py:389
  49.3 1.7 %collective-permute-start.3 = (bf16[112,128]{1,0:T(8,128)(2,1)S(1)}, bf16[112,128]{1,0:T(8,128)(2,1)S(1)}, u32[]{:S(2)}, u32[]{:S(2)}) collective-permute-start(bf16[112,128]{1,0:T(8,128)(2,1)S(1)} %get-tuple-element.40), channel_id=1, source_target_pairs={{0,6},{2,0},{4,2},{6,4},{1,7},{3,1},{5,3},{7,5},{8,14},{10,8},{12,... | collective-permute-start | bytes 86024 | tf_op jit(solution)/shard_map/ppermute | solution.py:389
  51.1 1.5 %collective-permute-done.2.refs_2_ = bf16[112,128]{1,0:T(8,128)(2,1)S(1)} collective-permute-done((bf16[112,128]{1,0:T(8,128)(2,1)S(1)}, bf16[112,128]{1,0:T(8,128)(2,1)S(1)}, u32[]{:S(2)}, u32[]{:S(2)}) %collective-permute-start.2) | collective-permute-done | bytes 28704 | tf_op jit(solution)/shard_map/ppermute | solution.py:389
  52.6 0.6 collective-permute-done.3.refs_3_
  53.2 0.1 mix.1
  53.3 19.8 %all_to_all.22.mixed_ref = bf16[32,64,128]{2,1,0:T(8,128)(2,1)S(1)} all-to-all(bf16[32,64,128]{2,1,0:T(8,128)(2,1)S(1)} %get-tuple-element.41), channel_id=1, replica_groups=mesh['z'=8,'y'=4,'x'=4,'c'=2] {'z','y'}, dimensions={0} | all-to-all | bytes 1048576 | tf_op jit(solution)/shard_map/all_to_all | solution.py:395
  73.0 0.0 collective-permute-done.4.refs_2_
  73.0 0.0 collective-permute-done.5.refs_3_
  73.0 1.2 %widen.1.mine_ref = f32[232,128]{1,0:T(8,128)S(1)} custom-call(bf16[32,64,128]{2,1,0:T(8,128)(2,1)S(1)} %all_to_all.22.mixed_ref, f32[32,128]{1,0:T(8,128)S(1)} %get-tuple-element.42.gain_ref, bf16[112,8192]{1,0:T(8,128)(2,1)S(1)} %bitcast.5, bf16[112,8192]{1,0:T(8,128)(2,1)S(1)} %bitcast.7, bf16[112,8192]{1,0:T(8,128)(2,1)S(1)} %collective-permute-done.4.refs_2_, ...), custom_call_target="tpu_custom_call" | custom-call | tf_op jit(solution)/shard_map/widen/pallas_call | solution.py:291
  74.3 0.1 collective-permute-start.6
  74.4 0.0 collective-permute-done.7.other_ref
  74.4 1.3 %collective-permute-done.6.theirs_ref = f32[232,128]{1,0:T(8,128)S(1)} collective-permute-done((f32[232,128]{1,0:T(8,128)S(1)}, f32[232,128]{1,0:T(8,128)S(1)}, u32[]{:S(2)}, u32[]{:S(2)}) %collective-permute-start.6) | collective-permute-done | bytes 118816 | tf_op jit(solution)/shard_map/ppermute | solution.py:384
  75.7 1.1 %narrow.1 = (bf16[32,16,128]{2,1,0:T(8,128)(2,1)S(1)}, bf16[32,16,128]{2,1,0:T(8,128)(2,1)S(1)}, bf16[32,16,128]{2,1,0:T(8,128)(2,1)S(1)}, bf16[32,16,128]{2,1,0:T(8,128)(2,1)S(1)}) custom-call(f32[232,128]{1,0:T(8,128)S(1)} %widen.1.mine_ref, f32[232,128]{1,0:T(8,128)S(1)} %collective-permute-done.6.theirs_ref, bf16[112,8192]{1,0:T(8,128)(2,1)S(1)} %copy-done.2, ...), custom_call_target="tpu_custom_call" | custom-call | tf_op jit(solution)/shard_map/narrow/pallas_call | solution.py:331
  76.8 0.6 collective-permute-start.8
  77.4 2.7 %collective-permute-start.9 = (bf16[32,16,128]{2,1,0:T(8,128)(2,1)S(1)}, bf16[32,16,128]{2,1,0:T(8,128)(2,1)S(1)}, u32[]{:S(2)}, u32[]{:S(2)}) collective-permute-start(bf16[32,16,128]{2,1,0:T(8,128)(2,1)S(1)} %get-tuple-element.48), channel_id=1, source_target_pairs={{0,16},{8,24},{16,0},{24,8},{1,17},{9,25},{17,1},{25,9},{2,18},{10... | collective-permute-start | bytes 393224 | tf_op jit(solution)/shard_map/ppermute | solution.py:389
  80.1 1.5 %collective-permute-start.10 = (bf16[32,16,128]{2,1,0:T(8,128)(2,1)S(1)}, bf16[32,16,128]{2,1,0:T(8,128)(2,1)S(1)}, u32[]{:S(2)}, u32[]{:S(2)}) collective-permute-start(bf16[32,16,128]{2,1,0:T(8,128)(2,1)S(1)} %get-tuple-element.49), channel_id=1, source_target_pairs={{0,24},{8,0},{16,8},{24,16},{1,25},{9,1},{17,9},{25,17},{2,26},{10... | collective-permute-start | bytes 393224 | tf_op jit(solution)/shard_map/ppermute | solution.py:389
  81.6 2.9 %collective-permute-done.8.refs_1_ = bf16[32,16,128]{2,1,0:T(8,128)(2,1)S(1)} collective-permute-done((bf16[32,16,128]{2,1,0:T(8,128)(2,1)S(1)}, bf16[32,16,128]{2,1,0:T(8,128)(2,1)S(1)}, u32[]{:S(2)}, u32[]{:S(2)}) %collective-permute-start.8) | collective-permute-done | bytes 131104 | tf_op jit(solution)/shard_map/ppermute | solution.py:389
  84.5 2.0 %collective-permute-done.9.refs_2_ = bf16[32,16,128]{2,1,0:T(8,128)(2,1)S(1)} collective-permute-done((bf16[32,16,128]{2,1,0:T(8,128)(2,1)S(1)}, bf16[32,16,128]{2,1,0:T(8,128)(2,1)S(1)}, u32[]{:S(2)}, u32[]{:S(2)}) %collective-permute-start.9) | collective-permute-done | bytes 131104 | tf_op jit(solution)/shard_map/ppermute | solution.py:389
  86.5 0.6 collective-permute-done.10.refs_3_
  87.1 0.1 partial_sum.1
  87.1 15.5 %all_to_all.23.parts_ref = bf16[32,16,128]{2,1,0:T(8,128)(2,1)S(1)} all-to-all(bf16[32,16,128]{2,1,0:T(8,128)(2,1)S(1)} %partial_sum.1), channel_id=1, replica_groups=mesh['z'=8,'y'=4,'x'=4,'c'=2] {'z','x'}, dimensions={0} | all-to-all | bytes 262144 | tf_op jit(solution)/shard_map/all_to_all | solution.py:395
  102.6 0.8 finish.1
  (1 shorter events, 0.0 us)
Async XLA Ops:
  28.3 14.6 %copy-start.3 = (bf16[1024,256]{1,0:T(8,128)(2,1)S(1)}, bf16[1024,256]{1,0:T(8,128)(2,1)}, u32[]{:S(2)}) copy-start(bf16[1024,256]{1,0:T(8,128)(2,1)} %weight_ref.1) | copy-start | bytes 1572868
  28.3 14.6 %copy-start.4 = (bf16[64,32]{0,1:T(8,128)(2,1)S(1)}, bf16[64,32]{0,1:T(8,128)(2,1)}, u32[]{:S(2)}) copy-start(bf16[64,32]{0,1:T(8,128)(2,1)} %param.14) | copy-start | bytes 12292
  28.3 16.9 %copy-start.2 = (bf16[112,8192]{1,0:T(8,128)(2,1)S(1)}, bf16[112,8192]{1,0:T(8,128)(2,1)}, u32[]{:S(2)}) copy-start(bf16[112,8192]{1,0:T(8,128)(2,1)} %own_ref) | copy-start | bytes 5505028
  42.9 1.7 %copy-start = (bf16[8192,112]{0,1:T(8,128)(2,1)S(1)}, bf16[8192,112]{0,1:T(8,128)(2,1)}, u32[]{:S(2)}) copy-start(bf16[8192,112]{0,1:T(8,128)(2,1)} %param.17) | copy-start | bytes 5505028
  42.9 2.1 %copy-start.1 = (bf16[8192,112]{0,1:T(8,128)(2,1)S(1)}, bf16[8192,112]{0,1:T(8,128)(2,1)}, u32[]{:S(2)}) copy-start(bf16[8192,112]{0,1:T(8,128)(2,1)} %param.18) | copy-start | bytes 5505028
  43.3 1.3 %collective-permute-start = (bf16[160,128]{1,0:T(8,128)(2,1)S(1)}, bf16[160,128]{1,0:T(8,128)(2,1)S(1)}, u32[]{:S(2)}, u32[]{:S(2)}) collective-permute-start(bf16[160,128]{1,0:T(8,128)(2,1)S(1)} %get-tuple-element.32), channel_id=1, source_target_pairs={{0,1},{1,0},{2,3},{3,2},{4,5},{5,4},{6,7},{7,6},{8,9},{9,8},{10,11... | collective-permute-start | bytes 122888 | tf_op jit(solution)/shard_map/ppermute | solution.py:384
  44.6 28.4 %collective-permute-start.4 = (bf16[112,8192]{1,0:T(8,128)(2,1)S(1)}, bf16[112,8192]{1,0:T(8,128)(2,1)S(1)}, u32[]{:S(2)}, u32[]{:S(2)}) collective-permute-start(bf16[112,8192]{1,0:T(8,128)(2,1)S(1)} %bitcast.4), channel_id=1, source_target_pairs={{0,1},{1,0},{2,3},{3,2},{4,5},{5,4},{6,7},{7,6},{8,9},{9,8},{10,11... | collective-permute-start | bytes 5505032 | tf_op jit(solution)/shard_map/ppermute | solution.py:384
  45.0 28.1 %collective-permute-start.5 = (bf16[112,8192]{1,0:T(8,128)(2,1)S(1)}, bf16[112,8192]{1,0:T(8,128)(2,1)S(1)}, u32[]{:S(2)}, u32[]{:S(2)}) collective-permute-start(bf16[112,8192]{1,0:T(8,128)(2,1)S(1)} %bitcast.6), channel_id=1, source_target_pairs={{0,1},{1,0},{2,3},{3,2},{4,5},{5,4},{6,7},{7,6},{8,9},{9,8},{10,11... | collective-permute-start | bytes 5505032 | tf_op jit(solution)/shard_map/ppermute | solution.py:384
  45.2 29.2 %collective-permute-start.7 = (bf16[112,8192]{1,0:T(8,128)(2,1)S(1)}, bf16[112,8192]{1,0:T(8,128)(2,1)S(1)}, u32[]{:S(2)}, u32[]{:S(2)}) collective-permute-start(bf16[112,8192]{1,0:T(8,128)(2,1)S(1)} %copy-done.2), channel_id=1, source_target_pairs={{0,1},{1,0},{2,3},{3,2},{4,5},{5,4},{6,7},{7,6},{8,9},{9,8},{10,11... | collective-permute-start | bytes 5505032 | tf_op jit(solution)/shard_map/ppermute | solution.py:384
  45.5 3.9 %collective-permute-start.1 = (bf16[112,128]{1,0:T(8,128)(2,1)S(1)}, bf16[112,128]{1,0:T(8,128)(2,1)S(1)}, u32[]{:S(2)}, u32[]{:S(2)}) collective-permute-start(bf16[112,128]{1,0:T(8,128)(2,1)S(1)} %get-tuple-element.38), channel_id=1, source_target_pairs={{0,2},{2,4},{4,6},{6,0},{1,3},{3,5},{5,7},{7,1},{8,10},{10,12},{12... | collective-permute-start | bytes 86024 | tf_op jit(solution)/shard_map/ppermute | solution.py:389
  47.0 5.6 %collective-permute-start.2 = (bf16[112,128]{1,0:T(8,128)(2,1)S(1)}, bf16[112,128]{1,0:T(8,128)(2,1)S(1)}, u32[]{:S(2)}, u32[]{:S(2)}) collective-permute-start(bf16[112,128]{1,0:T(8,128)(2,1)S(1)} %get-tuple-element.39), channel_id=1, source_target_pairs={{0,4},{2,6},{4,0},{6,2},{1,5},{3,7},{5,1},{7,3},{8,12},{10,14},{12... | collective-permute-start | bytes 86024 | tf_op jit(solution)/shard_map/ppermute | solution.py:389
  49.3 3.9 %collective-permute-start.3 = (bf16[112,128]{1,0:T(8,128)(2,1)S(1)}, bf16[112,128]{1,0:T(8,128)(2,1)S(1)}, u32[]{:S(2)}, u32[]{:S(2)}) collective-permute-start(bf16[112,128]{1,0:T(8,128)(2,1)S(1)} %get-tuple-element.40), channel_id=1, source_target_pairs={{0,6},{2,0},{4,2},{6,4},{1,7},{3,1},{5,3},{7,5},{8,14},{10,8},{12,... | collective-permute-start | bytes 86024 | tf_op jit(solution)/shard_map/ppermute | solution.py:389
  74.3 1.4 %collective-permute-start.6 = (f32[232,128]{1,0:T(8,128)S(1)}, f32[232,128]{1,0:T(8,128)S(1)}, u32[]{:S(2)}, u32[]{:S(2)}) collective-permute-start(f32[232,128]{1,0:T(8,128)S(1)} %widen.1.mine_ref), channel_id=1, source_target_pairs={{0,1},{1,0},{2,3},{3,2},{4,5},{5,4},{6,7},{7,6},{8,9},{9,8},{10,11... | collective-permute-start | bytes 356360 | tf_op jit(solution)/shard_map/ppermute | solution.py:384
  76.8 7.6 %collective-permute-start.8 = (bf16[32,16,128]{2,1,0:T(8,128)(2,1)S(1)}, bf16[32,16,128]{2,1,0:T(8,128)(2,1)S(1)}, u32[]{:S(2)}, u32[]{:S(2)}) collective-permute-start(bf16[32,16,128]{2,1,0:T(8,128)(2,1)S(1)} %get-tuple-element.47), channel_id=1, source_target_pairs={{0,8},{8,16},{16,24},{24,0},{1,9},{9,17},{17,25},{25,1},{2,10},{10... | collective-permute-start | bytes 393224 | tf_op jit(solution)/shard_map/ppermute | solution.py:389
  77.4 9.1 %collective-permute-start.9 = (bf16[32,16,128]{2,1,0:T(8,128)(2,1)S(1)}, bf16[32,16,128]{2,1,0:T(8,128)(2,1)S(1)}, u32[]{:S(2)}, u32[]{:S(2)}) collective-permute-start(bf16[32,16,128]{2,1,0:T(8,128)(2,1)S(1)} %get-tuple-element.48), channel_id=1, source_target_pairs={{0,16},{8,24},{16,0},{24,8},{1,17},{9,25},{17,1},{25,9},{2,18},{10... | collective-permute-start | bytes 393224 | tf_op jit(solution)/shard_map/ppermute | solution.py:389
  80.1 6.9 %collective-permute-start.10 = (bf16[32,16,128]{2,1,0:T(8,128)(2,1)S(1)}, bf16[32,16,128]{2,1,0:T(8,128)(2,1)S(1)}, u32[]{:S(2)}, u32[]{:S(2)}) collective-permute-start(bf16[32,16,128]{2,1,0:T(8,128)(2,1)S(1)} %get-tuple-element.49), channel_id=1, source_target_pairs={{0,24},{8,0},{16,8},{24,16},{1,25},{9,1},{17,9},{25,17},{2,26},{10... | collective-permute-start | bytes 393224 | tf_op jit(solution)/shard_map/ppermute | solution.py:389
